TPU v7x, 32 devices: a whole 2x2x4 slice. The times are simulated.
32 devices in a mesh: group: 4 (over y, x), blk: 4 (over z), att: 2 (over core).
Axes of the slice: x: 2, y: 2, z: 4, core: 2. Of those that a mesh axis runs over, the one named last changes fastest.
Arguments:
- tokens: bfloat16 [2048, 4096], P(('group', 'blk')), may hold values from -6 to 6
- routed_experts: int32 [2048, 8], P(('group', 'blk')), may hold values from 0 to 127, all different within a row; in each aligned block of 128 rows (0 to 127, 128 to 255, ...) at most 16 rows name the same one
- act_cotangent: bfloat16 [2048, 8, 768], P(('group', 'blk'), None, 'att'), may hold values from -2.5 to 2.5
- weight_codes: bfloat16 [4096, 4, 2, 768], P('blk', 'group', None, 'att'), may hold values from -0.09375 to 0.09375
- weight_scales: bfloat16 [32, 4, 2, 6], P('blk', 'group', None, 'att'), may hold values from 0.3984375 to 2.5
Outputs:
- gate_up_gradient: bfloat16 [4096, 4, 2, 768], P('blk', 'group', None, 'att')
Inputs may be any that keep to these rules, and one draw needn't show every extreme that they name: `routed_experts`: each row names 8 different experts. Among the 128 rows of one device (aligned blocks of 128 rows), no expert is named by more than 16 rows, a bound that some block reaches.
All inputs are finite; a program needn't handle non-finite values.
Results may differ from a plain program's by a relative error of at most 0.023.
Values may be sent and summed in bfloat16 or wider, within the bound.
No kernel may reach another device: no remote copies, remote signals or barrier semaphores. Data moves between devices by JAX's collectives and lax.ppermute only.
A program may use at most 64 MiB of HBM per device.

v0:
```python
import jax
import jax.numpy as jnp
from jax import lax
from jax.sharding import PartitionSpec as P

QB = 128
CAP = 16


def swiglu_back(gate_up, cotangent_rows):
    gate_pre = gate_up[:, 0]
    up_pre = gate_up[:, 1]
    sigmoid_gate = jax.nn.sigmoid(gate_pre)
    gate_cotangent = (
        cotangent_rows * up_pre * sigmoid_gate * (1.0 + gate_pre * (1.0 - sigmoid_gate))
    )
    up_cotangent = cotangent_rows * gate_pre * sigmoid_gate
    return jnp.stack([gate_cotangent, up_cotangent], axis=1).astype(jnp.bfloat16)


def local(tokens, routed_experts, act_cotangent, weight_codes, weight_scales):
    groups = lax.axis_size("group")
    hidden_dev = weight_codes.shape[3]
    flight_ids = jnp.arange(groups, dtype=jnp.int32)
    matches = (routed_experts[:, :, None] == flight_ids[None, None, :]).astype(jnp.float32)
    chosen = jnp.sum(matches, axis=1)
    position = jnp.cumsum(chosen, axis=0) - 1.0
    slot_index = jnp.arange(CAP, dtype=jnp.int32).astype(jnp.float32)
    selector = (
        chosen.T[:, None, :]
        * (position.T[:, None, :] == slot_index[None, :, None]).astype(jnp.float32)
    ).astype(jnp.bfloat16)
    sent_tokens = jnp.einsum(
        "ect,td->ecd", selector, tokens, preferred_element_type=jnp.float32
    ).astype(jnp.bfloat16)
    pair_cotangent = jnp.einsum(
        "tke,tkh->teh",
        matches.astype(jnp.bfloat16),
        act_cotangent,
        preferred_element_type=jnp.float32,
    ).astype(jnp.bfloat16)
    sent_cotangent = jnp.einsum(
        "ect,teh->ech", selector, pair_cotangent, preferred_element_type=jnp.float32
    ).astype(jnp.bfloat16)
    arrived_tokens, arrived_cotangent = (
        lax.all_to_all(sent_tokens, "group", split_axis=0, concat_axis=0, tiled=True),
        lax.all_to_all(sent_cotangent, "group", split_axis=0, concat_axis=0, tiled=True),
    )
    row_count = groups * CAP
    width = arrived_tokens.shape[2]
    token_rows = arrived_tokens.reshape(row_count, width)
    cotangent_rows = arrived_cotangent.reshape(row_count, hidden_dev).astype(jnp.float32)
    local_scales = jnp.repeat(weight_scales, QB, axis=0)
    code_piece = lax.all_gather(weight_codes, "blk", axis=0, tiled=True)
    scale_piece = lax.all_gather(local_scales, "blk", axis=0, tiled=True)
    expanded = jnp.repeat(scale_piece[:, 0].astype(jnp.float32), QB, axis=2)
    weights = (code_piece[:, 0].astype(jnp.float32) * expanded).astype(jnp.bfloat16)
    gate_up = jnp.einsum("rn,njh->rjh", token_rows, weights, preferred_element_type=jnp.float32)
    pre_cotangent = swiglu_back(gate_up, cotangent_rows)
    own_columns = lax.all_to_all(token_rows, "blk", split_axis=1, concat_axis=0, tiled=True)
    piece = lax.all_gather(pre_cotangent, "blk", axis=0, tiled=True)
    shards = piece.shape[0] // row_count
    column_block = own_columns
    column_block = column_block.reshape(shards, row_count, column_block.shape[1])
    cotangent_block = piece.reshape(shards, row_count, 2, hidden_dev)
    partials = jnp.einsum(
        "krd,krjh->kdjh", column_block, cotangent_block, preferred_element_type=jnp.float32
    )
    rounded = lax.optimization_barrier(partials.astype(jnp.bfloat16)).astype(jnp.float32)
    gradient = jnp.sum(rounded, axis=0)
    return gradient.astype(jnp.bfloat16)[:, None]


def solution(mesh):
    return jax.shard_map(
        local,
        mesh=mesh,
        in_specs=(
            P(("group", "blk"), None),
            P(("group", "blk"), None),
            P(("group", "blk"), None, "att"),
            P("blk", "group", None, "att"),
            P("blk", "group", None, "att"),
        ),
        out_specs=P("blk", "group", None, "att"),
        check_vma=False,
    )
```

profile of v0, /device:TPU:0, one launch (start us, length us, event | category | flops | bytes accessed | tf_op | source)
XLA Modules:
  0.0 182.8 jit_solution(1821733704673112352)
XLA Ops:
  6.5 0.0 copy-start
  6.5 0.0 copy-start.2
  6.5 0.0 copy-start.1
  6.5 0.0 all-gather.2.cloned.1.call-start
  6.5 5.0 %copy.35 = bf16[1024,1,2,384]{0,3,2,1:T(8,128)(2,1)} copy(bf16[1024,1,2,384]{3,2,1,0:T(2,128)(2,1)} %param.8) | data formatting | bytes 3145728 | tf_op args[3]
  11.6 0.0 all-gather.2.cloned.1.call-update
  11.6 0.8 copy.30
  12.4 0.2 convert_reduce_fusion
  12.6 0.2 reduce_window_sum.11
  12.8 0.1 copy.31
  12.9 0.1 copy.32
  12.9 0.0 copy-done
  13.0 1.2 convolution_convert_fusion
  14.1 5.2 %all-to-all-start = ((bf16[4,16,4096]{2,1,0:T(8,128)(2,1)}), bf16[4,16,4096]{2,1,0:T(8,128)(2,1)S(1)}, u32[]{:S(2)}, u32[]{:S(2)}) async-start(bf16[4,16,4096]{2,1,0:T(8,128)(2,1)} %convolution_convert_fusion), calls=%async_computation | async-start | bytes 1048576 | tf_op jit(solution)/shard_map/all_to_all | solution.py:46
  19.3 0.0 copy-done.2
  19.3 0.1 broadcast_in_dim.16
  19.4 13.6 %all_gather.10 = bf16[4096,1,2,3]{0,2,3,1:T(2,128)(2,1)S(1)} all-gather(bf16[1024,1,2,3]{0,2,3,1:T(2,128)(2,1)S(1)} %broadcast_in_dim.17), channel_id=1, replica_groups=mesh['group'=4,'blk'=4,'att'=2] {'blk'}, dimensions={0}, use_global_device_ids=true | all-gather | bytes 61440 | tf_op jit(solution)/shard_map/all_gather | solution.py:55
  33.0 0.1 copy.36
  33.1 0.0 copy-done.1
  33.1 0.4 convolution_convert_fusion.2
  33.5 0.9 convolution_convert_fusion.3
  34.4 0.0 all-to-all-done
  34.4 7.4 %all-to-all-start.2 = ((bf16[4,16,384]{2,1,0:T(8,128)(2,1)}), bf16[4,16,384]{2,1,0:T(8,128)(2,1)S(1)}, u32[]{:S(2)}, u32[]{:S(2)}) async-start(bf16[4,16,384]{2,1,0:T(8,128)(2,1)} %convolution_convert_fusion.3), calls=%async_computation.2 | async-start | bytes 98304 | tf_op jit(solution)/shard_map/all_to_all | solution.py:47
  41.8 0.4 all_to_all.19
  42.2 1.0 copy.33
  43.1 87.0 %all-gather.2.cloned.1.call-done = bf16[4096,1,2,384]{0,3,2,1:T(8,128)(2,1)} async-done(((bf16[1024,1,2,384]{0,3,2,1:T(8,128)(2,1)}), bf16[4096,1,2,384]{0,3,2,1:T(8,128)(2,1)}) %all-gather.2.cloned.1.call-update) | async-done | bytes 6291472 | tf_op jit(solution)/shard_map/all_gather | solution.py:54
  130.2 7.3 %fusion = bf16[4096,2,3,128]{0,3,2,1:T(8,128)(2,1)} fusion(bf16[4096,2,3,128]{0,3,2,1:T(8,128)(2,1)} %bitcast.37, f32[4096,2,3]{0,2,1:T(4,128)S(1)} %copy.36), kind=kLoop, calls=%fused_computation.1 | loop fusion | flops 9437184 | bytes 12681216 | tf_op jit(solution)/shard_map/convert_element_type | solution.py:57
  137.5 0.0 all-to-all-done.2
  137.5 3.5 %all-to-all-start.1 = ((bf16[64,4,1024]{2,0,1:T(8,128)(2,1)}), bf16[64,4,1024]{2,0,1:T(8,128)(2,1)S(1)}, u32[]{:S(2)}, u32[]{:S(2)}) async-start(bf16[64,4,1024]{2,0,1:T(8,128)(2,1)} %copy.33), calls=%async_computation.1 | async-start | bytes 1048576 | tf_op jit(solution)/shard_map/all_to_all | solution.py:60
  141.0 4.8 %fusion.21 = f32[64,2,384]{2,0,1:T(8,128)S(1)} fusion(bf16[64,4096,1]{1,0,2:T(8,128)(2,1)S(1)} %bitcast.39, bf16[4096,2,384]{0,2,1:T(8,128)(2,1)} %bitcast.36), kind=kOutput, calls=%fused_computation.37 | convolution fusion | flops 402653184 | bytes 7012352 | tf_op jit(solution)/shard_map/rn,njh->rjh/dot_general | solution.py:58
  145.8 0.1 fusion.8
  145.9 18.5 %all_gather.11 = bf16[256,2,384]{2,0,1:T(8,128)(2,1)S(1)} all-gather(bf16[64,2,384]{2,0,1:T(8,128)(2,1)S(1)} %pad_maximum_fusion), channel_id=1, replica_groups=mesh['group'=4,'blk'=4,'att'=2] {'blk'}, dimensions={0}, use_global_device_ids=true | all-gather | bytes 491520 | tf_op jit(solution)/shard_map/all_gather | solution.py:61
  164.4 0.0 all-to-all-done.1
  164.4 4.5 %convolution_convert_fusion.1 = bf16[4,1024,2,384]{3,1,2,0:T(8,128)(2,1)} fusion(bf16[64,4,1024]{2,0,1:T(8,128)(2,1)S(1)} %all-to-all-done.1, bf16[4,64,2,384]{3,1,0,2:T(8,128)(2,1)S(1)} %bitcast.40), kind=kOutput, calls=%fused_computation.3 | convolution fusion | flops 405798912 | bytes 7208960 | tf_op jit(solution)/shard_map/krd,krjh->kdjh/dot_general | solution.py:66
  168.9 4.3 %reduce_sum.22 = bf16[1024,2,384]{2,0,1:T(8,128)(2,1)S(1)} reduce(bf16[4,1024,2,384]{3,1,2,0:T(8,128)(2,1)} %convolution_convert_fusion.1, bf16[]{:T(256)} %constant.12.clone.1), dimensions={0}, to_apply=%region_2.3 | reduce | flops 2359296 | bytes 7864322 | tf_op jit(solution)/shard_map/reduce_sum | solution.py:70
  173.2 2.8 %copy.39 = bf16[1024,1,2,384]{3,2,1,0:T(2,128)(2,1)} copy(bf16[1024,1,2,384]{3,0,2,1:T(8,128)(2,1)S(1)} %bitcast.38) | data formatting | bytes 3145728 | tf_op jit(solution)/shard_map/broadcast_in_dim | solution.py:71
  (5 shorter events, 0.1 us)
Async XLA Ops:
  6.5 6.4 %copy-start = (bf16[128,4096]{1,0:T(8,128)(2,1)S(1)}, bf16[128,4096]{1,0:T(8,128)(2,1)}, u32[]{:S(2)}) copy-start(bf16[128,4096]{1,0:T(8,128)(2,1)} %param.5) | copy-start | bytes 3145732
  6.5 12.8 %copy-start.2 = (bf16[8,1,2,3]{0,2,3,1:T(2,128)(2,1)S(1)}, bf16[8,1,2,3]{0,2,3,1:T(2,128)(2,1)}, u32[]{:S(2)}) copy-start(bf16[8,1,2,3]{0,2,3,1:T(2,128)(2,1)} %param.9) | copy-start | bytes 292
  6.5 26.6 %copy-start.1 = (bf16[128,8,384]{2,1,0:T(8,128)(2,1)S(1)}, bf16[128,8,384]{2,1,0:T(8,128)(2,1)}, u32[]{:S(2)}) copy-start(bf16[128,8,384]{2,1,0:T(8,128)(2,1)} %param.7) | copy-start | bytes 2359300
  6.5 123.6 %all-gather.2.cloned.1.call-start = ((), (), s32[]{:S(2)}) async-start(), calls=%async_computation.3 | async-start | bytes 7864320 | tf_op jit(solution)/shard_map/all_gather | solution.py:54
  14.1 20.3 %all-to-all-start = ((bf16[4,16,4096]{2,1,0:T(8,128)(2,1)}), bf16[4,16,4096]{2,1,0:T(8,128)(2,1)S(1)}, u32[]{:S(2)}, u32[]{:S(2)}) async-start(bf16[4,16,4096]{2,1,0:T(8,128)(2,1)} %convolution_convert_fusion), calls=%async_computation | async-start | bytes 1048576 | tf_op jit(solution)/shard_map/all_to_all | solution.py:46
  34.4 103.1 %all-to-all-start.2 = ((bf16[4,16,384]{2,1,0:T(8,128)(2,1)}), bf16[4,16,384]{2,1,0:T(8,128)(2,1)S(1)}, u32[]{:S(2)}, u32[]{:S(2)}) async-start(bf16[4,16,384]{2,1,0:T(8,128)(2,1)} %convolution_convert_fusion.3), calls=%async_computation.2 | async-start | bytes 98304 | tf_op jit(solution)/shard_map/all_to_all | solution.py:47
  137.5 26.9 %all-to-all-start.1 = ((bf16[64,4,1024]{2,0,1:T(8,128)(2,1)}), bf16[64,4,1024]{2,0,1:T(8,128)(2,1)S(1)}, u32[]{:S(2)}, u32[]{:S(2)}) async-start(bf16[64,4,1024]{2,0,1:T(8,128)(2,1)} %copy.33), calls=%async_computation.1 | async-start | bytes 1048576 | tf_op jit(solution)/shard_map/all_to_all | solution.py:60
Sparse Core Ops, SparseCore 0:
  11.7 118.4 all-gather.1
where the time goes:
time: 183 us
  waiting for transfers between devices  87.1 us (48%)
  blocking collectives  32.1 us (18%)
  starting transfers between devices  16 us (9%)
  between operations  13.5 us (7%)
  other arithmetic  12.1 us (7%)
  matrix products  11.7 us (6%)
  local copies, waits for them, and re-layouts  10.3 us (6%)
    all_gather x1, waiting for transfers between devices, local(): code_piece = lax.all_gather(weight_codes, 'blk', axis=0, tiled=True)  87 us
    all_gather x1, blocking collectives, local(): piece = lax.all_gather(pre_cotangent, 'blk', axis=0, tiled=True)  18.5 us
    all_gather x1, blocking collectives, local(): scale_piece = lax.all_gather(local_scales, 'blk', axis=0, tiled=True)  13.6 us
    all_to_all x1, starting transfers between devices, local(): lax.all_to_all(sent_cotangent, 'group', split_axis=0, concat_axis=0, tile...  7.4 us
    convert_element_type x1, other arithmetic, local(): (code_piece[:, 0].astype(jnp.float32) * expanded).astype(jnp.bfloat16)  7.33 us
    unnamed x8, local copies, waits for them, and re-layouts  5.84 us
    all_to_all x1, starting transfers between devices, local(): lax.all_to_all(sent_tokens, 'group', split_axis=0, concat_axis=0, tiled=T...  5.16 us
    dot_general x1, matrix products, local(): jnp.einsum('rn,njh->rjh', token_rows, weights, preferred_element_type=jnp...  4.81 us
  transfers between devices with their start and end apart: 4, of which 1 were waited for; matrix products, arithmetic and copies ran while one was open for 9% of the time, Pallas kernels for 0%

commit v1 on v0

v1 whole, which is shorter than its diff:
```python
import functools

import jax
import jax.numpy as jnp
from jax import lax
from jax.experimental import pallas as pl
from jax.experimental.pallas import tpu as pltpu
from jax.sharding import PartitionSpec as P

CAP = 16
BF16 = jnp.bfloat16
F32 = jnp.float32
VMEM_BYTES = 40 * 1024 * 1024


def call(kernel, out_shape, args, in_specs, out_specs=None, scratch=(), flops=0, nbytes=0):
    vmem = pl.BlockSpec(memory_space=pltpu.VMEM)
    return pl.pallas_call(
        kernel,
        out_shape=out_shape,
        in_specs=in_specs,
        out_specs=jax.tree.map(lambda _: vmem, out_shape) if out_specs is None else out_specs,
        scratch_shapes=scratch,
        compiler_params=pltpu.CompilerParams(vmem_limit_bytes=VMEM_BYTES),
        cost_estimate=pl.CostEstimate(flops=flops, bytes_accessed=nbytes, transcendentals=0),
    )(*args)


VMEM = pl.BlockSpec(memory_space=pltpu.VMEM)
SMEM = pl.BlockSpec(memory_space=pltpu.SMEM)


def dot(a, b, dims=((1,), (0,))):
    return lax.dot_general(a, b, (dims, ((), ())), preferred_element_type=F32)


def iota(shape, dim):
    return lax.broadcasted_iota(jnp.int32, shape, dim)


def pack_kernel(ng, nb, halves, me, tokens, routed, act, *outs):
    top, count = routed.shape
    rows = ng * CAP
    width = tokens.shape[1] // (nb * halves)
    group, block, half = me[0], me[1], me[2]
    ids = routed[...]
    chosen = [jnp.sum((ids == (group ^ s)).astype(F32), axis=0, keepdims=True) for s in range(ng)]
    chosen_rows = jnp.concatenate([jnp.broadcast_to(c, (CAP, count)) for c in chosen], axis=0)
    upto = (iota((count, count), 0) <= iota((count, count), 1)).astype(F32).astype(BF16)
    place = dot(chosen_rows.astype(BF16), upto)
    slot = (iota((rows, count), 0) % CAP + 1).astype(F32)
    selector = jnp.where(place == slot, chosen_rows, 0.0).astype(BF16)
    spread = (iota((count, count * top), 1) // top == iota((count, count * top), 0)).astype(F32).astype(BF16)
    ids_wide = dot(ids.astype(F32).astype(BF16), spread)
    own_slot = iota((top, count * top), 1) % top == iota((top, count * top), 0)
    ids_flat = jnp.sum(jnp.where(own_slot, ids_wide, 0.0), axis=0, keepdims=True)
    expert = (group ^ (iota((rows, 1), 0) // CAP)).astype(F32)
    pair = jnp.where(ids_flat == expert, dot(selector, spread), 0.0).astype(BF16)
    hidden = act.shape[2]
    cot = dot(pair, act[...].reshape(count * top, hidden)).astype(BF16)
    for p in range(nb):
        start = pl.multiple_of(((block ^ p) * halves + half) * width, width)
        part = dot(selector, tokens[:, pl.ds(start, width)]).astype(BF16)
        for s in range(ng):
            outs[s][:, p * width : (p + 1) * width] = part[s * CAP : (s + 1) * CAP]
    for s in range(ng):
        outs[s][:, nb * width :] = cot[s * CAP : (s + 1) * CAP]


def regroup_kernel(ng, nb, width, *refs):
    pieces, outs = refs[:ng], refs[ng:]
    for s in range(ng):
        for p in range(nb):
            outs[p][s * CAP : (s + 1) * CAP, :] = pieces[s][:, p * width : (p + 1) * width]
        outs[nb][s * CAP : (s + 1) * CAP, :] = pieces[s][:, nb * width :]


def weights_kernel(halves, me, scales, codes, out):
    depth, _, hidden = codes.shape
    blocks, _, cols = scales.shape
    qrows, qcols = depth // blocks, hidden // cols
    half = me[2]
    per_half = blocks // halves
    pick = [
        (iota((qrows, 2 * qrows), 1) == 2 * iota((qrows, 2 * qrows), 0) + j).astype(F32).astype(BF16)
        for j in range(2)
    ]
    for q in range(blocks):
        source = (q + half * per_half) % blocks if halves > 1 else q
        rows = codes[pl.ds(pl.multiple_of(source * qrows, qrows), qrows)].reshape(2 * qrows, hidden)
        for j in range(2):
            values = dot(pick[j], rows)
            for c in range(cols):
                at = j * hidden + c * qcols
                out[q * qrows : (q + 1) * qrows, at : at + qcols] = (
                    values[:, c * qcols : (c + 1) * qcols] * scales[source, j, c]
                ).astype(BF16)


def gate_up_kernel(nb, halves, *refs):
    pieces, weights, outs = refs[: nb * halves], refs[nb * halves], refs[nb * halves + 1 :]
    rows, width = pieces[0].shape
    for p in range(nb):
        total = dot(pieces[p][...], weights[:width])
        for h in range(1, halves):
            total += dot(pieces[h * nb + p][...], weights[h * width : (h + 1) * width])
        outs[p][...] = total.astype(outs[p].dtype)


def swiglu_kernel(nb, *refs):
    parts, cot, out = refs[:nb], refs[nb], refs[nb + 1]
    hidden = cot.shape[1]
    total = parts[0][...]
    for p in range(1, nb):
        total += parts[p][...].astype(F32)
    gate, up = total[:, :hidden], total[:, hidden:]
    c = cot[...].astype(F32)
    s = jax.nn.sigmoid(gate)
    out[:, :hidden] = (c * up * s * (1.0 + gate * (1.0 - s))).astype(BF16)
    out[:, hidden:] = (c * gate * s).astype(BF16)


def spread_kernel(nb, halves, me, *refs):
    pieces, out = refs[: nb * halves], refs[nb * halves]
    rows, width = pieces[0].shape
    step = min(128, width)
    half = me[2]
    put = [
        (iota((2 * step, step), 0) == 2 * iota((2 * step, step), 1) + j).astype(F32).astype(BF16)
        for j in range(2)
    ]
    for h in range(halves):
        for p in range(nb):
            for k in range(width // step):
                block = pieces[h * nb + p][:, k * step : (k + 1) * step]
                start = ((half ^ h) * width + k * step) * 2
                for j in range(2):
                    at = (j * nb + p) * rows
                    out[pl.ds(pl.multiple_of(start, 2 * step), 2 * step), at : at + rows] = dot(
                        put[j], block, ((1,), (1,))
                    ).astype(BF16)


def gradient_kernel(nb, *refs):
    parts, spread, out, stacked = refs[:nb], refs[nb], refs[nb + 1], refs[nb + 2]
    rows = parts[0].shape[0]
    hidden = out.shape[2]
    for j in range(2):
        for p in range(nb):
            at = (j * nb + p) * rows
            stacked[at : at + rows, :] = parts[p][:, j * hidden : (j + 1) * hidden]
    step = min(256, spread.shape[0])
    for k in range(spread.shape[0] // step):
        values = dot(spread[k * step : (k + 1) * step, :], stacked[...])
        out[k * step // 2 : (k + 1) * step // 2] = values.reshape(step // 2, 2, hidden).astype(BF16)


def swap(x, axis, size, s):
    return lax.ppermute(x, axis, [(i, i ^ s) for i in range(size)])


def local(tokens, routed_experts, act_cotangent, weight_codes, weight_scales):
    ng, nb, na = lax.axis_size("group"), lax.axis_size("blk"), lax.axis_size("att")
    depth, _, _, hidden = weight_codes.shape
    halves = 2 if na == 2 and depth % 256 == 0 else 1
    width = depth // halves
    rows = ng * CAP
    me = jnp.stack(
        [lax.axis_index("group"), lax.axis_index("blk"), lax.axis_index("att") if halves == 2 else 0]
    ).astype(jnp.int32)
    sds = jax.ShapeDtypeStruct
    sent = call(
        functools.partial(pack_kernel, ng, nb, halves),
        [sds((CAP, nb * width + hidden), BF16)] * ng,
        (me, tokens, routed_experts.T, act_cotangent),
        [SMEM, VMEM, VMEM, VMEM],
        nbytes=2 << 20,
    )
    pieces = [sent[0]] + [swap(sent[s], "group", ng, s) for s in range(1, ng)]
    *columns, cot = call(
        functools.partial(regroup_kernel, ng, nb, width),
        [sds((rows, width), BF16)] * nb + [sds((rows, hidden), BF16)],
        pieces,
        [VMEM] * ng,
        nbytes=1 << 20,
    )
    x = [columns[0]] + [swap(columns[p], "blk", nb, p) for p in range(1, nb)]
    if halves == 2:
        x += [swap(piece, "att", 2, 1) for piece in x]
    weights = call(
        functools.partial(weights_kernel, halves),
        sds((depth, 2 * hidden), BF16),
        (me, weight_scales[:, 0].astype(F32), weight_codes[:, 0]),
        [SMEM, SMEM, VMEM],
        nbytes=8 << 20,
    )
    partial = call(
        functools.partial(gate_up_kernel, nb, halves),
        [sds((rows, 2 * hidden), F32)] + [sds((rows, 2 * hidden), BF16)] * (nb - 1),
        (*x, weights),
        [VMEM] * (nb * halves + 1),
        flops=2 * nb * rows * depth * 2 * hidden,
        nbytes=3 << 20,
    )
    parts = [partial[0]] + [swap(partial[p], "blk", nb, p) for p in range(1, nb)]
    own = call(
        functools.partial(swiglu_kernel, nb),
        sds((rows, 2 * hidden), BF16),
        (*parts, cot),
        [VMEM] * (nb + 1),
        nbytes=1 << 20,
    )
    spread = call(
        functools.partial(spread_kernel, nb, halves),
        sds((2 * depth, 2 * nb * rows), BF16),
        (me, *x),
        [SMEM] + [VMEM] * (nb * halves),
        nbytes=8 << 20,
    )
    gathered = [own] + [swap(own, "blk", nb, p) for p in range(1, nb)]
    gradient = call(
        functools.partial(gradient_kernel, nb),
        sds((depth, 2, hidden), BF16),
        (*gathered, spread),
        [VMEM] * (nb + 1),
        scratch=[pltpu.VMEM((2 * nb * rows, hidden), BF16)],
        flops=4 * nb * rows * depth * 2 * hidden,
        nbytes=4 << 20,
    )
    return gradient[:, None]


def solution(mesh):
    return jax.shard_map(
        local,
        mesh=mesh,
        in_specs=(
            P(("group", "blk"), None),
            P(("group", "blk"), None),
            P(("group", "blk"), None, "att"),
            P("blk", "group", None, "att"),
            P("blk", "group", None, "att"),
        ),
        out_specs=P("blk", "group", None, "att"),
        check_vma=False,
    )
```

time: 183 us -> 53.9 us (0.29)
  waiting for transfers between devices: 87.1 us -> 22.4 us
  blocking collectives: 32.1 us -> 0 us
  between operations: 13.5 us -> 0.1 us
  other arithmetic: 12.1 us -> 0.08 us
  matrix products: 11.7 us -> 0 us
  Pallas kernels: 0 us -> 9.54 us
  local copies, waits for them, and re-layouts: 10.3 us -> 3.25 us
  starting transfers between devices: 16 us -> 18.4 us
    all_gather x1 -> x0, waiting for transfers between devices: 87 us -> none  [local(): code_piece = lax.all_gather(weight_codes, 'blk', axis=0, tiled=True)]
    all_gather x2 -> x0, blocking collectives: 32.1 us -> none  [the longest x1 18.5 us: local(): piece = lax.all_gather(pre_cotangent, 'blk', axis=0, tiled=True)]
    ppermute x0 -> x16, waiting for transfers between devices: none -> 22.4 us  [swap(): return lax.ppermute(x, axis, [(i, i ^ s) for i in range(size)])]
    ppermute x0 -> x16, starting transfers between devices: none -> 18.4 us  [swap(): return lax.ppermute(x, axis, [(i, i ^ s) for i in range(size)])]
    all_to_all x3 -> x0, starting transfers between devices: 16 us -> none  [the longest x1 7.4 us: local(): lax.all_to_all(sent_cotangent, 'group', split_axis=0, concat_axis=0, tile...]
    dot_general x5 -> x0, matrix products: 11.7 us -> none  [the longest x1 4.81 us: local(): jnp.einsum('rn,njh->rjh', token_rows, weights, preferred_element_type=jnp...]
    pallas_call x0 -> x7, Pallas kernels: none -> 9.54 us  [call(): pl.pallas_call(kernel, out_shape=out_shape, in_specs=in_specs, out_specs=...]
    convert_element_type x3 -> x1, other arithmetic: 7.37 us -> 0.01 us  [local(): weight_scales[:, 0].astype(F32)]
  transfers between devices with their start and end apart: 4 -> 16, of which waited for: 1 -> 9; matrix products, arithmetic and copies ran while one was open for 9% -> 0% of each run, Pallas kernels for 0% -> 7%
where the time goes in v1:
time: 53.9 us; the launch traced here: 53.8 us
  waiting for transfers between devices  22.4 us (42%)
  starting transfers between devices  18.4 us (34%)
  Pallas kernels  9.54 us (18%)
  local copies, waits for them, and re-layouts  3.25 us (6%)
    ppermute x16, waiting for transfers between devices, swap(): return lax.ppermute(x, axis, [(i, i ^ s) for i in range(size)])  22.4 us
    ppermute x16, starting transfers between devices, swap(): return lax.ppermute(x, axis, [(i, i ^ s) for i in range(size)])  18.4 us
    pallas_call x7, Pallas kernels, call(): pl.pallas_call(kernel, out_shape=out_shape, in_specs=in_specs, out_specs=...  9.54 us
    unnamed x10, local copies, waits for them, and re-layouts  3.16 us
  transfers between devices with their start and end apart: 16, of which 9 were waited for; matrix products, arithmetic and copies ran while one was open for 0% of the time, Pallas kernels for 7%

profile of v1, /device:TPU:0, one launch (start us, length us, event | category | flops | bytes accessed | tf_op | source)
XLA Modules:
  0.0 53.8 jit_solution(2380975857911307748)
XLA Ops:
  0.0 0.1 pad_add_fusion.me
  0.1 0.0 copy-start.1
  0.1 1.3 %copy-done.1 = bf16[128,4096]{1,0:T(8,128)(2,1)S(1)} copy-done((bf16[128,4096]{1,0:T(8,128)(2,1)S(1)}, bf16[128,4096]{1,0:T(8,128)(2,1)}, u32[]{:S(2)}) %copy-start.1) | copy-done | bytes 1048600
  1.4 0.0 copy-start.2
  1.4 1.1 %copy-done.2 = bf16[128,8,384]{2,1,0:T(8,128)(2,1)S(1)} copy-done((bf16[128,8,384]{2,1,0:T(8,128)(2,1)S(1)}, bf16[128,8,384]{2,1,0:T(8,128)(2,1)}, u32[]{:S(2)}) %copy-start.2) | copy-done | bytes 786456
  2.5 0.0 copy-start.3
  2.5 0.7 %copy-done.3 = s32[128,8]{0,1:T(8,128)S(1)} copy-done((s32[128,8]{0,1:T(8,128)S(1)}, s32[128,8]{0,1:T(8,128)}, u32[]{:S(2)}) %copy-start.3) | copy-done | bytes 4120
  3.2 1.1 %shard_map.55 = (bf16[16,2432]{1,0:T(8,128)(2,1)S(1)}, bf16[16,2432]{1,0:T(8,128)(2,1)S(1)}, bf16[16,2432]{1,0:T(8,128)(2,1)S(1)}, bf16[16,2432]{1,0:T(8,128)(2,1)S(1)}) custom-call(s32[3]{0:T(128)S(1)} %pad_add_fusion.me, bf16[128,4096]{1,0:T(8,128)(2,1)S(1)} %copy-done.1, s32[8,128]{1,0:T(8,128)S(1)} %bitcast.12, bf16[128,8,384]{2,1,0:T(8,128)(2,1)S(1)} %copy-done.2), custom_call_target="tpu_custom_call" | custom-call | bytes 2097152 | tf_op jit(solution)/shard_map/pallas_call | solution.py:18
  4.3 3.0 %collective-permute-start = (bf16[16,2432]{1,0:T(8,128)(2,1)S(1)}, bf16[16,2432]{1,0:T(8,128)(2,1)S(1)}, u32[]{:S(2)}, u32[]{:S(2)}) collective-permute-start(bf16[16,2432]{1,0:T(8,128)(2,1)S(1)} %get-tuple-element.19), channel_id=1, source_target_pairs={{0,8},{8,0},{16,24},{24,16},{1,9},{9,1},{17,25},{25,17},{2,10},{10... | collective-permute-start | bytes 233480 | tf_op jit(solution)/shard_map/ppermute | solution.py:159
  7.4 1.5 %collective-permute-start.1 = (bf16[16,2432]{1,0:T(8,128)(2,1)S(1)}, bf16[16,2432]{1,0:T(8,128)(2,1)S(1)}, u32[]{:S(2)}, u32[]{:S(2)}) collective-permute-start(bf16[16,2432]{1,0:T(8,128)(2,1)S(1)} %get-tuple-element.20), channel_id=1, source_target_pairs={{0,16},{8,24},{16,0},{24,8},{1,17},{9,25},{17,1},{25,9},{2,18},{10... | collective-permute-start | bytes 233480 | tf_op jit(solution)/shard_map/ppermute | solution.py:159
  8.9 0.0 collective-permute-start.2
  8.9 1.1 %collective-permute-done.refs_1_ = bf16[16,2432]{1,0:T(8,128)(2,1)S(1)} collective-permute-done((bf16[16,2432]{1,0:T(8,128)(2,1)S(1)}, bf16[16,2432]{1,0:T(8,128)(2,1)S(1)}, u32[]{:S(2)}, u32[]{:S(2)}) %collective-permute-start) | collective-permute-done | bytes 77856 | tf_op jit(solution)/shard_map/ppermute | solution.py:159
  10.0 2.6 %collective-permute-done.1.refs_2_ = bf16[16,2432]{1,0:T(8,128)(2,1)S(1)} collective-permute-done((bf16[16,2432]{1,0:T(8,128)(2,1)S(1)}, bf16[16,2432]{1,0:T(8,128)(2,1)S(1)}, u32[]{:S(2)}, u32[]{:S(2)}) %collective-permute-start.1) | collective-permute-done | bytes 77856 | tf_op jit(solution)/shard_map/ppermute | solution.py:159
  12.6 1.6 %collective-permute-done.2.refs_3_ = bf16[16,2432]{1,0:T(8,128)(2,1)S(1)} collective-permute-done((bf16[16,2432]{1,0:T(8,128)(2,1)S(1)}, bf16[16,2432]{1,0:T(8,128)(2,1)S(1)}, u32[]{:S(2)}, u32[]{:S(2)}) %collective-permute-start.2) | collective-permute-done | bytes 77856 | tf_op jit(solution)/shard_map/ppermute | solution.py:159
  14.2 1.6 %collective-permute-start.3 = (bf16[64,512]{1,0:T(8,128)(2,1)S(1)}, bf16[64,512]{1,0:T(8,128)(2,1)S(1)}, u32[]{:S(2)}, u32[]{:S(2)}) collective-permute-start(bf16[64,512]{1,0:T(8,128)(2,1)S(1)} %get-tuple-element.23), channel_id=1, source_target_pairs={{0,2},{2,0},{4,6},{6,4},{1,3},{3,1},{5,7},{7,5},{8,10},{10,8},{12,... | collective-permute-start | bytes 196616 | tf_op jit(solution)/shard_map/ppermute | solution.py:159
  15.8 2.6 %collective-permute-start.4 = (bf16[64,512]{1,0:T(8,128)(2,1)S(1)}, bf16[64,512]{1,0:T(8,128)(2,1)S(1)}, u32[]{:S(2)}, u32[]{:S(2)}) collective-permute-start(bf16[64,512]{1,0:T(8,128)(2,1)S(1)} %get-tuple-element.24), channel_id=1, source_target_pairs={{0,4},{2,6},{4,0},{6,2},{1,5},{3,7},{5,1},{7,3},{8,12},{10,14},{12... | collective-permute-start | bytes 196616 | tf_op jit(solution)/shard_map/ppermute | solution.py:159
  18.4 0.2 collective-permute-start.5
  18.6 0.0 collective-permute-start.6
  18.6 0.0 collective-permute-done.3.refs_1_
  18.6 0.5 collective-permute-start.7
  19.2 3.2 %collective-permute-done.4.refs_2_ = bf16[64,512]{1,0:T(8,128)(2,1)S(1)} collective-permute-done((bf16[64,512]{1,0:T(8,128)(2,1)S(1)}, bf16[64,512]{1,0:T(8,128)(2,1)S(1)}, u32[]{:S(2)}, u32[]{:S(2)}) %collective-permute-start.4) | collective-permute-done | bytes 65568 | tf_op jit(solution)/shard_map/ppermute | solution.py:159
  22.4 0.0 collective-permute-start.8
  22.4 2.1 %collective-permute-done.5.refs_3_ = bf16[64,512]{1,0:T(8,128)(2,1)S(1)} collective-permute-done((bf16[64,512]{1,0:T(8,128)(2,1)S(1)}, bf16[64,512]{1,0:T(8,128)(2,1)S(1)}, u32[]{:S(2)}, u32[]{:S(2)}) %collective-permute-start.5) | collective-permute-done | bytes 65568 | tf_op jit(solution)/shard_map/ppermute | solution.py:159
  24.5 0.0 collective-permute-start.9
  24.5 0.0 copy-done.4
  24.5 0.1 copy.6.scales
  24.6 0.0 copy-done
  24.6 1.5 %shard_map.57.refs_8_ = bf16[1024,768]{1,0:T(8,128)(2,1)S(1)} custom-call(s32[3]{0:T(128)S(1)} %pad_add_fusion.me, f32[8,2,3]{2,1,0:T(2,128)S(1)} %copy.6.scales, bf16[1024,2,384]{2,1,0:T(2,128)(2,1)S(1)} %bitcast.11), custom_call_target="tpu_custom_call" | custom-call | bytes 8388608 | tf_op jit(solution)/shard_map/pallas_call | solution.py:18
  26.1 0.0 collective-permute-done.6.refs_4_
  26.1 0.0 collective-permute-done.7.refs_5_
  26.1 0.0 collective-permute-done.8.refs_6_
  26.1 0.0 collective-permute-done.9.refs_7_
  26.1 1.2 %shard_map.58 = (f32[64,768]{1,0:T(8,128)S(1)}, bf16[64,768]{1,0:T(8,128)(2,1)S(1)}, bf16[64,768]{1,0:T(8,128)(2,1)S(1)}, bf16[64,768]{1,0:T(8,128)(2,1)S(1)}) custom-call(bf16[64,512]{1,0:T(8,128)(2,1)S(1)} %get-tuple-element.22.refs_0_, bf16[64,512]{1,0:T(8,128)(2,1)S(1)} %collective-permute-done.3.refs_1_, ...), custom_call_target="tpu_custom_call" | custom-call | flops 402653184 | bytes 3145728 | tf_op jit(solution)/shard_map/pallas_call | solution.py:18
  27.3 0.1 collective-permute-start.10
  27.4 1.4 %collective-permute-start.11 = (bf16[64,768]{1,0:T(8,128)(2,1)S(1)}, bf16[64,768]{1,0:T(8,128)(2,1)S(1)}, u32[]{:S(2)}, u32[]{:S(2)}) collective-permute-start(bf16[64,768]{1,0:T(8,128)(2,1)S(1)} %get-tuple-element.28), channel_id=1, source_target_pairs={{0,4},{2,6},{4,0},{6,2},{1,5},{3,7},{5,1},{7,3},{8,12},{10,14},{12... | collective-permute-start | bytes 294920 | tf_op jit(solution)/shard_map/ppermute | solution.py:159
  28.8 3.0 %collective-permute-start.12 = (bf16[64,768]{1,0:T(8,128)(2,1)S(1)}, bf16[64,768]{1,0:T(8,128)(2,1)S(1)}, u32[]{:S(2)}, u32[]{:S(2)}) collective-permute-start(bf16[64,768]{1,0:T(8,128)(2,1)S(1)} %get-tuple-element.29), channel_id=1, source_target_pairs={{0,6},{2,4},{4,2},{6,0},{1,7},{3,5},{5,3},{7,1},{8,14},{10,12},{12... | collective-permute-start | bytes 294920 | tf_op jit(solution)/shard_map/ppermute | solution.py:159
  31.8 2.0 %collective-permute-done.10.refs_1_ = bf16[64,768]{1,0:T(8,128)(2,1)S(1)} collective-permute-done((bf16[64,768]{1,0:T(8,128)(2,1)S(1)}, bf16[64,768]{1,0:T(8,128)(2,1)S(1)}, u32[]{:S(2)}, u32[]{:S(2)}) %collective-permute-start.10) | collective-permute-done | bytes 98336 | tf_op jit(solution)/shard_map/ppermute | solution.py:159
  33.8 4.5 %collective-permute-done.11.refs_2_ = bf16[64,768]{1,0:T(8,128)(2,1)S(1)} collective-permute-done((bf16[64,768]{1,0:T(8,128)(2,1)S(1)}, bf16[64,768]{1,0:T(8,128)(2,1)S(1)}, u32[]{:S(2)}, u32[]{:S(2)}) %collective-permute-start.11) | collective-permute-done | bytes 98336 | tf_op jit(solution)/shard_map/ppermute | solution.py:159
  38.2 0.0 collective-permute-done.12.refs_3_
  38.2 0.1 shard_map.59.refs_0_
  38.3 1.8 %collective-permute-start.15 = (bf16[64,768]{1,0:T(8,128)(2,1)S(1)}, bf16[64,768]{1,0:T(8,128)(2,1)S(1)}, u32[]{:S(2)}, u32[]{:S(2)}) collective-permute-start(bf16[64,768]{1,0:T(8,128)(2,1)S(1)} %shard_map.59.refs_0_), channel_id=1, source_target_pairs={{0,6},{2,4},{4,2},{6,0},{1,7},{3,5},{5,3},{7,1},{8,14},{10,12},{12... | collective-permute-start | bytes 294920 | tf_op jit(solution)/shard_map/ppermute | solution.py:159
  40.1 2.0 %collective-permute-start.14 = (bf16[64,768]{1,0:T(8,128)(2,1)S(1)}, bf16[64,768]{1,0:T(8,128)(2,1)S(1)}, u32[]{:S(2)}, u32[]{:S(2)}) collective-permute-start(bf16[64,768]{1,0:T(8,128)(2,1)S(1)} %shard_map.59.refs_0_), channel_id=1, source_target_pairs={{0,4},{2,6},{4,0},{6,2},{1,5},{3,7},{5,1},{7,3},{8,12},{10,14},{12... | collective-permute-start | bytes 294920 | tf_op jit(solution)/shard_map/ppermute | solution.py:159
  42.1 0.6 %collective-permute-start.13 = (bf16[64,768]{1,0:T(8,128)(2,1)S(1)}, bf16[64,768]{1,0:T(8,128)(2,1)S(1)}, u32[]{:S(2)}, u32[]{:S(2)}) collective-permute-start(bf16[64,768]{1,0:T(8,128)(2,1)S(1)} %shard_map.59.refs_0_), channel_id=1, source_target_pairs={{0,2},{2,0},{4,6},{6,4},{1,3},{3,1},{5,7},{7,5},{8,10},{10,8},{12,... | collective-permute-start | bytes 294920 | tf_op jit(solution)/shard_map/ppermute | solution.py:159
  42.8 2.4 %shard_map.60.refs_4_ = bf16[2048,512]{1,0:T(8,128)(2,1)S(1)} custom-call(s32[3]{0:T(128)S(1)} %pad_add_fusion.me, bf16[64,512]{1,0:T(8,128)(2,1)S(1)} %get-tuple-element.22.refs_0_, bf16[64,512]{1,0:T(8,128)(2,1)S(1)} %collective-permute-done.3.refs_1_, bf16[64,512]{1,0:T(8,128)(2,1)S(1)} %collective-permute-done.4.refs_2_, ...), custom_call_target="tpu_custom_call" | custom-call | bytes 8388608 | tf_op jit(solution)/shard_map/pallas_call | solution.py:18
  45.2 0.5 %collective-permute-done.15.refs_3_ = bf16[64,768]{1,0:T(8,128)(2,1)S(1)} collective-permute-done((bf16[64,768]{1,0:T(8,128)(2,1)S(1)}, bf16[64,768]{1,0:T(8,128)(2,1)S(1)}, u32[]{:S(2)}, u32[]{:S(2)}) %collective-permute-start.15) | collective-permute-done | bytes 98336 | tf_op jit(solution)/shard_map/ppermute | solution.py:159
  45.8 4.8 %collective-permute-done.14.refs_2_ = bf16[64,768]{1,0:T(8,128)(2,1)S(1)} collective-permute-done((bf16[64,768]{1,0:T(8,128)(2,1)S(1)}, bf16[64,768]{1,0:T(8,128)(2,1)S(1)}, u32[]{:S(2)}, u32[]{:S(2)}) %collective-permute-start.14) | collective-permute-done | bytes 98336 | tf_op jit(solution)/shard_map/ppermute | solution.py:159
  50.5 0.0 collective-permute-done.13.refs_1_
  50.6 3.2 %shard_map.61 = bf16[1024,2,384]{2,1,0:T(2,128)(2,1)} custom-call(bf16[64,768]{1,0:T(8,128)(2,1)S(1)} %shard_map.59.refs_0_, bf16[64,768]{1,0:T(8,128)(2,1)S(1)} %collective-permute-done.13.refs_1_, bf16[64,768]{1,0:T(8,128)(2,1)S(1)} %collective-permute-done.14.refs_2_, bf16[64,768]{1,0:T(8,128)(2,1)S(1)} %collective-permute-done.15.refs_3_, ...), custom_call_target="tpu_custom_call" | custom-call | flops 805306368 | bytes 4194304 | tf_op jit(solution)/shard_map/pallas_call | solution.py:18
  (4 shorter events, 0.0 us)
Async XLA Ops:
  0.0 24.6 %copy-start = (bf16[1024,1,2,384]{3,2,1,0:T(2,128)(2,1)S(1)}, bf16[1024,1,2,384]{3,2,1,0:T(2,128)(2,1)}, u32[]{:S(2)}) copy-start(bf16[1024,1,2,384]{3,2,1,0:T(2,128)(2,1)} %param.8) | copy-start | bytes 4718596
  0.1 1.3 %copy-start.1 = (bf16[128,4096]{1,0:T(8,128)(2,1)S(1)}, bf16[128,4096]{1,0:T(8,128)(2,1)}, u32[]{:S(2)}) copy-start(bf16[128,4096]{1,0:T(8,128)(2,1)} %tokens.1) | copy-start | bytes 3145732
  1.4 1.1 %copy-start.2 = (bf16[128,8,384]{2,1,0:T(8,128)(2,1)S(1)}, bf16[128,8,384]{2,1,0:T(8,128)(2,1)}, u32[]{:S(2)}) copy-start(bf16[128,8,384]{2,1,0:T(8,128)(2,1)} %act.1) | copy-start | bytes 2359300
  2.5 0.7 %copy-start.3 = (s32[128,8]{0,1:T(8,128)S(1)}, s32[128,8]{0,1:T(8,128)}, u32[]{:S(2)}) copy-start(s32[128,8]{0,1:T(8,128)} %param.6) | copy-start | bytes 12292
  3.2 21.3 %copy-start.4 = (bf16[8,1,2,3]{0,2,3,1:T(2,128)(2,1)S(1)}, bf16[8,1,2,3]{0,2,3,1:T(2,128)(2,1)}, u32[]{:S(2)}) copy-start(bf16[8,1,2,3]{0,2,3,1:T(2,128)(2,1)} %param.9) | copy-start | bytes 292
  4.3 5.6 %collective-permute-start = (bf16[16,2432]{1,0:T(8,128)(2,1)S(1)}, bf16[16,2432]{1,0:T(8,128)(2,1)S(1)}, u32[]{:S(2)}, u32[]{:S(2)}) collective-permute-start(bf16[16,2432]{1,0:T(8,128)(2,1)S(1)} %get-tuple-element.19), channel_id=1, source_target_pairs={{0,8},{8,0},{16,24},{24,16},{1,9},{9,1},{17,25},{25,17},{2,10},{10... | collective-permute-start | bytes 233480 | tf_op jit(solution)/shard_map/ppermute | solution.py:159
  7.4 5.2 %collective-permute-start.1 = (bf16[16,2432]{1,0:T(8,128)(2,1)S(1)}, bf16[16,2432]{1,0:T(8,128)(2,1)S(1)}, u32[]{:S(2)}, u32[]{:S(2)}) collective-permute-start(bf16[16,2432]{1,0:T(8,128)(2,1)S(1)} %get-tuple-element.20), channel_id=1, source_target_pairs={{0,16},{8,24},{16,0},{24,8},{1,17},{9,25},{17,1},{25,9},{2,18},{10... | collective-permute-start | bytes 233480 | tf_op jit(solution)/shard_map/ppermute | solution.py:159
  8.9 5.3 %collective-permute-start.2 = (bf16[16,2432]{1,0:T(8,128)(2,1)S(1)}, bf16[16,2432]{1,0:T(8,128)(2,1)S(1)}, u32[]{:S(2)}, u32[]{:S(2)}) collective-permute-start(bf16[16,2432]{1,0:T(8,128)(2,1)S(1)} %get-tuple-element.21), channel_id=1, source_target_pairs={{0,24},{8,16},{16,8},{24,0},{1,25},{9,17},{17,9},{25,1},{2,26},{10... | collective-permute-start | bytes 233480 | tf_op jit(solution)/shard_map/ppermute | solution.py:159
  14.2 4.5 %collective-permute-start.3 = (bf16[64,512]{1,0:T(8,128)(2,1)S(1)}, bf16[64,512]{1,0:T(8,128)(2,1)S(1)}, u32[]{:S(2)}, u32[]{:S(2)}) collective-permute-start(bf16[64,512]{1,0:T(8,128)(2,1)S(1)} %get-tuple-element.23), channel_id=1, source_target_pairs={{0,2},{2,0},{4,6},{6,4},{1,3},{3,1},{5,7},{7,5},{8,10},{10,8},{12,... | collective-permute-start | bytes 196616 | tf_op jit(solution)/shard_map/ppermute | solution.py:159
  15.8 6.6 %collective-permute-start.4 = (bf16[64,512]{1,0:T(8,128)(2,1)S(1)}, bf16[64,512]{1,0:T(8,128)(2,1)S(1)}, u32[]{:S(2)}, u32[]{:S(2)}) collective-permute-start(bf16[64,512]{1,0:T(8,128)(2,1)S(1)} %get-tuple-element.24), channel_id=1, source_target_pairs={{0,4},{2,6},{4,0},{6,2},{1,5},{3,7},{5,1},{7,3},{8,12},{10,14},{12... | collective-permute-start | bytes 196616 | tf_op jit(solution)/shard_map/ppermute | solution.py:159
  18.4 6.1 %collective-permute-start.5 = (bf16[64,512]{1,0:T(8,128)(2,1)S(1)}, bf16[64,512]{1,0:T(8,128)(2,1)S(1)}, u32[]{:S(2)}, u32[]{:S(2)}) collective-permute-start(bf16[64,512]{1,0:T(8,128)(2,1)S(1)} %get-tuple-element.25), channel_id=1, source_target_pairs={{0,6},{2,4},{4,2},{6,0},{1,7},{3,5},{5,3},{7,1},{8,14},{10,12},{12... | collective-permute-start | bytes 196616 | tf_op jit(solution)/shard_map/ppermute | solution.py:159
  18.6 7.4 %collective-permute-start.6 = (bf16[64,512]{1,0:T(8,128)(2,1)S(1)}, bf16[64,512]{1,0:T(8,128)(2,1)S(1)}, u32[]{:S(2)}, u32[]{:S(2)}) collective-permute-start(bf16[64,512]{1,0:T(8,128)(2,1)S(1)} %get-tuple-element.22.refs_0_), channel_id=1, source_target_pairs={{0,1},{1,0},{2,3},{3,2},{4,5},{5,4},{6,7},{7,6},{8,9},{9,8},{10,11... | collective-permute-start | bytes 196616 | tf_op jit(solution)/shard_map/ppermute | solution.py:159
  18.6 7.4 %collective-permute-start.7 = (bf16[64,512]{1,0:T(8,128)(2,1)S(1)}, bf16[64,512]{1,0:T(8,128)(2,1)S(1)}, u32[]{:S(2)}, u32[]{:S(2)}) collective-permute-start(bf16[64,512]{1,0:T(8,128)(2,1)S(1)} %collective-permute-done.3.refs_1_), channel_id=1, source_target_pairs={{0,1},{1,0},{2,3},{3,2},{4,5},{5,4},{6,7},{7,6},{8,9},{9,8},{10,11... | collective-permute-start | bytes 196616 | tf_op jit(solution)/shard_map/ppermute | solution.py:159
  22.4 3.7 %collective-permute-start.8 = (bf16[64,512]{1,0:T(8,128)(2,1)S(1)}, bf16[64,512]{1,0:T(8,128)(2,1)S(1)}, u32[]{:S(2)}, u32[]{:S(2)}) collective-permute-start(bf16[64,512]{1,0:T(8,128)(2,1)S(1)} %collective-permute-done.4.refs_2_), channel_id=1, source_target_pairs={{0,1},{1,0},{2,3},{3,2},{4,5},{5,4},{6,7},{7,6},{8,9},{9,8},{10,11... | collective-permute-start | bytes 196616 | tf_op jit(solution)/shard_map/ppermute | solution.py:159
  24.5 1.6 %collective-permute-start.9 = (bf16[64,512]{1,0:T(8,128)(2,1)S(1)}, bf16[64,512]{1,0:T(8,128)(2,1)S(1)}, u32[]{:S(2)}, u32[]{:S(2)}) collective-permute-start(bf16[64,512]{1,0:T(8,128)(2,1)S(1)} %collective-permute-done.5.refs_3_), channel_id=1, source_target_pairs={{0,1},{1,0},{2,3},{3,2},{4,5},{5,4},{6,7},{7,6},{8,9},{9,8},{10,11... | collective-permute-start | bytes 196616 | tf_op jit(solution)/shard_map/ppermute | solution.py:159
  27.3 6.4 %collective-permute-start.10 = (bf16[64,768]{1,0:T(8,128)(2,1)S(1)}, bf16[64,768]{1,0:T(8,128)(2,1)S(1)}, u32[]{:S(2)}, u32[]{:S(2)}) collective-permute-start(bf16[64,768]{1,0:T(8,128)(2,1)S(1)} %get-tuple-element.27), channel_id=1, source_target_pairs={{0,2},{2,0},{4,6},{6,4},{1,3},{3,1},{5,7},{7,5},{8,10},{10,8},{12,... | collective-permute-start | bytes 294920 | tf_op jit(solution)/shard_map/ppermute | solution.py:159
  27.4 10.8 %collective-permute-start.11 = (bf16[64,768]{1,0:T(8,128)(2,1)S(1)}, bf16[64,768]{1,0:T(8,128)(2,1)S(1)}, u32[]{:S(2)}, u32[]{:S(2)}) collective-permute-start(bf16[64,768]{1,0:T(8,128)(2,1)S(1)} %get-tuple-element.28), channel_id=1, source_target_pairs={{0,4},{2,6},{4,0},{6,2},{1,5},{3,7},{5,1},{7,3},{8,12},{10,14},{12... | collective-permute-start | bytes 294920 | tf_op jit(solution)/shard_map/ppermute | solution.py:159
  28.8 9.5 %collective-permute-start.12 = (bf16[64,768]{1,0:T(8,128)(2,1)S(1)}, bf16[64,768]{1,0:T(8,128)(2,1)S(1)}, u32[]{:S(2)}, u32[]{:S(2)}) collective-permute-start(bf16[64,768]{1,0:T(8,128)(2,1)S(1)} %get-tuple-element.29), channel_id=1, source_target_pairs={{0,6},{2,4},{4,2},{6,0},{1,7},{3,5},{5,3},{7,1},{8,14},{10,12},{12... | collective-permute-start | bytes 294920 | tf_op jit(solution)/shard_map/ppermute | solution.py:159
  38.3 7.4 %collective-permute-start.15 = (bf16[64,768]{1,0:T(8,128)(2,1)S(1)}, bf16[64,768]{1,0:T(8,128)(2,1)S(1)}, u32[]{:S(2)}, u32[]{:S(2)}) collective-permute-start(bf16[64,768]{1,0:T(8,128)(2,1)S(1)} %shard_map.59.refs_0_), channel_id=1, source_target_pairs={{0,6},{2,4},{4,2},{6,0},{1,7},{3,5},{5,3},{7,1},{8,14},{10,12},{12... | collective-permute-start | bytes 294920 | tf_op jit(solution)/shard_map/ppermute | solution.py:159
  40.1 10.4 %collective-permute-start.14 = (bf16[64,768]{1,0:T(8,128)(2,1)S(1)}, bf16[64,768]{1,0:T(8,128)(2,1)S(1)}, u32[]{:S(2)}, u32[]{:S(2)}) collective-permute-start(bf16[64,768]{1,0:T(8,128)(2,1)S(1)} %shard_map.59.refs_0_), channel_id=1, source_target_pairs={{0,4},{2,6},{4,0},{6,2},{1,5},{3,7},{5,1},{7,3},{8,12},{10,14},{12... | collective-permute-start | bytes 294920 | tf_op jit(solution)/shard_map/ppermute | solution.py:159
  42.1 8.4 %collective-permute-start.13 = (bf16[64,768]{1,0:T(8,128)(2,1)S(1)}, bf16[64,768]{1,0:T(8,128)(2,1)S(1)}, u32[]{:S(2)}, u32[]{:S(2)}) collective-permute-start(bf16[64,768]{1,0:T(8,128)(2,1)S(1)} %shard_map.59.refs_0_), channel_id=1, source_target_pairs={{0,2},{2,0},{4,6},{6,4},{1,3},{3,1},{5,7},{7,5},{8,10},{10,8},{12,... | collective-permute-start | bytes 294920 | tf_op jit(solution)/shard_map/ppermute | solution.py:159

commit v2 on v1

v2 whole, which is shorter than its diff:
```python
import functools

import jax
import jax.numpy as jnp
from jax import lax
from jax.experimental import pallas as pl
from jax.experimental.pallas import tpu as pltpu
from jax.sharding import PartitionSpec as P

CAP = 16
BF16 = jnp.bfloat16
F32 = jnp.float32
VMEM_BYTES = 40 * 1024 * 1024
PACK_VMEM = 60 * 1024 * 1024


def call(kernel, out_shape, args, in_specs, out_specs=None, scratch=(), flops=0, nbytes=0, vmem_bytes=VMEM_BYTES):
    vmem = pl.BlockSpec(memory_space=pltpu.VMEM)
    return pl.pallas_call(
        kernel,
        out_shape=out_shape,
        in_specs=in_specs,
        out_specs=jax.tree.map(lambda _: vmem, out_shape) if out_specs is None else out_specs,
        scratch_shapes=scratch,
        compiler_params=pltpu.CompilerParams(vmem_limit_bytes=vmem_bytes),
        cost_estimate=pl.CostEstimate(flops=flops, bytes_accessed=nbytes, transcendentals=0),
    )(*args)


VMEM = pl.BlockSpec(memory_space=pltpu.VMEM)
SMEM = pl.BlockSpec(memory_space=pltpu.SMEM)
HBM = pl.BlockSpec(memory_space=pltpu.HBM)


def dot(a, b, dims=((1,), (0,))):
    return lax.dot_general(a, b, (dims, ((), ())), preferred_element_type=F32)


def iota(shape, dim):
    return lax.broadcasted_iota(jnp.int32, shape, dim)


def own_half(halves):
    return lax.axis_index("att") if halves == 2 else 0


def pack_kernel(ng, nb, halves, tokens, routed, act, *refs):
    outs, (token_buf, routed_buf, act_buf, sem) = refs[:ng], refs[ng:]
    top, count = routed.shape
    rows = ng * CAP
    width = tokens.shape[1] // (nb * halves)
    group, block, half = lax.axis_index("group"), lax.axis_index("blk"), own_half(halves)
    copies = [pltpu.make_async_copy(routed, routed_buf, sem.at[0])]
    copies.append(pltpu.make_async_copy(act, act_buf, sem.at[1]))
    for p in range(nb):
        start = pl.multiple_of(((block ^ p) * halves + half) * width, width)
        copies.append(
            pltpu.make_async_copy(tokens.at[:, pl.ds(start, width)], token_buf.at[p], sem.at[2 + p])
        )
    for copy in copies:
        copy.start()
    upto = (iota((count, count), 0) <= iota((count, count), 1)).astype(F32).astype(BF16)
    spread = (iota((count, count * top), 1) // top == iota((count, count * top), 0)).astype(F32).astype(BF16)
    own_slot = iota((top, count * top), 1) % top == iota((top, count * top), 0)
    slot = (iota((rows, count), 0) % CAP + 1).astype(F32)
    expert = (group ^ (iota((rows, 1), 0) // CAP)).astype(F32)
    copies[0].wait()
    ids = routed_buf[...]
    chosen = [jnp.sum((ids == (group ^ s)).astype(F32), axis=0, keepdims=True) for s in range(ng)]
    chosen_rows = jnp.concatenate([jnp.broadcast_to(c, (CAP, count)) for c in chosen], axis=0)
    place = dot(chosen_rows.astype(BF16), upto)
    selector = jnp.where(place == slot, chosen_rows, 0.0).astype(BF16)
    ids_wide = dot(ids.astype(F32).astype(BF16), spread)
    ids_flat = jnp.sum(jnp.where(own_slot, ids_wide, 0.0), axis=0, keepdims=True)
    pair = jnp.where(ids_flat == expert, dot(selector, spread), 0.0).astype(BF16)
    copies[1].wait()
    hidden = act.shape[2]
    cot = dot(pair, act_buf[...].reshape(count * top, hidden)).astype(BF16)
    for s in range(ng):
        outs[s][:, nb * width :] = cot[s * CAP : (s + 1) * CAP]
    for p in range(nb):
        copies[2 + p].wait()
        part = dot(selector, token_buf[p]).astype(BF16)
        for s in range(ng):
            outs[s][:, p * width : (p + 1) * width] = part[s * CAP : (s + 1) * CAP]


def regroup_kernel(ng, nb, width, *refs):
    pieces, outs = refs[:ng], refs[ng:]
    for s in range(ng):
        for p in range(nb):
            outs[p][s * CAP : (s + 1) * CAP, :] = pieces[s][:, p * width : (p + 1) * width]
        outs[nb][s * CAP : (s + 1) * CAP, :] = pieces[s][:, nb * width :]


def weights_kernel(halves, scales, codes, out):
    depth, _, hidden = codes.shape
    blocks, _, cols = scales.shape
    qrows, qcols = depth // blocks, hidden // cols
    half = own_half(halves)
    per_half = blocks // halves
    pick = [
        (iota((qrows, 2 * qrows), 1) == 2 * iota((qrows, 2 * qrows), 0) + j).astype(F32).astype(BF16)
        for j in range(2)
    ]
    for q in range(blocks):
        source = (q + half * per_half) % blocks if halves > 1 else q
        rows = codes[pl.ds(pl.multiple_of(source * qrows, qrows), qrows)].reshape(2 * qrows, hidden)
        for j in range(2):
            values = dot(pick[j], rows)
            for c in range(cols):
                at = j * hidden + c * qcols
                out[q * qrows : (q + 1) * qrows, at : at + qcols] = (
                    values[:, c * qcols : (c + 1) * qcols] * scales[source, j, c]
                ).astype(BF16)


def gate_up_kernel(nb, halves, *refs):
    pieces, weights, outs = refs[: nb * halves], refs[nb * halves], refs[nb * halves + 1 :]
    rows, width = pieces[0].shape
    for p in range(nb):
        total = dot(pieces[p][...], weights[:width])
        for h in range(1, halves):
            total += dot(pieces[h * nb + p][...], weights[h * width : (h + 1) * width])
        outs[p][...] = total.astype(outs[p].dtype)


def features_kernel(nb, halves, *refs):
    pieces, out = refs[: nb * halves], refs[nb * halves]
    rows, width = pieces[0].shape
    half = own_half(halves)
    for h in range(halves):
        start = pl.multiple_of((half ^ h) * width, width)
        for p in range(nb):
            out[p * rows : (p + 1) * rows, pl.ds(start, width)] = pieces[h * nb + p][...]


def swiglu_kernel(nb, *refs):
    parts, cot, out = refs[:nb], refs[nb], refs[nb + 1]
    hidden = cot.shape[1]
    total = parts[0][...]
    for p in range(1, nb):
        total += parts[p][...].astype(F32)
    gate, up = total[:, :hidden], total[:, hidden:]
    c = cot[...].astype(F32)
    s = jax.nn.sigmoid(gate)
    out[:, :hidden] = (c * up * s * (1.0 + gate * (1.0 - s))).astype(BF16)
    out[:, hidden:] = (c * gate * s).astype(BF16)


def gradient_kernel(nb, *refs):
    parts, features, out, stacked, buf, sem = refs[:nb], *refs[nb:]
    rows = parts[0].shape[0]
    depth, _, hidden = out.shape
    for p in range(nb):
        stacked[p * rows : (p + 1) * rows, :] = parts[p][...]
    step = min(128, depth)
    copies = []
    for k in range(depth // step):
        at = slice(k * step, (k + 1) * step)
        for j in range(2):
            buf[at, j, :] = dot(
                features[:, at], stacked[:, j * hidden : (j + 1) * hidden], ((0,), (0,))
            ).astype(BF16)
        copies.append(pltpu.make_async_copy(buf.at[at], out.at[at], sem.at[k]))
        copies[-1].start()
    for copy in copies:
        copy.wait()


def swap(x, axis, size, s):
    return lax.ppermute(x, axis, [(i, i ^ s) for i in range(size)])


def local(tokens, routed_experts, act_cotangent, weight_codes, weight_scales):
    ng, nb, na = lax.axis_size("group"), lax.axis_size("blk"), lax.axis_size("att")
    depth, _, _, hidden = weight_codes.shape
    halves = 2 if na == 2 and depth % 256 == 0 else 1
    width = depth // halves
    rows = ng * CAP
    sds = jax.ShapeDtypeStruct
    top, count = routed_experts.shape[1], tokens.shape[0]
    sent = call(
        functools.partial(pack_kernel, ng, nb, halves),
        [sds((CAP, nb * width + hidden), BF16)] * ng,
        (tokens, routed_experts.T, act_cotangent),
        [HBM, HBM, HBM],
        scratch=[
            pltpu.VMEM((nb, count, width), BF16),
            pltpu.VMEM((top, count), jnp.int32),
            pltpu.VMEM(act_cotangent.shape, BF16),
            pltpu.SemaphoreType.DMA((2 + nb,)),
        ],
        nbytes=2 << 20,
        vmem_bytes=PACK_VMEM,
    )
    codes, *sent = lax.optimization_barrier((weight_codes, *sent))
    weights = call(
        functools.partial(weights_kernel, halves),
        sds((depth, 2 * hidden), BF16),
        (weight_scales[:, 0].astype(F32), codes[:, 0]),
        [SMEM, VMEM],
        nbytes=4 << 20,
    )
    pieces = [sent[0]] + [swap(sent[s], "group", ng, s) for s in range(1, ng)]
    weights, *pieces = lax.optimization_barrier((weights, *pieces))
    *columns, cot = call(
        functools.partial(regroup_kernel, ng, nb, width),
        [sds((rows, width), BF16)] * nb + [sds((rows, hidden), BF16)],
        pieces,
        [VMEM] * ng,
        nbytes=1 << 20,
    )
    x = [columns[0]] + [swap(columns[p], "blk", nb, p) for p in range(1, nb)]
    if halves == 2:
        x += [swap(piece, "att", 2, 1) for piece in x]
    *partial, = call(
        functools.partial(gate_up_kernel, nb, halves),
        [sds((rows, 2 * hidden), F32)] + [sds((rows, 2 * hidden), BF16)] * (nb - 1),
        (*x, weights),
        [VMEM] * (nb * halves + 1),
        flops=2 * nb * rows * depth * 2 * hidden,
        nbytes=3 << 20,
    )
    *x, partial[1] = lax.optimization_barrier((*x, partial[1]))
    features = call(
        functools.partial(features_kernel, nb, halves),
        sds((nb * rows, depth), BF16),
        x,
        [VMEM] * (nb * halves),
        nbytes=3 << 20,
    )
    parts = [partial[0]] + [swap(partial[p], "blk", nb, p) for p in range(1, nb)]
    features, *parts = lax.optimization_barrier((features, *parts))
    own = call(
        functools.partial(swiglu_kernel, nb),
        sds((rows, 2 * hidden), BF16),
        (*parts, cot),
        [VMEM] * (nb + 1),
        nbytes=1 << 20,
    )
    gathered = [own] + [swap(own, "blk", nb, p) for p in range(1, nb)]
    step = min(128, depth)
    gradient = call(
        functools.partial(gradient_kernel, nb),
        sds((depth, 2, hidden), BF16),
        (*gathered, features),
        [VMEM] * (nb + 1),
        out_specs=HBM,
        scratch=[
            pltpu.VMEM((nb * rows, 2 * hidden), BF16),
            pltpu.VMEM((depth, 2, hidden), BF16),
            pltpu.SemaphoreType.DMA((depth // step,)),
        ],
        flops=2 * nb * rows * depth * 2 * hidden,
        nbytes=4 << 20,
    )
    return gradient[:, None]


def solution(mesh):
    return jax.shard_map(
        local,
        mesh=mesh,
        in_specs=(
            P(("group", "blk"), None),
            P(("group", "blk"), None),
            P(("group", "blk"), None, "att"),
            P("blk", "group", None, "att"),
            P("blk", "group", None, "att"),
        ),
        out_specs=P("blk", "group", None, "att"),
        check_vma=False,
    )
```

time: 53.9 us -> 50.7 us (0.941)
  local copies, waits for them, and re-layouts: 3.25 us -> 0.11 us
  waiting for transfers between devices: 22.4 us -> 23.9 us
  Pallas kernels: 9.54 us -> 8.14 us
    unnamed x10 -> x6, local copies, waits for them, and re-layouts: 3.16 us -> 0.01 us
    ppermute x16, waiting for transfers between devices: 22.4 us -> 23.9 us  [swap(): return lax.ppermute(x, axis, [(i, i ^ s) for i in range(size)])]
    pallas_call x7, Pallas kernels: 9.54 us -> 8.14 us  [call(): pl.pallas_call(kernel, out_shape=out_shape, in_specs=in_specs, out_specs=...]
  transfers between devices with their start and end apart: 16 -> 16, of which waited for: 9 -> 9; matrix products, arithmetic and copies ran while one was open for 0% -> 0% of each run, Pallas kernels for 7% -> 3%
where the time goes in v2:
time: 50.7 us; the launch traced here: 50.6 us
  waiting for transfers between devices  23.9 us (47%)
  starting transfers between devices  18.4 us (36%)
  Pallas kernels  8.14 us (16%)
    ppermute x16, waiting for transfers between devices, swap(): return lax.ppermute(x, axis, [(i, i ^ s) for i in range(size)])  23.9 us
    ppermute x16, starting transfers between devices, swap(): return lax.ppermute(x, axis, [(i, i ^ s) for i in range(size)])  18.4 us
    pallas_call x7, Pallas kernels, call(): pl.pallas_call(kernel, out_shape=out_shape, in_specs=in_specs, out_specs=...  8.14 us
  transfers between devices with their start and end apart: 16, of which 9 were waited for; matrix products, arithmetic and copies ran while one was open for 0% of the time, Pallas kernels for 3%

profile of v2, /device:TPU:0, one launch (start us, length us, event | category | flops | bytes accessed | tf_op | source)
XLA Modules:
  0.0 50.6 jit_solution(12839368783010896230)
XLA Ops:
  0.0 0.0 copy-start
  0.0 0.0 copy-start.2
  0.0 2.9 %shard_map.55 = (bf16[16,2432]{1,0:T(8,128)(2,1)}, bf16[16,2432]{1,0:T(8,128)(2,1)}, bf16[16,2432]{1,0:T(8,128)(2,1)}, bf16[16,2432]{1,0:T(8,128)(2,1)}) custom-call(bf16[128,4096]{1,0:T(8,128)(2,1)} %tokens.1, s32[8,128]{1,0:T(8,128)} %bitcast.9, bf16[128,8,384]{2,1,0:T(8,128)(2,1)} %act.1), custom_call_target="tpu_custom_call" | custom-call | bytes 2097152 | tf_op jit(solution)/shard_map/pallas_call | solution.py:19
  3.0 3.0 %collective-permute-start = (bf16[16,2432]{1,0:T(8,128)(2,1)}, bf16[16,2432]{1,0:T(8,128)(2,1)S(1)}, u32[]{:S(2)}, u32[]{:S(2)}) collective-permute-start(bf16[16,2432]{1,0:T(8,128)(2,1)} %get-tuple-element.48), channel_id=1, source_target_pairs={{0,8},{8,0},{16,24},{24,16},{1,9},{9,1},{17,25},{25,17},{2,10},{10... | collective-permute-start | bytes 233480 | tf_op jit(solution)/shard_map/ppermute | solution.py:172
  6.0 1.5 %collective-permute-start.1 = (bf16[16,2432]{1,0:T(8,128)(2,1)}, bf16[16,2432]{1,0:T(8,128)(2,1)S(1)}, u32[]{:S(2)}, u32[]{:S(2)}) collective-permute-start(bf16[16,2432]{1,0:T(8,128)(2,1)} %get-tuple-element.49), channel_id=1, source_target_pairs={{0,16},{8,24},{16,0},{24,8},{1,17},{9,25},{17,1},{25,9},{2,18},{10... | collective-permute-start | bytes 233480 | tf_op jit(solution)/shard_map/ppermute | solution.py:172
  7.5 0.0 collective-permute-start.2
  7.5 0.0 copy-done.2
  7.5 0.1 copy.6.scales
  7.6 0.0 copy-done
  7.6 0.0 copy-start.1
  7.6 1.5 %shard_map.56.refs_8_ = bf16[1024,768]{1,0:T(8,128)(2,1)S(1)} custom-call(f32[8,2,3]{2,1,0:T(2,128)S(1)} %copy.6.scales, bf16[1024,2,384]{2,1,0:T(2,128)(2,1)S(1)} %bitcast.8), custom_call_target="tpu_custom_call" | custom-call | bytes 4194304 | tf_op jit(solution)/shard_map/pallas_call | solution.py:19
  9.1 0.0 collective-permute-done.refs_1_
  9.1 2.3 %collective-permute-done.1.refs_2_ = bf16[16,2432]{1,0:T(8,128)(2,1)S(1)} collective-permute-done((bf16[16,2432]{1,0:T(8,128)(2,1)}, bf16[16,2432]{1,0:T(8,128)(2,1)S(1)}, u32[]{:S(2)}, u32[]{:S(2)}) %collective-permute-start.1) | collective-permute-done | bytes 77856 | tf_op jit(solution)/shard_map/ppermute | solution.py:172
  11.4 1.6 %collective-permute-done.2.refs_3_ = bf16[16,2432]{1,0:T(8,128)(2,1)S(1)} collective-permute-done((bf16[16,2432]{1,0:T(8,128)(2,1)}, bf16[16,2432]{1,0:T(8,128)(2,1)S(1)}, u32[]{:S(2)}, u32[]{:S(2)}) %collective-permute-start.2) | collective-permute-done | bytes 77856 | tf_op jit(solution)/shard_map/ppermute | solution.py:172
  13.0 0.0 copy-done.1
  13.0 1.6 %collective-permute-start.3 = (bf16[64,512]{1,0:T(8,128)(2,1)S(1)}, bf16[64,512]{1,0:T(8,128)(2,1)S(1)}, u32[]{:S(2)}, u32[]{:S(2)}) collective-permute-start(bf16[64,512]{1,0:T(8,128)(2,1)S(1)} %get-tuple-element.56), channel_id=1, source_target_pairs={{0,2},{2,0},{4,6},{6,4},{1,3},{3,1},{5,7},{7,5},{8,10},{10,8},{12,... | collective-permute-start | bytes 196616 | tf_op jit(solution)/shard_map/ppermute | solution.py:172
  14.7 2.6 %collective-permute-start.4 = (bf16[64,512]{1,0:T(8,128)(2,1)S(1)}, bf16[64,512]{1,0:T(8,128)(2,1)S(1)}, u32[]{:S(2)}, u32[]{:S(2)}) collective-permute-start(bf16[64,512]{1,0:T(8,128)(2,1)S(1)} %get-tuple-element.57), channel_id=1, source_target_pairs={{0,4},{2,6},{4,0},{6,2},{1,5},{3,7},{5,1},{7,3},{8,12},{10,14},{12... | collective-permute-start | bytes 196616 | tf_op jit(solution)/shard_map/ppermute | solution.py:172
  17.2 0.2 collective-permute-start.5
  17.5 0.0 collective-permute-start.6
  17.5 0.0 collective-permute-done.3.refs_1_
  17.5 0.5 %collective-permute-start.7 = (bf16[64,512]{1,0:T(8,128)(2,1)S(1)}, bf16[64,512]{1,0:T(8,128)(2,1)S(1)}, u32[]{:S(2)}, u32[]{:S(2)}) collective-permute-start(bf16[64,512]{1,0:T(8,128)(2,1)S(1)} %collective-permute-done.3.refs_1_), channel_id=1, source_target_pairs={{0,1},{1,0},{2,3},{3,2},{4,5},{5,4},{6,7},{7,6},{8,9},{9,8},{10,11... | collective-permute-start | bytes 196616 | tf_op jit(solution)/shard_map/ppermute | solution.py:172
  18.0 3.2 %collective-permute-done.4.refs_2_ = bf16[64,512]{1,0:T(8,128)(2,1)S(1)} collective-permute-done((bf16[64,512]{1,0:T(8,128)(2,1)S(1)}, bf16[64,512]{1,0:T(8,128)(2,1)S(1)}, u32[]{:S(2)}, u32[]{:S(2)}) %collective-permute-start.4) | collective-permute-done | bytes 65568 | tf_op jit(solution)/shard_map/ppermute | solution.py:172
  21.2 0.0 collective-permute-start.8
  21.2 2.1 %collective-permute-done.5.refs_3_ = bf16[64,512]{1,0:T(8,128)(2,1)S(1)} collective-permute-done((bf16[64,512]{1,0:T(8,128)(2,1)S(1)}, bf16[64,512]{1,0:T(8,128)(2,1)S(1)}, u32[]{:S(2)}, u32[]{:S(2)}) %collective-permute-start.5) | collective-permute-done | bytes 65568 | tf_op jit(solution)/shard_map/ppermute | solution.py:172
  23.3 0.0 collective-permute-start.9
  23.3 0.0 collective-permute-done.6.refs_4_
  23.3 0.0 collective-permute-done.7.refs_5_
  23.3 0.0 collective-permute-done.8.refs_6_
  23.3 1.2 %collective-permute-done.9.refs_7_ = bf16[64,512]{1,0:T(8,128)(2,1)S(1)} collective-permute-done((bf16[64,512]{1,0:T(8,128)(2,1)S(1)}, bf16[64,512]{1,0:T(8,128)(2,1)S(1)}, u32[]{:S(2)}, u32[]{:S(2)}) %collective-permute-start.9) | collective-permute-done | bytes 65568 | tf_op jit(solution)/shard_map/ppermute | solution.py:172
  24.6 1.2 %shard_map.58 = (f32[64,768]{1,0:T(8,128)S(1)}, bf16[64,768]{1,0:T(8,128)(2,1)S(1)}, bf16[64,768]{1,0:T(8,128)(2,1)S(1)}, bf16[64,768]{1,0:T(8,128)(2,1)S(1)}) custom-call(bf16[64,512]{1,0:T(8,128)(2,1)S(1)} %get-tuple-element.61.refs_0_, bf16[64,512]{1,0:T(8,128)(2,1)S(1)} %collective-permute-done.3.refs_1_, ...), custom_call_target="tpu_custom_call" | custom-call | flops 402653184 | bytes 3145728 | tf_op jit(solution)/shard_map/pallas_call | solution.py:19
  25.8 0.1 collective-permute-start.10
  25.9 1.4 %collective-permute-start.11 = (bf16[64,768]{1,0:T(8,128)(2,1)S(1)}, bf16[64,768]{1,0:T(8,128)(2,1)S(1)}, u32[]{:S(2)}, u32[]{:S(2)}) collective-permute-start(bf16[64,768]{1,0:T(8,128)(2,1)S(1)} %get-tuple-element.71), channel_id=1, source_target_pairs={{0,4},{2,6},{4,0},{6,2},{1,5},{3,7},{5,1},{7,3},{8,12},{10,14},{12... | collective-permute-start | bytes 294920 | tf_op jit(solution)/shard_map/ppermute | solution.py:172
  27.2 3.0 %collective-permute-start.12 = (bf16[64,768]{1,0:T(8,128)(2,1)S(1)}, bf16[64,768]{1,0:T(8,128)(2,1)S(1)}, u32[]{:S(2)}, u32[]{:S(2)}) collective-permute-start(bf16[64,768]{1,0:T(8,128)(2,1)S(1)} %get-tuple-element.72), channel_id=1, source_target_pairs={{0,6},{2,4},{4,2},{6,0},{1,7},{3,5},{5,3},{7,1},{8,14},{10,12},{12... | collective-permute-start | bytes 294920 | tf_op jit(solution)/shard_map/ppermute | solution.py:172
  30.3 1.6 %collective-permute-done.10.refs_1_ = bf16[64,768]{1,0:T(8,128)(2,1)S(1)} collective-permute-done((bf16[64,768]{1,0:T(8,128)(2,1)S(1)}, bf16[64,768]{1,0:T(8,128)(2,1)S(1)}, u32[]{:S(2)}, u32[]{:S(2)}) %collective-permute-start.10) | collective-permute-done | bytes 98336 | tf_op jit(solution)/shard_map/ppermute | solution.py:172
  31.9 4.8 %collective-permute-done.11.refs_2_ = bf16[64,768]{1,0:T(8,128)(2,1)S(1)} collective-permute-done((bf16[64,768]{1,0:T(8,128)(2,1)S(1)}, bf16[64,768]{1,0:T(8,128)(2,1)S(1)}, u32[]{:S(2)}, u32[]{:S(2)}) %collective-permute-start.11) | collective-permute-done | bytes 98336 | tf_op jit(solution)/shard_map/ppermute | solution.py:172
  36.7 0.0 collective-permute-done.12.refs_3_
  36.7 0.1 shard_map.60.refs_0_
  36.8 1.6 %collective-permute-start.15 = (bf16[64,768]{1,0:T(8,128)(2,1)S(1)}, bf16[64,768]{1,0:T(8,128)(2,1)S(1)}, u32[]{:S(2)}, u32[]{:S(2)}) collective-permute-start(bf16[64,768]{1,0:T(8,128)(2,1)S(1)} %shard_map.60.refs_0_), channel_id=1, source_target_pairs={{0,6},{2,4},{4,2},{6,0},{1,7},{3,5},{5,3},{7,1},{8,14},{10,12},{12... | collective-permute-start | bytes 294920 | tf_op jit(solution)/shard_map/ppermute | solution.py:172
  38.4 1.8 %collective-permute-start.14 = (bf16[64,768]{1,0:T(8,128)(2,1)S(1)}, bf16[64,768]{1,0:T(8,128)(2,1)S(1)}, u32[]{:S(2)}, u32[]{:S(2)}) collective-permute-start(bf16[64,768]{1,0:T(8,128)(2,1)S(1)} %shard_map.60.refs_0_), channel_id=1, source_target_pairs={{0,4},{2,6},{4,0},{6,2},{1,5},{3,7},{5,1},{7,3},{8,12},{10,14},{12... | collective-permute-start | bytes 294920 | tf_op jit(solution)/shard_map/ppermute | solution.py:172
  40.2 1.0 %collective-permute-start.13 = (bf16[64,768]{1,0:T(8,128)(2,1)S(1)}, bf16[64,768]{1,0:T(8,128)(2,1)S(1)}, u32[]{:S(2)}, u32[]{:S(2)}) collective-permute-start(bf16[64,768]{1,0:T(8,128)(2,1)S(1)} %shard_map.60.refs_0_), channel_id=1, source_target_pairs={{0,2},{2,0},{4,6},{6,4},{1,3},{3,1},{5,7},{7,5},{8,10},{10,8},{12,... | collective-permute-start | bytes 294920 | tf_op jit(solution)/shard_map/ppermute | solution.py:172
  41.3 3.1 %collective-permute-done.15.refs_3_ = bf16[64,768]{1,0:T(8,128)(2,1)S(1)} collective-permute-done((bf16[64,768]{1,0:T(8,128)(2,1)S(1)}, bf16[64,768]{1,0:T(8,128)(2,1)S(1)}, u32[]{:S(2)}, u32[]{:S(2)}) %collective-permute-start.15) | collective-permute-done | bytes 98336 | tf_op jit(solution)/shard_map/ppermute | solution.py:172
  44.4 3.9 %collective-permute-done.14.refs_2_ = bf16[64,768]{1,0:T(8,128)(2,1)S(1)} collective-permute-done((bf16[64,768]{1,0:T(8,128)(2,1)S(1)}, bf16[64,768]{1,0:T(8,128)(2,1)S(1)}, u32[]{:S(2)}, u32[]{:S(2)}) %collective-permute-start.14) | collective-permute-done | bytes 98336 | tf_op jit(solution)/shard_map/ppermute | solution.py:172
  48.2 0.0 collective-permute-done.13.refs_1_
  48.2 2.4 %shard_map.61 = bf16[1024,2,384]{2,1,0:T(2,128)(2,1)} custom-call(bf16[64,768]{1,0:T(8,128)(2,1)S(1)} %shard_map.60.refs_0_, bf16[64,768]{1,0:T(8,128)(2,1)S(1)} %collective-permute-done.13.refs_1_, bf16[64,768]{1,0:T(8,128)(2,1)S(1)} %collective-permute-done.14.refs_2_, bf16[64,768]{1,0:T(8,128)(2,1)S(1)} %collective-permute-done.15.refs_3_, ...), custom_call_target="tpu_custom_call" | custom-call | flops 402653184 | bytes 4194304 | tf_op jit(solution)/shard_map/pallas_call | solution.py:19
  (3 shorter events, 0.1 us)
Async XLA Ops:
  0.0 7.6 %copy-start = (bf16[1024,1,2,384]{3,2,1,0:T(2,128)(2,1)S(1)}, bf16[1024,1,2,384]{3,2,1,0:T(2,128)(2,1)}, u32[]{:S(2)}) copy-start(bf16[1024,1,2,384]{3,2,1,0:T(2,128)(2,1)} %param.8) | copy-start | bytes 4718596
  0.0 7.5 %copy-start.2 = (bf16[8,1,2,3]{0,2,3,1:T(2,128)(2,1)S(1)}, bf16[8,1,2,3]{0,2,3,1:T(2,128)(2,1)}, u32[]{:S(2)}) copy-start(bf16[8,1,2,3]{0,2,3,1:T(2,128)(2,1)} %param.9) | copy-start | bytes 292
  3.0 6.1 %collective-permute-start = (bf16[16,2432]{1,0:T(8,128)(2,1)}, bf16[16,2432]{1,0:T(8,128)(2,1)S(1)}, u32[]{:S(2)}, u32[]{:S(2)}) collective-permute-start(bf16[16,2432]{1,0:T(8,128)(2,1)} %get-tuple-element.48), channel_id=1, source_target_pairs={{0,8},{8,0},{16,24},{24,16},{1,9},{9,1},{17,25},{25,17},{2,10},{10... | collective-permute-start | bytes 233480 | tf_op jit(solution)/shard_map/ppermute | solution.py:172
  6.0 5.4 %collective-permute-start.1 = (bf16[16,2432]{1,0:T(8,128)(2,1)}, bf16[16,2432]{1,0:T(8,128)(2,1)S(1)}, u32[]{:S(2)}, u32[]{:S(2)}) collective-permute-start(bf16[16,2432]{1,0:T(8,128)(2,1)} %get-tuple-element.49), channel_id=1, source_target_pairs={{0,16},{8,24},{16,0},{24,8},{1,17},{9,25},{17,1},{25,9},{2,18},{10... | collective-permute-start | bytes 233480 | tf_op jit(solution)/shard_map/ppermute | solution.py:172
  7.5 5.5 %collective-permute-start.2 = (bf16[16,2432]{1,0:T(8,128)(2,1)}, bf16[16,2432]{1,0:T(8,128)(2,1)S(1)}, u32[]{:S(2)}, u32[]{:S(2)}) collective-permute-start(bf16[16,2432]{1,0:T(8,128)(2,1)} %get-tuple-element.50), channel_id=1, source_target_pairs={{0,24},{8,16},{16,8},{24,0},{1,25},{9,17},{17,9},{25,1},{2,26},{10... | collective-permute-start | bytes 233480 | tf_op jit(solution)/shard_map/ppermute | solution.py:172
  7.6 5.4 %copy-start.1 = (bf16[16,2432]{1,0:T(8,128)(2,1)S(1)}, bf16[16,2432]{1,0:T(8,128)(2,1)}, u32[]{:S(2)}) copy-start(bf16[16,2432]{1,0:T(8,128)(2,1)} %get-tuple-element.51.refs_0_) | copy-start | bytes 233476
  13.0 4.5 %collective-permute-start.3 = (bf16[64,512]{1,0:T(8,128)(2,1)S(1)}, bf16[64,512]{1,0:T(8,128)(2,1)S(1)}, u32[]{:S(2)}, u32[]{:S(2)}) collective-permute-start(bf16[64,512]{1,0:T(8,128)(2,1)S(1)} %get-tuple-element.56), channel_id=1, source_target_pairs={{0,2},{2,0},{4,6},{6,4},{1,3},{3,1},{5,7},{7,5},{8,10},{10,8},{12,... | collective-permute-start | bytes 196616 | tf_op jit(solution)/shard_map/ppermute | solution.py:172
  14.7 6.6 %collective-permute-start.4 = (bf16[64,512]{1,0:T(8,128)(2,1)S(1)}, bf16[64,512]{1,0:T(8,128)(2,1)S(1)}, u32[]{:S(2)}, u32[]{:S(2)}) collective-permute-start(bf16[64,512]{1,0:T(8,128)(2,1)S(1)} %get-tuple-element.57), channel_id=1, source_target_pairs={{0,4},{2,6},{4,0},{6,2},{1,5},{3,7},{5,1},{7,3},{8,12},{10,14},{12... | collective-permute-start | bytes 196616 | tf_op jit(solution)/shard_map/ppermute | solution.py:172
  17.2 6.1 %collective-permute-start.5 = (bf16[64,512]{1,0:T(8,128)(2,1)S(1)}, bf16[64,512]{1,0:T(8,128)(2,1)S(1)}, u32[]{:S(2)}, u32[]{:S(2)}) collective-permute-start(bf16[64,512]{1,0:T(8,128)(2,1)S(1)} %get-tuple-element.58), channel_id=1, source_target_pairs={{0,6},{2,4},{4,2},{6,0},{1,7},{3,5},{5,3},{7,1},{8,14},{10,12},{12... | collective-permute-start | bytes 196616 | tf_op jit(solution)/shard_map/ppermute | solution.py:172
  17.5 5.9 %collective-permute-start.6 = (bf16[64,512]{1,0:T(8,128)(2,1)S(1)}, bf16[64,512]{1,0:T(8,128)(2,1)S(1)}, u32[]{:S(2)}, u32[]{:S(2)}) collective-permute-start(bf16[64,512]{1,0:T(8,128)(2,1)S(1)} %get-tuple-element.61.refs_0_), channel_id=1, source_target_pairs={{0,1},{1,0},{2,3},{3,2},{4,5},{5,4},{6,7},{7,6},{8,9},{9,8},{10,11... | collective-permute-start | bytes 196616 | tf_op jit(solution)/shard_map/ppermute | solution.py:172
  17.5 5.8 %collective-permute-start.7 = (bf16[64,512]{1,0:T(8,128)(2,1)S(1)}, bf16[64,512]{1,0:T(8,128)(2,1)S(1)}, u32[]{:S(2)}, u32[]{:S(2)}) collective-permute-start(bf16[64,512]{1,0:T(8,128)(2,1)S(1)} %collective-permute-done.3.refs_1_), channel_id=1, source_target_pairs={{0,1},{1,0},{2,3},{3,2},{4,5},{5,4},{6,7},{7,6},{8,9},{9,8},{10,11... | collective-permute-start | bytes 196616 | tf_op jit(solution)/shard_map/ppermute | solution.py:172
  21.2 2.1 %collective-permute-start.8 = (bf16[64,512]{1,0:T(8,128)(2,1)S(1)}, bf16[64,512]{1,0:T(8,128)(2,1)S(1)}, u32[]{:S(2)}, u32[]{:S(2)}) collective-permute-start(bf16[64,512]{1,0:T(8,128)(2,1)S(1)} %collective-permute-done.4.refs_2_), channel_id=1, source_target_pairs={{0,1},{1,0},{2,3},{3,2},{4,5},{5,4},{6,7},{7,6},{8,9},{9,8},{10,11... | collective-permute-start | bytes 196616 | tf_op jit(solution)/shard_map/ppermute | solution.py:172
  23.3 1.3 %collective-permute-start.9 = (bf16[64,512]{1,0:T(8,128)(2,1)S(1)}, bf16[64,512]{1,0:T(8,128)(2,1)S(1)}, u32[]{:S(2)}, u32[]{:S(2)}) collective-permute-start(bf16[64,512]{1,0:T(8,128)(2,1)S(1)} %collective-permute-done.5.refs_3_), channel_id=1, source_target_pairs={{0,1},{1,0},{2,3},{3,2},{4,5},{5,4},{6,7},{7,6},{8,9},{9,8},{10,11... | collective-permute-start | bytes 196616 | tf_op jit(solution)/shard_map/ppermute | solution.py:172
  25.8 6.1 %collective-permute-start.10 = (bf16[64,768]{1,0:T(8,128)(2,1)S(1)}, bf16[64,768]{1,0:T(8,128)(2,1)S(1)}, u32[]{:S(2)}, u32[]{:S(2)}) collective-permute-start(bf16[64,768]{1,0:T(8,128)(2,1)S(1)} %get-tuple-element.70), channel_id=1, source_target_pairs={{0,2},{2,0},{4,6},{6,4},{1,3},{3,1},{5,7},{7,5},{8,10},{10,8},{12,... | collective-permute-start | bytes 294920 | tf_op jit(solution)/shard_map/ppermute | solution.py:172
  25.9 10.9 %collective-permute-start.11 = (bf16[64,768]{1,0:T(8,128)(2,1)S(1)}, bf16[64,768]{1,0:T(8,128)(2,1)S(1)}, u32[]{:S(2)}, u32[]{:S(2)}) collective-permute-start(bf16[64,768]{1,0:T(8,128)(2,1)S(1)} %get-tuple-element.71), channel_id=1, source_target_pairs={{0,4},{2,6},{4,0},{6,2},{1,5},{3,7},{5,1},{7,3},{8,12},{10,14},{12... | collective-permute-start | bytes 294920 | tf_op jit(solution)/shard_map/ppermute | solution.py:172
  27.2 9.5 %collective-permute-start.12 = (bf16[64,768]{1,0:T(8,128)(2,1)S(1)}, bf16[64,768]{1,0:T(8,128)(2,1)S(1)}, u32[]{:S(2)}, u32[]{:S(2)}) collective-permute-start(bf16[64,768]{1,0:T(8,128)(2,1)S(1)} %get-tuple-element.72), channel_id=1, source_target_pairs={{0,6},{2,4},{4,2},{6,0},{1,7},{3,5},{5,3},{7,1},{8,14},{10,12},{12... | collective-permute-start | bytes 294920 | tf_op jit(solution)/shard_map/ppermute | solution.py:172
  36.8 7.6 %collective-permute-start.15 = (bf16[64,768]{1,0:T(8,128)(2,1)S(1)}, bf16[64,768]{1,0:T(8,128)(2,1)S(1)}, u32[]{:S(2)}, u32[]{:S(2)}) collective-permute-start(bf16[64,768]{1,0:T(8,128)(2,1)S(1)} %shard_map.60.refs_0_), channel_id=1, source_target_pairs={{0,6},{2,4},{4,2},{6,0},{1,7},{3,5},{5,3},{7,1},{8,14},{10,12},{12... | collective-permute-start | bytes 294920 | tf_op jit(solution)/shard_map/ppermute | solution.py:172
  38.4 9.8 %collective-permute-start.14 = (bf16[64,768]{1,0:T(8,128)(2,1)S(1)}, bf16[64,768]{1,0:T(8,128)(2,1)S(1)}, u32[]{:S(2)}, u32[]{:S(2)}) collective-permute-start(bf16[64,768]{1,0:T(8,128)(2,1)S(1)} %shard_map.60.refs_0_), channel_id=1, source_target_pairs={{0,4},{2,6},{4,0},{6,2},{1,5},{3,7},{5,1},{7,3},{8,12},{10,14},{12... | collective-permute-start | bytes 294920 | tf_op jit(solution)/shard_map/ppermute | solution.py:172
  40.2 8.0 %collective-permute-start.13 = (bf16[64,768]{1,0:T(8,128)(2,1)S(1)}, bf16[64,768]{1,0:T(8,128)(2,1)S(1)}, u32[]{:S(2)}, u32[]{:S(2)}) collective-permute-start(bf16[64,768]{1,0:T(8,128)(2,1)S(1)} %shard_map.60.refs_0_), channel_id=1, source_target_pairs={{0,2},{2,0},{4,6},{6,4},{1,3},{3,1},{5,7},{7,5},{8,10},{10,8},{12,... | collective-permute-start | bytes 294920 | tf_op jit(solution)/shard_map/ppermute | solution.py:172

commit v3 on v2

--- a/solution.py
+++ b/solution.py
@@ -11,7 +11,7 @@
 BF16 = jnp.bfloat16
 F32 = jnp.float32
 VMEM_BYTES = 40 * 1024 * 1024
-PACK_VMEM = 60 * 1024 * 1024
+PACK_VMEM = 53 * 1024 * 1024
 
 
 def call(kernel, out_shape, args, in_specs, out_specs=None, scratch=(), flops=0, nbytes=0, vmem_bytes=VMEM_BYTES):
@@ -44,6 +44,14 @@
     return lax.axis_index("att") if halves == 2 else 0
 
 
+def blk_partner(nb, halves, k):
+    return jnp.where(lax.axis_index("att") == 0, k, nb - k) if halves == 2 and k else k
+
+
+def group_partner(ng, k):
+    return ng - k if k else 0
+
+
 def pack_kernel(ng, nb, halves, tokens, routed, act, *refs):
     outs, (token_buf, routed_buf, act_buf, sem) = refs[:ng], refs[ng:]
     top, count = routed.shape
@@ -53,7 +61,8 @@
     copies = [pltpu.make_async_copy(routed, routed_buf, sem.at[0])]
     copies.append(pltpu.make_async_copy(act, act_buf, sem.at[1]))
     for p in range(nb):
-        start = pl.multiple_of(((block ^ p) * halves + half) * width, width)
+        partner = block ^ blk_partner(nb, halves, p)
+        start = pl.multiple_of((partner * halves + half) * width, width)
         copies.append(
             pltpu.make_async_copy(tokens.at[:, pl.ds(start, width)], token_buf.at[p], sem.at[2 + p])
         )
@@ -63,10 +72,11 @@
     spread = (iota((count, count * top), 1) // top == iota((count, count * top), 0)).astype(F32).astype(BF16)
     own_slot = iota((top, count * top), 1) % top == iota((top, count * top), 0)
     slot = (iota((rows, count), 0) % CAP + 1).astype(F32)
-    expert = (group ^ (iota((rows, 1), 0) // CAP)).astype(F32)
+    slots = iota((rows, 1), 0) // CAP
+    expert = (group ^ jnp.where(slots == 0, 0, ng - slots)).astype(F32)
     copies[0].wait()
     ids = routed_buf[...]
-    chosen = [jnp.sum((ids == (group ^ s)).astype(F32), axis=0, keepdims=True) for s in range(ng)]
+    chosen = [jnp.sum((ids == (group ^ group_partner(ng, s))).astype(F32), axis=0, keepdims=True) for s in range(ng)]
     chosen_rows = jnp.concatenate([jnp.broadcast_to(c, (CAP, count)) for c in chosen], axis=0)
     place = dot(chosen_rows.astype(BF16), upto)
     selector = jnp.where(place == slot, chosen_rows, 0.0).astype(BF16)
@@ -115,14 +125,13 @@
                 ).astype(BF16)
 
 
-def gate_up_kernel(nb, halves, *refs):
-    pieces, weights, outs = refs[: nb * halves], refs[nb * halves], refs[nb * halves + 1 :]
-    rows, width = pieces[0].shape
-    for p in range(nb):
-        total = dot(pieces[p][...], weights[:width])
-        for h in range(1, halves):
-            total += dot(pieces[h * nb + p][...], weights[h * width : (h + 1) * width])
-        outs[p][...] = total.astype(outs[p].dtype)
+def gate_up_kernel(halves, *refs):
+    pieces, weights, out = refs[:halves], refs[halves], refs[halves + 1]
+    width = pieces[0].shape[1]
+    total = dot(pieces[0][...], weights[:width])
+    for h in range(1, halves):
+        total += dot(pieces[h][...], weights[h * width : (h + 1) * width])
+    out[...] = total.astype(out.dtype)
 
 
 def features_kernel(nb, halves, *refs):
@@ -168,8 +177,23 @@
         copy.wait()
 
 
-def swap(x, axis, size, s):
-    return lax.ppermute(x, axis, [(i, i ^ s) for i in range(size)])
+def swap_group(x, size, k):
+    s = group_partner(size, k)
+    return lax.ppermute(x, "group", [(i, i ^ s) for i in range(size)])
+
+
+def swap_blk(x, size, halves, k):
+    if halves == 1:
+        return lax.ppermute(x, "blk", [(i, i ^ k) for i in range(size)])
+    return lax.ppermute(
+        x,
+        ("blk", "att"),
+        [(2 * i + c, 2 * (i ^ s) + c) for i in range(size) for c, s in ((0, k), (1, size - k))],
+    )
+
+
+def swap_att(x):
+    return lax.ppermute(x, "att", [(0, 1), (1, 0)])
 
 
 def local(tokens, routed_experts, act_cotangent, weight_codes, weight_scales):
@@ -202,7 +226,7 @@
         [SMEM, VMEM],
         nbytes=4 << 20,
     )
-    pieces = [sent[0]] + [swap(sent[s], "group", ng, s) for s in range(1, ng)]
+    pieces = [sent[0]] + [swap_group(sent[s], ng, s) for s in range(1, ng)]
     weights, *pieces = lax.optimization_barrier((weights, *pieces))
     *columns, cot = call(
         functools.partial(regroup_kernel, ng, nb, width),
@@ -211,26 +235,29 @@
         [VMEM] * ng,
         nbytes=1 << 20,
     )
-    x = [columns[0]] + [swap(columns[p], "blk", nb, p) for p in range(1, nb)]
+    x = [columns[0]] + [swap_blk(columns[p], nb, halves, p) for p in range(1, nb)]
     if halves == 2:
-        x += [swap(piece, "att", 2, 1) for piece in x]
-    *partial, = call(
-        functools.partial(gate_up_kernel, nb, halves),
-        [sds((rows, 2 * hidden), F32)] + [sds((rows, 2 * hidden), BF16)] * (nb - 1),
-        (*x, weights),
-        [VMEM] * (nb * halves + 1),
-        flops=2 * nb * rows * depth * 2 * hidden,
-        nbytes=3 << 20,
-    )
-    *x, partial[1] = lax.optimization_barrier((*x, partial[1]))
+        other = [swap_att(piece) for piece in x]
+        x += [other[0], *other[:0:-1]]
+    partial = [
+        call(
+            functools.partial(gate_up_kernel, halves),
+            sds((rows, 2 * hidden), BF16 if p else F32),
+            (*x[p::nb], weights),
+            [VMEM] * (halves + 1),
+            flops=2 * rows * depth * 2 * hidden,
+            nbytes=1 << 20,
+        )
+        for p in range(nb)
+    ]
+    parts = [partial[0]] + [swap_blk(partial[p], nb, halves, p) for p in range(1, nb)]
     features = call(
         functools.partial(features_kernel, nb, halves),
         sds((nb * rows, depth), BF16),
-        x,
+        [piece for h in range(halves) for piece in (x[h * nb], *x[(h + 1) * nb - 1 : h * nb : -1])],
         [VMEM] * (nb * halves),
         nbytes=3 << 20,
     )
-    parts = [partial[0]] + [swap(partial[p], "blk", nb, p) for p in range(1, nb)]
     features, *parts = lax.optimization_barrier((features, *parts))
     own = call(
         functools.partial(swiglu_kernel, nb),
@@ -239,7 +266,7 @@
         [VMEM] * (nb + 1),
         nbytes=1 << 20,
     )
-    gathered = [own] + [swap(own, "blk", nb, p) for p in range(1, nb)]
+    gathered = [own] + [swap_blk(own, nb, halves, p) for p in range(nb - 1, 0, -1)]
     step = min(128, depth)
     gradient = call(
         functools.partial(gradient_kernel, nb),

time: 50.7 us -> 46.9 us (0.925)
  waiting for transfers between devices: 23.9 us -> 20.1 us
  local copies, waits for them, and re-layouts: 0.11 us -> 0.91 us
    ppermute x16, waiting for transfers between devices: 23.9 us -> 20.1 us  [the longest x9 16.2 us: swap_blk(): lax.ppermute(x, ('blk', 'att'), [(2 * i + c, 2 * (i ^ s) + c) for i in ra...]
    unnamed x6, local copies, waits for them, and re-layouts: 0.01 us -> 0.81 us
    pallas_call x7 -> x10, Pallas kernels: 8.14 us -> 7.65 us  [call(): pl.pallas_call(kernel, out_shape=out_shape, in_specs=in_specs, out_specs=...]
  transfers between devices with their start and end apart: 16 -> 16, of which waited for: 9 -> 11; matrix products, arithmetic and copies ran while one was open for 0% -> 0% of each run, Pallas kernels for 3% -> 7%
where the time goes in v3:
time: 46.9 us; the launch traced here: 46.8 us
  waiting for transfers between devices  20.1 us (43%)
  starting transfers between devices  18 us (38%)
  Pallas kernels  7.65 us (16%)
  local copies, waits for them, and re-layouts  0.91 us (2%)
    ppermute x9, waiting for transfers between devices, swap_blk(): lax.ppermute(x, ('blk', 'att'), [(2 * i + c, 2 * (i ^ s) + c) for i in ra...  16.2 us
    ppermute x9, starting transfers between devices, swap_blk(): lax.ppermute(x, ('blk', 'att'), [(2 * i + c, 2 * (i ^ s) + c) for i in ra...  13.3 us
    pallas_call x10, Pallas kernels, call(): pl.pallas_call(kernel, out_shape=out_shape, in_specs=in_specs, out_specs=...  7.65 us
    ppermute x3, starting transfers between devices, swap_group(): return lax.ppermute(x, 'group', [(i, i ^ s) for i in range(size)])  4.6 us
    ppermute x3, waiting for transfers between devices, swap_group(): return lax.ppermute(x, 'group', [(i, i ^ s) for i in range(size)])  2.67 us
    ppermute x4, waiting for transfers between devices, swap_att(): return lax.ppermute(x, 'att', [(0, 1), (1, 0)])  1.26 us
  transfers between devices with their start and end apart: 16, of which 11 were waited for; matrix products, arithmetic and copies ran while one was open for 0% of the time, Pallas kernels for 7%

profile of v3, /device:TPU:0, one launch (start us, length us, event | category | flops | bytes accessed | tf_op | source)
XLA Modules:
  0.0 46.8 jit_solution(7118809813997067632)
XLA Ops:
  0.0 0.0 copy-start
  0.0 0.0 copy-start.1
  0.0 0.8 %copy-done.1 = s32[128,8]{0,1:T(8,128)S(1)} copy-done((s32[128,8]{0,1:T(8,128)S(1)}, s32[128,8]{0,1:T(8,128)}, u32[]{:S(2)}) %copy-start.1) | copy-done | bytes 4120
  0.8 0.0 copy-start.2
  0.8 2.1 %shard_map.55 = (bf16[16,2432]{1,0:T(8,128)(2,1)S(1)}, bf16[16,2432]{1,0:T(8,128)(2,1)S(1)}, bf16[16,2432]{1,0:T(8,128)(2,1)S(1)}, bf16[16,2432]{1,0:T(8,128)(2,1)S(1)}) custom-call(bf16[128,4096]{1,0:T(8,128)(2,1)} %tokens.1, s32[8,128]{1,0:T(8,128)S(1)} %bitcast.9, bf16[128,8,384]{2,1,0:T(8,128)(2,1)} %act.1), custom_call_target="tpu_custom_call" | custom-call | bytes 2097152 | tf_op jit(solution)/shard_map/pallas_call | solution.py:19
  2.9 4.0 %collective-permute-start = (bf16[16,2432]{1,0:T(8,128)(2,1)S(1)}, bf16[16,2432]{1,0:T(8,128)(2,1)S(1)}, u32[]{:S(2)}, u32[]{:S(2)}) collective-permute-start(bf16[16,2432]{1,0:T(8,128)(2,1)S(1)} %get-tuple-element.35), channel_id=1, source_target_pairs={{0,24},{8,16},{16,8},{24,0},{1,25},{9,17},{17,9},{25,1},{2,26},{10... | collective-permute-start | bytes 233480 | tf_op jit(solution)/shard_map/ppermute | solution.py:182
  6.9 0.5 %collective-permute-start.1 = (bf16[16,2432]{1,0:T(8,128)(2,1)S(1)}, bf16[16,2432]{1,0:T(8,128)(2,1)S(1)}, u32[]{:S(2)}, u32[]{:S(2)}) collective-permute-start(bf16[16,2432]{1,0:T(8,128)(2,1)S(1)} %get-tuple-element.36), channel_id=1, source_target_pairs={{0,16},{8,24},{16,0},{24,8},{1,17},{9,25},{17,1},{25,9},{2,18},{10... | collective-permute-start | bytes 233480 | tf_op jit(solution)/shard_map/ppermute | solution.py:182
  7.4 0.1 collective-permute-start.2
  7.5 0.0 copy-done.2
  7.5 0.1 copy.6.scales
  7.6 0.0 copy-done
  7.6 1.5 %shard_map.56.refs_2_ = bf16[1024,768]{1,0:T(8,128)(2,1)S(1)} custom-call(f32[8,2,3]{2,1,0:T(2,128)S(1)} %copy.6.scales, bf16[1024,2,384]{2,1,0:T(2,128)(2,1)S(1)} %bitcast.8), custom_call_target="tpu_custom_call" | custom-call | bytes 4194304 | tf_op jit(solution)/shard_map/pallas_call | solution.py:19
  9.1 0.2 collective-permute-done.refs_1_
  9.3 1.9 %collective-permute-done.1.refs_2_ = bf16[16,2432]{1,0:T(8,128)(2,1)S(1)} collective-permute-done((bf16[16,2432]{1,0:T(8,128)(2,1)S(1)}, bf16[16,2432]{1,0:T(8,128)(2,1)S(1)}, u32[]{:S(2)}, u32[]{:S(2)}) %collective-permute-start.1) | collective-permute-done | bytes 77856 | tf_op jit(solution)/shard_map/ppermute | solution.py:182
  11.3 0.5 %collective-permute-done.2.refs_3_ = bf16[16,2432]{1,0:T(8,128)(2,1)S(1)} collective-permute-done((bf16[16,2432]{1,0:T(8,128)(2,1)S(1)}, bf16[16,2432]{1,0:T(8,128)(2,1)S(1)}, u32[]{:S(2)}, u32[]{:S(2)}) %collective-permute-start.2) | collective-permute-done | bytes 77856 | tf_op jit(solution)/shard_map/ppermute | solution.py:182
  11.8 2.7 %collective-permute-start.4 = (bf16[64,512]{1,0:T(8,128)(2,1)S(1)}, bf16[64,512]{1,0:T(8,128)(2,1)S(1)}, u32[]{:S(2)}, u32[]{:S(2)}) collective-permute-start(bf16[64,512]{1,0:T(8,128)(2,1)S(1)} %get-tuple-element.44), channel_id=1, source_target_pairs={{0,4},{1,5},{2,6},{3,7},{4,0},{5,1},{6,2},{7,3},{8,12},{9,13},{10,... | collective-permute-start | bytes 196616 | tf_op jit(solution)/shard_map/ppermute | solution.py:188
  14.5 1.3 %collective-permute-start.3 = (bf16[64,512]{1,0:T(8,128)(2,1)S(1)}, bf16[64,512]{1,0:T(8,128)(2,1)S(1)}, u32[]{:S(2)}, u32[]{:S(2)}) collective-permute-start(bf16[64,512]{1,0:T(8,128)(2,1)S(1)} %get-tuple-element.43), channel_id=1, source_target_pairs={{0,6},{1,3},{2,4},{3,1},{4,2},{5,7},{6,0},{7,5},{8,14},{9,11},{10,... | collective-permute-start | bytes 196616 | tf_op jit(solution)/shard_map/ppermute | solution.py:188
  15.8 0.2 collective-permute-start.5
  16.1 1.2 %collective-permute-done.4.refs_2_.refs_0_ = bf16[64,512]{1,0:T(8,128)(2,1)S(1)} collective-permute-done((bf16[64,512]{1,0:T(8,128)(2,1)S(1)}, bf16[64,512]{1,0:T(8,128)(2,1)S(1)}, u32[]{:S(2)}, u32[]{:S(2)}) %collective-permute-start.4) | collective-permute-done | bytes 65568 | tf_op jit(solution)/shard_map/ppermute | solution.py:188
  17.2 0.0 collective-permute-start.8
  17.2 3.4 %collective-permute-done.3.refs_1_.refs_0_ = bf16[64,512]{1,0:T(8,128)(2,1)S(1)} collective-permute-done((bf16[64,512]{1,0:T(8,128)(2,1)S(1)}, bf16[64,512]{1,0:T(8,128)(2,1)S(1)}, u32[]{:S(2)}, u32[]{:S(2)}) %collective-permute-start.3) | collective-permute-done | bytes 65568 | tf_op jit(solution)/shard_map/ppermute | solution.py:188
  20.6 0.0 collective-permute-start.9
  20.6 0.3 collective-permute-done.5.refs_3_.refs_0_
  21.0 0.2 collective-permute-start.7
  21.1 0.0 collective-permute-done.8.refs_6_.refs_1_
  21.1 0.4 shard_map.61
  21.5 2.0 %collective-permute-start.11 = (bf16[64,768]{1,0:T(8,128)(2,1)S(1)}, bf16[64,768]{1,0:T(8,128)(2,1)S(1)}, u32[]{:S(2)}, u32[]{:S(2)}) collective-permute-start(bf16[64,768]{1,0:T(8,128)(2,1)S(1)} %shard_map.61), channel_id=1, source_target_pairs={{0,4},{1,5},{2,6},{3,7},{4,0},{5,1},{6,2},{7,3},{8,12},{9,13},{10,... | collective-permute-start | bytes 294920 | tf_op jit(solution)/shard_map/ppermute | solution.py:188
  23.5 0.0 collective-permute-done.9.refs_7_.refs_1_
  23.5 0.4 shard_map.60
  23.9 1.7 %collective-permute-start.10 = (bf16[64,768]{1,0:T(8,128)(2,1)S(1)}, bf16[64,768]{1,0:T(8,128)(2,1)S(1)}, u32[]{:S(2)}, u32[]{:S(2)}) collective-permute-start(bf16[64,768]{1,0:T(8,128)(2,1)S(1)} %shard_map.60), channel_id=1, source_target_pairs={{0,2},{1,7},{2,0},{3,5},{4,6},{5,3},{6,4},{7,1},{8,10},{9,15},{10,... | collective-permute-start | bytes 294920 | tf_op jit(solution)/shard_map/ppermute | solution.py:188
  25.6 0.0 collective-permute-done.7.refs_5_.refs_1_
  25.6 0.4 shard_map.62
  26.0 0.9 %collective-permute-start.12 = (bf16[64,768]{1,0:T(8,128)(2,1)S(1)}, bf16[64,768]{1,0:T(8,128)(2,1)S(1)}, u32[]{:S(2)}, u32[]{:S(2)}) collective-permute-start(bf16[64,768]{1,0:T(8,128)(2,1)S(1)} %shard_map.62), channel_id=1, source_target_pairs={{0,6},{1,3},{2,4},{3,1},{4,2},{5,7},{6,0},{7,5},{8,14},{9,11},{10,... | collective-permute-start | bytes 294920 | tf_op jit(solution)/shard_map/ppermute | solution.py:188
  26.9 0.0 collective-permute-start.6
  26.9 1.3 %collective-permute-done.6.refs_4_.refs_1_ = bf16[64,512]{1,0:T(8,128)(2,1)S(1)} collective-permute-done((bf16[64,512]{1,0:T(8,128)(2,1)S(1)}, bf16[64,512]{1,0:T(8,128)(2,1)S(1)}, u32[]{:S(2)}, u32[]{:S(2)}) %collective-permute-start.6) | collective-permute-done | bytes 65568 | tf_op jit(solution)/shard_map/ppermute | solution.py:196
  28.2 0.4 shard_map.59.refs_0_
  28.5 0.1 shard_map.58.refs_4_
  28.6 2.4 %collective-permute-done.11.refs_2_ = bf16[64,768]{1,0:T(8,128)(2,1)S(1)} collective-permute-done((bf16[64,768]{1,0:T(8,128)(2,1)S(1)}, bf16[64,768]{1,0:T(8,128)(2,1)S(1)}, u32[]{:S(2)}, u32[]{:S(2)}) %collective-permute-start.11) | collective-permute-done | bytes 98336 | tf_op jit(solution)/shard_map/ppermute | solution.py:188
  31.0 2.4 %collective-permute-done.10.refs_1_ = bf16[64,768]{1,0:T(8,128)(2,1)S(1)} collective-permute-done((bf16[64,768]{1,0:T(8,128)(2,1)S(1)}, bf16[64,768]{1,0:T(8,128)(2,1)S(1)}, u32[]{:S(2)}, u32[]{:S(2)}) %collective-permute-start.10) | collective-permute-done | bytes 98336 | tf_op jit(solution)/shard_map/ppermute | solution.py:188
  33.4 0.0 collective-permute-done.12.refs_3_
  33.4 0.1 shard_map.63.refs_0_
  33.4 1.2 %collective-permute-start.15 = (bf16[64,768]{1,0:T(8,128)(2,1)S(1)}, bf16[64,768]{1,0:T(8,128)(2,1)S(1)}, u32[]{:S(2)}, u32[]{:S(2)}) collective-permute-start(bf16[64,768]{1,0:T(8,128)(2,1)S(1)} %shard_map.63.refs_0_), channel_id=1, source_target_pairs={{0,2},{1,7},{2,0},{3,5},{4,6},{5,3},{6,4},{7,1},{8,10},{9,15},{10,... | collective-permute-start | bytes 294920 | tf_op jit(solution)/shard_map/ppermute | solution.py:188
  34.6 1.1 %collective-permute-start.14 = (bf16[64,768]{1,0:T(8,128)(2,1)S(1)}, bf16[64,768]{1,0:T(8,128)(2,1)S(1)}, u32[]{:S(2)}, u32[]{:S(2)}) collective-permute-start(bf16[64,768]{1,0:T(8,128)(2,1)S(1)} %shard_map.63.refs_0_), channel_id=1, source_target_pairs={{0,4},{1,5},{2,6},{3,7},{4,0},{5,1},{6,2},{7,3},{8,12},{9,13},{10,... | collective-permute-start | bytes 294920 | tf_op jit(solution)/shard_map/ppermute | solution.py:188
  35.7 2.2 %collective-permute-start.13 = (bf16[64,768]{1,0:T(8,128)(2,1)S(1)}, bf16[64,768]{1,0:T(8,128)(2,1)S(1)}, u32[]{:S(2)}, u32[]{:S(2)}) collective-permute-start(bf16[64,768]{1,0:T(8,128)(2,1)S(1)} %shard_map.63.refs_0_), channel_id=1, source_target_pairs={{0,6},{1,3},{2,4},{3,1},{4,2},{5,7},{6,0},{7,5},{8,14},{9,11},{10,... | collective-permute-start | bytes 294920 | tf_op jit(solution)/shard_map/ppermute | solution.py:188
  37.9 0.2 collective-permute-done.15.refs_3_
  38.1 6.3 %collective-permute-done.14.refs_2_ = bf16[64,768]{1,0:T(8,128)(2,1)S(1)} collective-permute-done((bf16[64,768]{1,0:T(8,128)(2,1)S(1)}, bf16[64,768]{1,0:T(8,128)(2,1)S(1)}, u32[]{:S(2)}, u32[]{:S(2)}) %collective-permute-start.14) | collective-permute-done | bytes 98336 | tf_op jit(solution)/shard_map/ppermute | solution.py:188
  44.4 0.0 collective-permute-done.13.refs_1_
  44.4 2.4 %shard_map.64 = bf16[1024,2,384]{2,1,0:T(2,128)(2,1)} custom-call(bf16[64,768]{1,0:T(8,128)(2,1)S(1)} %shard_map.63.refs_0_, bf16[64,768]{1,0:T(8,128)(2,1)S(1)} %collective-permute-done.13.refs_1_, bf16[64,768]{1,0:T(8,128)(2,1)S(1)} %collective-permute-done.14.refs_2_, bf16[64,768]{1,0:T(8,128)(2,1)S(1)} %collective-permute-done.15.refs_3_, ...), custom_call_target="tpu_custom_call" | custom-call | flops 402653184 | bytes 4194304 | tf_op jit(solution)/shard_map/pallas_call | solution.py:19
  (2 shorter events, 0.0 us)
Async XLA Ops:
  0.0 7.6 %copy-start = (bf16[1024,1,2,384]{3,2,1,0:T(2,128)(2,1)S(1)}, bf16[1024,1,2,384]{3,2,1,0:T(2,128)(2,1)}, u32[]{:S(2)}) copy-start(bf16[1024,1,2,384]{3,2,1,0:T(2,128)(2,1)} %param.8) | copy-start | bytes 4718596
  0.0 0.8 %copy-start.1 = (s32[128,8]{0,1:T(8,128)S(1)}, s32[128,8]{0,1:T(8,128)}, u32[]{:S(2)}) copy-start(s32[128,8]{0,1:T(8,128)} %param.6) | copy-start | bytes 12292
  0.8 6.7 %copy-start.2 = (bf16[8,1,2,3]{0,2,3,1:T(2,128)(2,1)S(1)}, bf16[8,1,2,3]{0,2,3,1:T(2,128)(2,1)}, u32[]{:S(2)}) copy-start(bf16[8,1,2,3]{0,2,3,1:T(2,128)(2,1)} %param.9) | copy-start | bytes 292
  2.9 6.4 %collective-permute-start = (bf16[16,2432]{1,0:T(8,128)(2,1)S(1)}, bf16[16,2432]{1,0:T(8,128)(2,1)S(1)}, u32[]{:S(2)}, u32[]{:S(2)}) collective-permute-start(bf16[16,2432]{1,0:T(8,128)(2,1)S(1)} %get-tuple-element.35), channel_id=1, source_target_pairs={{0,24},{8,16},{16,8},{24,0},{1,25},{9,17},{17,9},{25,1},{2,26},{10... | collective-permute-start | bytes 233480 | tf_op jit(solution)/shard_map/ppermute | solution.py:182
  6.9 4.4 %collective-permute-start.1 = (bf16[16,2432]{1,0:T(8,128)(2,1)S(1)}, bf16[16,2432]{1,0:T(8,128)(2,1)S(1)}, u32[]{:S(2)}, u32[]{:S(2)}) collective-permute-start(bf16[16,2432]{1,0:T(8,128)(2,1)S(1)} %get-tuple-element.36), channel_id=1, source_target_pairs={{0,16},{8,24},{16,0},{24,8},{1,17},{9,25},{17,1},{25,9},{2,18},{10... | collective-permute-start | bytes 233480 | tf_op jit(solution)/shard_map/ppermute | solution.py:182
  7.4 4.4 %collective-permute-start.2 = (bf16[16,2432]{1,0:T(8,128)(2,1)S(1)}, bf16[16,2432]{1,0:T(8,128)(2,1)S(1)}, u32[]{:S(2)}, u32[]{:S(2)}) collective-permute-start(bf16[16,2432]{1,0:T(8,128)(2,1)S(1)} %get-tuple-element.37), channel_id=1, source_target_pairs={{0,8},{8,0},{16,24},{24,16},{1,9},{9,1},{17,25},{25,17},{2,10},{10... | collective-permute-start | bytes 233480 | tf_op jit(solution)/shard_map/ppermute | solution.py:182
  11.8 5.4 %collective-permute-start.4 = (bf16[64,512]{1,0:T(8,128)(2,1)S(1)}, bf16[64,512]{1,0:T(8,128)(2,1)S(1)}, u32[]{:S(2)}, u32[]{:S(2)}) collective-permute-start(bf16[64,512]{1,0:T(8,128)(2,1)S(1)} %get-tuple-element.44), channel_id=1, source_target_pairs={{0,4},{1,5},{2,6},{3,7},{4,0},{5,1},{6,2},{7,3},{8,12},{9,13},{10,... | collective-permute-start | bytes 196616 | tf_op jit(solution)/shard_map/ppermute | solution.py:188
  14.5 6.1 %collective-permute-start.3 = (bf16[64,512]{1,0:T(8,128)(2,1)S(1)}, bf16[64,512]{1,0:T(8,128)(2,1)S(1)}, u32[]{:S(2)}, u32[]{:S(2)}) collective-permute-start(bf16[64,512]{1,0:T(8,128)(2,1)S(1)} %get-tuple-element.43), channel_id=1, source_target_pairs={{0,6},{1,3},{2,4},{3,1},{4,2},{5,7},{6,0},{7,5},{8,14},{9,11},{10,... | collective-permute-start | bytes 196616 | tf_op jit(solution)/shard_map/ppermute | solution.py:188
  15.8 5.1 %collective-permute-start.5 = (bf16[64,512]{1,0:T(8,128)(2,1)S(1)}, bf16[64,512]{1,0:T(8,128)(2,1)S(1)}, u32[]{:S(2)}, u32[]{:S(2)}) collective-permute-start(bf16[64,512]{1,0:T(8,128)(2,1)S(1)} %get-tuple-element.45), channel_id=1, source_target_pairs={{0,2},{1,7},{2,0},{3,5},{4,6},{5,3},{6,4},{7,1},{8,10},{9,15},{10,... | collective-permute-start | bytes 196616 | tf_op jit(solution)/shard_map/ppermute | solution.py:188
  17.2 3.9 %collective-permute-start.8 = (bf16[64,512]{1,0:T(8,128)(2,1)S(1)}, bf16[64,512]{1,0:T(8,128)(2,1)S(1)}, u32[]{:S(2)}, u32[]{:S(2)}) collective-permute-start(bf16[64,512]{1,0:T(8,128)(2,1)S(1)} %collective-permute-done.4.refs_2_.refs_0_), channel_id=1, source_target_pairs={{0,1},{1,0},{2,3},{3,2},{4,5},{5,4},{6,7},{7,6},{8,9},{9,8},{10,11... | collective-permute-start | bytes 196616 | tf_op jit(solution)/shard_map/ppermute | solution.py:196
  20.6 2.9 %collective-permute-start.9 = (bf16[64,512]{1,0:T(8,128)(2,1)S(1)}, bf16[64,512]{1,0:T(8,128)(2,1)S(1)}, u32[]{:S(2)}, u32[]{:S(2)}) collective-permute-start(bf16[64,512]{1,0:T(8,128)(2,1)S(1)} %collective-permute-done.3.refs_1_.refs_0_), channel_id=1, source_target_pairs={{0,1},{1,0},{2,3},{3,2},{4,5},{5,4},{6,7},{7,6},{8,9},{9,8},{10,11... | collective-permute-start | bytes 196616 | tf_op jit(solution)/shard_map/ppermute | solution.py:196
  21.0 4.6 %collective-permute-start.7 = (bf16[64,512]{1,0:T(8,128)(2,1)S(1)}, bf16[64,512]{1,0:T(8,128)(2,1)S(1)}, u32[]{:S(2)}, u32[]{:S(2)}) collective-permute-start(bf16[64,512]{1,0:T(8,128)(2,1)S(1)} %collective-permute-done.5.refs_3_.refs_0_), channel_id=1, source_target_pairs={{0,1},{1,0},{2,3},{3,2},{4,5},{5,4},{6,7},{7,6},{8,9},{9,8},{10,11... | collective-permute-start | bytes 196616 | tf_op jit(solution)/shard_map/ppermute | solution.py:196
  21.5 9.4 %collective-permute-start.11 = (bf16[64,768]{1,0:T(8,128)(2,1)S(1)}, bf16[64,768]{1,0:T(8,128)(2,1)S(1)}, u32[]{:S(2)}, u32[]{:S(2)}) collective-permute-start(bf16[64,768]{1,0:T(8,128)(2,1)S(1)} %shard_map.61), channel_id=1, source_target_pairs={{0,4},{1,5},{2,6},{3,7},{4,0},{5,1},{6,2},{7,3},{8,12},{9,13},{10,... | collective-permute-start | bytes 294920 | tf_op jit(solution)/shard_map/ppermute | solution.py:188
  23.9 9.4 %collective-permute-start.10 = (bf16[64,768]{1,0:T(8,128)(2,1)S(1)}, bf16[64,768]{1,0:T(8,128)(2,1)S(1)}, u32[]{:S(2)}, u32[]{:S(2)}) collective-permute-start(bf16[64,768]{1,0:T(8,128)(2,1)S(1)} %shard_map.60), channel_id=1, source_target_pairs={{0,2},{1,7},{2,0},{3,5},{4,6},{5,3},{6,4},{7,1},{8,10},{9,15},{10,... | collective-permute-start | bytes 294920 | tf_op jit(solution)/shard_map/ppermute | solution.py:188
  26.0 7.4 %collective-permute-start.12 = (bf16[64,768]{1,0:T(8,128)(2,1)S(1)}, bf16[64,768]{1,0:T(8,128)(2,1)S(1)}, u32[]{:S(2)}, u32[]{:S(2)}) collective-permute-start(bf16[64,768]{1,0:T(8,128)(2,1)S(1)} %shard_map.62), channel_id=1, source_target_pairs={{0,6},{1,3},{2,4},{3,1},{4,2},{5,7},{6,0},{7,5},{8,14},{9,11},{10,... | collective-permute-start | bytes 294920 | tf_op jit(solution)/shard_map/ppermute | solution.py:188
  26.9 1.3 %collective-permute-start.6 = (bf16[64,512]{1,0:T(8,128)(2,1)S(1)}, bf16[64,512]{1,0:T(8,128)(2,1)S(1)}, u32[]{:S(2)}, u32[]{:S(2)}) collective-permute-start(bf16[64,512]{1,0:T(8,128)(2,1)S(1)} %get-tuple-element.42.refs_0_), channel_id=1, source_target_pairs={{0,1},{1,0},{2,3},{3,2},{4,5},{5,4},{6,7},{7,6},{8,9},{9,8},{10,11... | collective-permute-start | bytes 196616 | tf_op jit(solution)/shard_map/ppermute | solution.py:196
  33.4 4.7 %collective-permute-start.15 = (bf16[64,768]{1,0:T(8,128)(2,1)S(1)}, bf16[64,768]{1,0:T(8,128)(2,1)S(1)}, u32[]{:S(2)}, u32[]{:S(2)}) collective-permute-start(bf16[64,768]{1,0:T(8,128)(2,1)S(1)} %shard_map.63.refs_0_), channel_id=1, source_target_pairs={{0,2},{1,7},{2,0},{3,5},{4,6},{5,3},{6,4},{7,1},{8,10},{9,15},{10,... | collective-permute-start | bytes 294920 | tf_op jit(solution)/shard_map/ppermute | solution.py:188
  34.6 9.8 %collective-permute-start.14 = (bf16[64,768]{1,0:T(8,128)(2,1)S(1)}, bf16[64,768]{1,0:T(8,128)(2,1)S(1)}, u32[]{:S(2)}, u32[]{:S(2)}) collective-permute-start(bf16[64,768]{1,0:T(8,128)(2,1)S(1)} %shard_map.63.refs_0_), channel_id=1, source_target_pairs={{0,4},{1,5},{2,6},{3,7},{4,0},{5,1},{6,2},{7,3},{8,12},{9,13},{10,... | collective-permute-start | bytes 294920 | tf_op jit(solution)/shard_map/ppermute | solution.py:188
  35.7 8.7 %collective-permute-start.13 = (bf16[64,768]{1,0:T(8,128)(2,1)S(1)}, bf16[64,768]{1,0:T(8,128)(2,1)S(1)}, u32[]{:S(2)}, u32[]{:S(2)}) collective-permute-start(bf16[64,768]{1,0:T(8,128)(2,1)S(1)} %shard_map.63.refs_0_), channel_id=1, source_target_pairs={{0,6},{1,3},{2,4},{3,1},{4,2},{5,7},{6,0},{7,5},{8,14},{9,11},{10,... | collective-permute-start | bytes 294920 | tf_op jit(solution)/shard_map/ppermute | solution.py:188

commit v4 on v3

v4 whole, which is shorter than its diff:
```python
import functools

import jax
import jax.numpy as jnp
from jax import lax
from jax.experimental import pallas as pl
from jax.experimental.pallas import tpu as pltpu
from jax.sharding import PartitionSpec as P

CAP = 16
BF16 = jnp.bfloat16
F32 = jnp.float32
VMEM_BYTES = 40 * 1024 * 1024
PAIRED_CUTS = (1, 2)
PACK_VMEM = 53 * 1024 * 1024


def call(kernel, out_shape, args, in_specs, out_specs=None, scratch=(), flops=0, nbytes=0, vmem_bytes=VMEM_BYTES, aliases=None):
    vmem = pl.BlockSpec(memory_space=pltpu.VMEM)
    return pl.pallas_call(
        kernel,
        out_shape=out_shape,
        in_specs=in_specs,
        out_specs=jax.tree.map(lambda _: vmem, out_shape) if out_specs is None else out_specs,
        scratch_shapes=scratch,
        input_output_aliases=aliases or {},
        compiler_params=pltpu.CompilerParams(vmem_limit_bytes=vmem_bytes),
        cost_estimate=pl.CostEstimate(flops=flops, bytes_accessed=nbytes, transcendentals=0),
    )(*args)


VMEM = pl.BlockSpec(memory_space=pltpu.VMEM)
SMEM = pl.BlockSpec(memory_space=pltpu.SMEM)
HBM = pl.BlockSpec(memory_space=pltpu.HBM)


def dot(a, b, dims=((1,), (0,))):
    return lax.dot_general(a, b, (dims, ((), ())), preferred_element_type=F32)


def iota(shape, dim):
    return lax.broadcasted_iota(jnp.int32, shape, dim)


def own_half(halves):
    return lax.axis_index("att") if halves == 2 else 0


def group_partner(ng, k):
    return ng - k if k else 0


def pack_kernel(ng, nb, halves, tokens, routed, act, *refs):
    outs, (token_buf, routed_buf, act_buf, sem) = refs[:ng], refs[ng:]
    top, count = routed.shape
    rows = ng * CAP
    width = tokens.shape[1] // (nb * halves)
    group, block, half = lax.axis_index("group"), lax.axis_index("blk"), own_half(halves)
    copies = [pltpu.make_async_copy(routed, routed_buf, sem.at[0])]
    copies.append(pltpu.make_async_copy(act, act_buf, sem.at[1]))
    for p in range(nb):
        partner = block ^ p
        start = pl.multiple_of((partner * halves + half) * width, width)
        copies.append(
            pltpu.make_async_copy(tokens.at[:, pl.ds(start, width)], token_buf.at[p], sem.at[2 + p])
        )
    for copy in copies:
        copy.start()
    upto = (iota((count, count), 0) <= iota((count, count), 1)).astype(F32).astype(BF16)
    spread = (iota((count, count * top), 1) // top == iota((count, count * top), 0)).astype(F32).astype(BF16)
    own_slot = iota((top, count * top), 1) % top == iota((top, count * top), 0)
    slot = (iota((rows, count), 0) % CAP + 1).astype(F32)
    slots = iota((rows, 1), 0) // CAP
    expert = (group ^ jnp.where(slots == 0, 0, ng - slots)).astype(F32)
    copies[0].wait()
    ids = routed_buf[...]
    chosen = [jnp.sum((ids == (group ^ group_partner(ng, s))).astype(F32), axis=0, keepdims=True) for s in range(ng)]
    chosen_rows = jnp.concatenate([jnp.broadcast_to(c, (CAP, count)) for c in chosen], axis=0)
    place = dot(chosen_rows.astype(BF16), upto)
    selector = jnp.where(place == slot, chosen_rows, 0.0).astype(BF16)
    ids_wide = dot(ids.astype(F32).astype(BF16), spread)
    ids_flat = jnp.sum(jnp.where(own_slot, ids_wide, 0.0), axis=0, keepdims=True)
    pair = jnp.where(ids_flat == expert, dot(selector, spread), 0.0).astype(BF16)
    copies[1].wait()
    hidden = act.shape[2]
    cot = dot(pair, act_buf[...].reshape(count * top, hidden)).astype(BF16)
    for s in range(ng):
        outs[s][:, nb * width :] = cot[s * CAP : (s + 1) * CAP]
    for p in range(nb):
        copies[2 + p].wait()
        part = dot(selector, token_buf[p]).astype(BF16)
        for s in range(ng):
            outs[s][:, p * width : (p + 1) * width] = part[s * CAP : (s + 1) * CAP]


def regroup_kernel(ng, nb, width, with_cot, *refs):
    pieces, outs = refs[:ng], refs[ng:]
    for s in range(ng):
        at = slice(s * CAP, (s + 1) * CAP)
        cot = pieces[s][:, nb * width :]
        for p in range(nb):
            outs[p][at, :width] = pieces[s][:, p * width : (p + 1) * width]
            if p in with_cot:
                outs[p][at, width:] = cot
        outs[nb][at, :] = cot


def weights_kernel(halves, scales, codes, out):
    depth, _, hidden = codes.shape
    blocks, _, cols = scales.shape
    qrows, qcols = depth // blocks, hidden // cols
    half = own_half(halves)
    per_half = blocks // halves
    pick = [
        (iota((qrows, 2 * qrows), 1) == 2 * iota((qrows, 2 * qrows), 0) + j).astype(F32).astype(BF16)
        for j in range(2)
    ]
    for q in range(blocks):
        source = (q + half * per_half) % blocks if halves > 1 else q
        rows = codes[pl.ds(pl.multiple_of(source * qrows, qrows), qrows)].reshape(2 * qrows, hidden)
        for j in range(2):
            values = dot(pick[j], rows)
            for c in range(cols):
                at = (2 * c + j) * qcols
                out[q * qrows : (q + 1) * qrows, at : at + qcols] = (
                    values[:, c * qcols : (c + 1) * qcols] * scales[source, j, c]
                ).astype(BF16)


def gate_up_kernel(halves, at, *refs):
    blocks, weights, out = refs[:-2], refs[-2], refs[-1]
    rows, width = blocks[0].shape[0], weights.shape[0] // halves
    cols = slice(at, at + out.shape[1])
    for i in range(len(blocks) // halves):
        total = dot(blocks[halves * i][:, :width], weights[:width, cols])
        for h in range(1, halves):
            total += dot(blocks[halves * i + h][:, :width], weights[h * width : (h + 1) * width, cols])
        out[i * rows : (i + 1) * rows, :] = total.astype(out.dtype)


def features_kernel(halves, *refs):
    blocks, out = refs[:-1], refs[-1]
    rows, width = blocks[0].shape[0], out.shape[1] // halves
    half = own_half(halves)
    for i in range(len(blocks) // halves):
        for h in range(halves):
            start = pl.multiple_of((half ^ h) * width, width)
            out[i * rows : (i + 1) * rows, pl.ds(start, width)] = blocks[halves * i + h][:, :width]


def add_kernel(kept, arrived, out):
    out[...] = (kept[...] + arrived[...].astype(F32)).astype(BF16)


def swiglu(total, cot, out):
    size = cot.shape[1]
    gate, up = total[:, :size], total[:, size:]
    c = cot.astype(F32)
    s = jax.nn.sigmoid(gate)
    out[:, :size] = (c * up * s * (1.0 + gate * (1.0 - s))).astype(BF16)
    out[:, size:] = (c * gate * s).astype(BF16)


def pair_swiglu_kernel(at, size, kept, near, far, cot, far_columns, out):
    rows, hidden = cot.shape
    total = kept[...] + near[...].astype(F32)
    total += jnp.concatenate([far[rows:, :], far[:rows, :]], axis=0).astype(F32)
    skip = far_columns.shape[1] - hidden
    for c in range(out.shape[1] // (2 * size)):
        cols = slice(2 * c * size, 2 * (c + 1) * size)
        h = at + c * size
        cots = [cot[:, h : h + size], far_columns[:, skip + h : skip + h + size]]
        swiglu(total[:, cols], jnp.concatenate(cots, axis=0), out.at[:, cols])


def swiglu_kernel(size, *refs):
    parts, cot, out = refs[:-2], refs[-2], refs[-1]
    total = parts[0][...]
    for part in parts[1:]:
        total += part[...].astype(F32)
    for c in range(cot.shape[1] // size):
        cols = slice(2 * c * size, 2 * (c + 1) * size)
        swiglu(total[:, cols], cot[:, c * size : (c + 1) * size], out.at[:, cols])


def gradient_chunk(parts, features, size, stacked, rows, out, written):
    count, depth = parts[0].shape[0], features.shape[1]
    for i, part in enumerate(parts):
        stacked[i * count : (i + 1) * count, :] = part[...]
    step = min(128, depth)
    for k in range(depth // step):
        d = slice(k * step, (k + 1) * step)
        values = dot(features[:, d], stacked[...], ((0,), (0,)))
        for c in range(stacked.shape[1] // (2 * size)):
            for j in range(2):
                at = (2 * c + j) * size
                rows[c, pl.ds(2 * k * step + j, step, stride=2), :] = values[:, at : at + size]
            both = rows[c, 2 * k * step : 2 * (k + 1) * step, :].astype(BF16)
            out[d, :, c * size : (c + 1) * size] = both.reshape(step, 2, size)
        written(k, d)


def chunk_kernel(at, size, first, *refs):
    *parts, features, out, stacked, rows = refs if first else refs[1:]
    out = out.at[:, :, at : at + stacked.shape[1] // 2]
    gradient_chunk(parts, features, size, stacked, rows, out, lambda k, d: None)


def gradient_kernel(at, size, *refs):
    finished, (*parts, features, out, stacked, rows, buf, sem) = refs[: at > 0], refs[at > 0 :]
    whole = finished[0] if finished else buf
    copies = []

    def copy(k, d):
        copies.append(pltpu.make_async_copy(whole.at[d], out.at[d], sem.at[k]))
        copies[-1].start()

    gradient_chunk(parts, features, size, stacked, rows, whole.at[:, :, at:], copy)
    for item in copies:
        item.wait()


def swap_group(x, size, k):
    s = group_partner(size, k)
    return lax.ppermute(x, "group", [(i, i ^ s) for i in range(size)])


def swap_blk(x, size, p):
    return lax.ppermute(x, "blk", [(i, i ^ p) for i in range(size)])


def swap_att(x):
    return lax.ppermute(x, "att", [(0, 1), (1, 0)])


def local(tokens, routed_experts, act_cotangent, weight_codes, weight_scales):
    ng, nb, na = lax.axis_size("group"), lax.axis_size("blk"), lax.axis_size("att")
    depth, _, _, hidden = weight_codes.shape
    halves = 2 if na == 2 and depth % 256 == 0 else 1
    width = depth // halves
    rows = ng * CAP
    sds = jax.ShapeDtypeStruct
    top, count = routed_experts.shape[1], tokens.shape[0]
    sent = call(
        functools.partial(pack_kernel, ng, nb, halves),
        [sds((CAP, nb * width + hidden), BF16)] * ng,
        (tokens, routed_experts.T, act_cotangent),
        [HBM, HBM, HBM],
        scratch=[
            pltpu.VMEM((nb, count, width), BF16),
            pltpu.VMEM((top, count), jnp.int32),
            pltpu.VMEM(act_cotangent.shape, BF16),
            pltpu.SemaphoreType.DMA((2 + nb,)),
        ],
        nbytes=2 << 20,
        vmem_bytes=PACK_VMEM,
    )
    codes, *sent = lax.optimization_barrier((weight_codes, *sent))
    weights = call(
        functools.partial(weights_kernel, halves),
        sds((depth, 2 * hidden), BF16),
        (weight_scales[:, 0].astype(F32), codes[:, 0]),
        [SMEM, VMEM],
        nbytes=4 << 20,
    )
    pieces = [sent[0]] + [swap_group(sent[s], ng, s) for s in range(1, ng)]
    weights, *pieces = lax.optimization_barrier((weights, *pieces))
    paired = halves == 2 and nb == 4
    with_cot = (3,) if paired else ()
    *columns, cot = call(
        functools.partial(regroup_kernel, ng, nb, width, with_cot),
        [sds((rows, width + hidden * (p in with_cot)), BF16) for p in range(nb)] + [sds((rows, hidden), BF16)],
        pieces,
        [VMEM] * ng,
        nbytes=1 << 20,
    )
    size = hidden // weight_scales.shape[3]
    x = {0: [columns[0]]} | {p: [swap_blk(columns[p], nb, p)] for p in range(1, nb)}
    if halves == 2:
        x = {p: [piece, swap_att(piece)] for p, (piece,) in x.items()}

    def gate_up(blocks, at, to, dtype):
        return call(
            functools.partial(gate_up_kernel, halves, 2 * at),
            sds((len(blocks) * rows, 2 * (to - at)), dtype),
            (*(piece for p in blocks for piece in x[p]), weights),
            [VMEM] * (len(blocks) * halves + 1),
            nbytes=1 << 20,
        )

    block_order = (0, 3, 1, 2) if paired else tuple(range(nb))
    if paired:
        cuts = [0, *(size * c for c in PAIRED_CUTS if size * c < hidden), hidden]
        chunks = list(zip(cuts[:-1], cuts[1:]))
        away = [gate_up((1, 2), *chunk, BF16) for chunk in chunks]
        features = call(
            functools.partial(features_kernel, halves),
            sds((nb * rows, depth), BF16),
            [piece for p in block_order for piece in x[p]],
            [VMEM] * (nb * halves),
            nbytes=3 << 20,
        )
        kept = [gate_up((0, 3), *chunk, F32) for chunk in chunks]
        near = [swap_blk(a, nb, 1) for a in away]
        pair = [
            call(add_kernel, sds(k.shape, BF16), (k, n), [VMEM] * 2, nbytes=1 << 18)
            for k, n in zip(kept, near)
        ]
        far = [swap_blk(p, nb, 3) for p in pair]
        own = [
            call(
                functools.partial(pair_swiglu_kernel, at, size),
                sds((2 * rows, 2 * (to - at)), BF16),
                (kept[c], near[c], far[c], cot, x[3][0]),
                [VMEM] * 5,
                nbytes=1 << 18,
            )
            for c, (at, to) in enumerate(chunks)
        ]
        parts = [[o, swap_blk(o, nb, 1)] for o in own]
    else:
        chunks = [(0, hidden)]
        features = call(
            functools.partial(features_kernel, halves),
            sds((nb * rows, depth), BF16),
            [piece for p in block_order for piece in x[p]],
            [VMEM] * (nb * halves),
            nbytes=3 << 20,
        )
        partial = [gate_up((p,), 0, hidden, BF16 if p else F32) for p in range(nb)]
        own = call(
            functools.partial(swiglu_kernel, size),
            sds((rows, 2 * hidden), BF16),
            (partial[0], *(swap_blk(partial[p], nb, p) for p in range(1, nb)), cot),
            [VMEM] * (nb + 1),
            nbytes=1 << 20,
        )
        parts = [[own] + [swap_blk(own, nb, p) for p in range(1, nb)]]

    def buffers(at, to):
        return [
            pltpu.VMEM((nb * rows, 2 * (to - at)), BF16),
            pltpu.VMEM(((to - at) // size, 2 * depth, size), F32),
        ]

    finished = []
    for (at, to), part in zip(chunks[:-1], parts):
        finished = [
            call(
                functools.partial(chunk_kernel, at, size, not finished),
                sds((depth, 2, hidden), BF16),
                (*finished, *part, features),
                [VMEM] * (len(finished) + len(part) + 1),
                scratch=buffers(at, to),
                nbytes=1 << 20,
                aliases={0: 0} if finished else {},
            )
        ]
    at, to = chunks[-1]
    step = min(128, depth)
    gradient = call(
        functools.partial(gradient_kernel, at, size),
        sds((depth, 2, hidden), BF16),
        (*finished, *parts[-1], features),
        [VMEM] * (len(finished) + len(parts[-1]) + 1),
        out_specs=HBM,
        scratch=[
            *buffers(at, to),
            pltpu.VMEM((16, 2, 128) if finished else (depth, 2, hidden), BF16),
            pltpu.SemaphoreType.DMA((depth // step,)),
        ],
        nbytes=4 << 20,
    )
    return gradient[:, None]


def solution(mesh):
    return jax.shard_map(
        local,
        mesh=mesh,
        in_specs=(
            P(("group", "blk"), None),
            P(("group", "blk"), None),
            P(("group", "blk"), None, "att"),
            P("blk", "group", None, "att"),
            P("blk", "group", None, "att"),
        ),
        out_specs=P("blk", "group", None, "att"),
        check_vma=False,
    )
```

time: 46.9 us -> 46 us (0.981)
  waiting for transfers between devices: 20.1 us -> 14 us
  starting transfers between devices: 18 us -> 22.6 us
  Pallas kernels: 7.65 us -> 8.2 us
    ppermute x9 -> x12, waiting for transfers between devices: 16.2 us -> 10.6 us  [swap_blk(): return lax.ppermute(x, 'blk', [(i, i ^ p) for i in range(size)])]
    ppermute x9 -> x12, starting transfers between devices: 13.3 us -> 17.4 us  [swap_blk(): return lax.ppermute(x, 'blk', [(i, i ^ p) for i in range(size)])]
    pallas_call x10 -> x19, Pallas kernels: 7.65 us -> 8.2 us  [call(): pl.pallas_call(kernel, out_shape=out_shape, in_specs=in_specs, out_specs=...]
    ppermute x4, waiting for transfers between devices: 1.26 us -> 0.74 us  [swap_att(): return lax.ppermute(x, 'att', [(0, 1), (1, 0)])]
  transfers between devices with their start and end apart: 16 -> 19, of which waited for: 11 -> 12; matrix products, arithmetic and copies ran while one was open for 0% -> 0% of each run, Pallas kernels for 7% -> 10%
where the time goes in v4:
time: 46 us; the launch traced here: 45.8 us
  starting transfers between devices  22.6 us (49%)
  waiting for transfers between devices  14 us (30%)
  Pallas kernels  8.2 us (18%)
  local copies, waits for them, and re-layouts  0.91 us (2%)
    ppermute x12, starting transfers between devices, swap_blk(): return lax.ppermute(x, 'blk', [(i, i ^ p) for i in range(size)])  17.4 us
    ppermute x12, waiting for transfers between devices, swap_blk(): return lax.ppermute(x, 'blk', [(i, i ^ p) for i in range(size)])  10.6 us
    pallas_call x19, Pallas kernels, call(): pl.pallas_call(kernel, out_shape=out_shape, in_specs=in_specs, out_specs=...  8.2 us
    ppermute x3, starting transfers between devices, swap_group(): return lax.ppermute(x, 'group', [(i, i ^ s) for i in range(size)])  4.6 us
    ppermute x3, waiting for transfers between devices, swap_group(): return lax.ppermute(x, 'group', [(i, i ^ s) for i in range(size)])  2.67 us
  transfers between devices with their start and end apart: 19, of which 12 were waited for; matrix products, arithmetic and copies ran while one was open for 0% of the time, Pallas kernels for 10%

profile of v4, /device:TPU:0, one launch (start us, length us, event | category | flops | bytes accessed | tf_op | source)
XLA Modules:
  0.0 45.8 jit_solution(8676626806747752086)
XLA Ops:
  0.0 0.8 %copy-done.1 = s32[128,8]{0,1:T(8,128)S(1)} copy-done((s32[128,8]{0,1:T(8,128)S(1)}, s32[128,8]{0,1:T(8,128)}, u32[]{:S(2)}) %copy-start.1) | copy-done | bytes 4120
  0.8 2.1 %shard_map.55 = (bf16[16,2432]{1,0:T(8,128)(2,1)S(1)}, bf16[16,2432]{1,0:T(8,128)(2,1)S(1)}, bf16[16,2432]{1,0:T(8,128)(2,1)S(1)}, bf16[16,2432]{1,0:T(8,128)(2,1)S(1)}) custom-call(bf16[128,4096]{1,0:T(8,128)(2,1)} %tokens.1, s32[8,128]{1,0:T(8,128)S(1)} %bitcast.9, bf16[128,8,384]{2,1,0:T(8,128)(2,1)} %act.1), custom_call_target="tpu_custom_call" | custom-call | bytes 2097152 | tf_op jit(solution)/shard_map/pallas_call | solution.py:20
  2.9 4.0 %collective-permute-start = (bf16[16,2432]{1,0:T(8,128)(2,1)S(1)}, bf16[16,2432]{1,0:T(8,128)(2,1)S(1)}, u32[]{:S(2)}, u32[]{:S(2)}) collective-permute-start(bf16[16,2432]{1,0:T(8,128)(2,1)S(1)} %get-tuple-element.30), channel_id=1, source_target_pairs={{0,24},{8,16},{16,8},{24,0},{1,25},{9,17},{17,9},{25,1},{2,26},{10... | collective-permute-start | bytes 233480 | tf_op jit(solution)/shard_map/ppermute | solution.py:225
  6.9 0.5 %collective-permute-start.1 = (bf16[16,2432]{1,0:T(8,128)(2,1)S(1)}, bf16[16,2432]{1,0:T(8,128)(2,1)S(1)}, u32[]{:S(2)}, u32[]{:S(2)}) collective-permute-start(bf16[16,2432]{1,0:T(8,128)(2,1)S(1)} %get-tuple-element.31), channel_id=1, source_target_pairs={{0,16},{8,24},{16,0},{24,8},{1,17},{9,25},{17,1},{25,9},{2,18},{10... | collective-permute-start | bytes 233480 | tf_op jit(solution)/shard_map/ppermute | solution.py:225
  7.4 0.1 collective-permute-start.2
  7.5 0.1 copy.7.scales
  7.6 1.5 %shard_map.56.refs_4_ = bf16[1024,768]{1,0:T(8,128)(2,1)S(1)} custom-call(f32[8,2,3]{2,1,0:T(2,128)S(1)} %copy.7.scales, bf16[1024,2,384]{2,1,0:T(2,128)(2,1)S(1)} %bitcast.8), custom_call_target="tpu_custom_call" | custom-call | bytes 4194304 | tf_op jit(solution)/shard_map/pallas_call | solution.py:20
  9.1 0.2 collective-permute-done.refs_1_
  9.3 1.9 %collective-permute-done.1.refs_2_ = bf16[16,2432]{1,0:T(8,128)(2,1)S(1)} collective-permute-done((bf16[16,2432]{1,0:T(8,128)(2,1)S(1)}, bf16[16,2432]{1,0:T(8,128)(2,1)S(1)}, u32[]{:S(2)}, u32[]{:S(2)}) %collective-permute-start.1) | collective-permute-done | bytes 77856 | tf_op jit(solution)/shard_map/ppermute | solution.py:225
  11.3 0.5 %collective-permute-done.2.refs_3_ = bf16[16,2432]{1,0:T(8,128)(2,1)S(1)} collective-permute-done((bf16[16,2432]{1,0:T(8,128)(2,1)S(1)}, bf16[16,2432]{1,0:T(8,128)(2,1)S(1)}, u32[]{:S(2)}, u32[]{:S(2)}) %collective-permute-start.2) | collective-permute-done | bytes 77856 | tf_op jit(solution)/shard_map/ppermute | solution.py:225
  11.8 3.7 %collective-permute-start.4 = (bf16[64,896]{1,0:T(8,128)(2,1)S(1)}, bf16[64,896]{1,0:T(8,128)(2,1)S(1)}, u32[]{:S(2)}, u32[]{:S(2)}) collective-permute-start(bf16[64,896]{1,0:T(8,128)(2,1)S(1)} %get-tuple-element.38), channel_id=1, source_target_pairs={{0,6},{2,4},{4,2},{6,0},{1,7},{3,5},{5,3},{7,1},{8,14},{10,12},{12... | collective-permute-start | bytes 344072 | tf_op jit(solution)/shard_map/ppermute | solution.py:229
  15.5 0.8 %collective-permute-start.8 = (bf16[64,512]{1,0:T(8,128)(2,1)S(1)}, bf16[64,512]{1,0:T(8,128)(2,1)S(1)}, u32[]{:S(2)}, u32[]{:S(2)}) collective-permute-start(bf16[64,512]{1,0:T(8,128)(2,1)S(1)} %get-tuple-element.41), channel_id=1, source_target_pairs={{0,4},{2,6},{4,0},{6,2},{1,5},{3,7},{5,1},{7,3},{8,12},{10,14},{12... | collective-permute-start | bytes 196616 | tf_op jit(solution)/shard_map/ppermute | solution.py:229
  16.3 3.6 %collective-permute-done.6.refs_0_.refs_4_ = bf16[64,512]{1,0:T(8,128)(2,1)S(1)} collective-permute-done((bf16[64,512]{1,0:T(8,128)(2,1)S(1)}, bf16[64,512]{1,0:T(8,128)(2,1)S(1)}, u32[]{:S(2)}, u32[]{:S(2)}) %collective-permute-start.6) | collective-permute-done | bytes 65568 | tf_op jit(solution)/shard_map/ppermute | solution.py:229
  19.9 1.6 %collective-permute-done.8.refs_2_.refs_6_ = bf16[64,512]{1,0:T(8,128)(2,1)S(1)} collective-permute-done((bf16[64,512]{1,0:T(8,128)(2,1)S(1)}, bf16[64,512]{1,0:T(8,128)(2,1)S(1)}, u32[]{:S(2)}, u32[]{:S(2)}) %collective-permute-start.8) | collective-permute-done | bytes 65568 | tf_op jit(solution)/shard_map/ppermute | solution.py:229
  21.5 0.0 collective-permute-start.9
  21.5 0.0 collective-permute-done.4.refs_2_.far_columns
  21.5 0.5 %collective-permute-start.5 = (bf16[64,896]{1,0:T(8,128)(2,1)S(1)}, bf16[64,896]{1,0:T(8,128)(2,1)S(1)}, u32[]{:S(2)}, u32[]{:S(2)}) collective-permute-start(bf16[64,896]{1,0:T(8,128)(2,1)S(1)} %collective-permute-done.4.refs_2_.far_columns), channel_id=1, source_target_pairs={{0,1},{1,0},{2,3},{3,2},{4,5},{5,4},{6,7},{7,6},{8,9},{9,8},{10,11... | collective-permute-start | bytes 344072 | tf_op jit(solution)/shard_map/ppermute | solution.py:233
  22.0 0.0 collective-permute-start.3
  22.0 0.7 %collective-permute-done.9.refs_3_.refs_7_ = bf16[64,512]{1,0:T(8,128)(2,1)S(1)} collective-permute-done((bf16[64,512]{1,0:T(8,128)(2,1)S(1)}, bf16[64,512]{1,0:T(8,128)(2,1)S(1)}, u32[]{:S(2)}, u32[]{:S(2)}) %collective-permute-start.9) | collective-permute-done | bytes 65568 | tf_op jit(solution)/shard_map/ppermute | solution.py:233
  22.8 0.3 shard_map.59
  23.1 1.3 %collective-permute-start.10 = (bf16[128,256]{1,0:T(8,128)(2,1)S(1)}, bf16[128,256]{1,0:T(8,128)(2,1)S(1)}, u32[]{:S(2)}, u32[]{:S(2)}) collective-permute-start(bf16[128,256]{1,0:T(8,128)(2,1)S(1)} %shard_map.59), channel_id=1, source_target_pairs={{0,2},{2,0},{4,6},{6,4},{1,3},{3,1},{5,7},{7,5},{8,10},{10,8},{12,... | collective-permute-start | bytes 196616 | tf_op jit(solution)/shard_map/ppermute | solution.py:229
  24.4 0.3 shard_map.65
  24.7 0.8 %collective-permute-start.13 = (bf16[128,256]{1,0:T(8,128)(2,1)S(1)}, bf16[128,256]{1,0:T(8,128)(2,1)S(1)}, u32[]{:S(2)}, u32[]{:S(2)}) collective-permute-start(bf16[128,256]{1,0:T(8,128)(2,1)S(1)} %shard_map.65), channel_id=1, source_target_pairs={{0,2},{2,0},{4,6},{6,4},{1,3},{3,1},{5,7},{7,5},{8,10},{10,8},{12,... | collective-permute-start | bytes 196616 | tf_op jit(solution)/shard_map/ppermute | solution.py:229
  25.5 0.3 shard_map.70
  25.8 1.3 %collective-permute-start.16 = (bf16[128,256]{1,0:T(8,128)(2,1)S(1)}, bf16[128,256]{1,0:T(8,128)(2,1)S(1)}, u32[]{:S(2)}, u32[]{:S(2)}) collective-permute-start(bf16[128,256]{1,0:T(8,128)(2,1)S(1)} %shard_map.70), channel_id=1, source_target_pairs={{0,2},{2,0},{4,6},{6,4},{1,3},{3,1},{5,7},{7,5},{8,10},{10,8},{12,... | collective-permute-start | bytes 196616 | tf_op jit(solution)/shard_map/ppermute | solution.py:229
  27.1 0.0 collective-permute-done.3.refs_1_
  27.1 0.0 collective-permute-done.5.refs_3_
  27.1 0.3 shard_map.58.kept
  27.4 0.2 collective-permute-done.10.arrived.near
  27.6 4.3 %collective-permute-start.11 = (bf16[128,256]{1,0:T(8,128)(2,1)S(1)}, bf16[128,256]{1,0:T(8,128)(2,1)S(1)}, u32[]{:S(2)}, u32[]{:S(2)}) collective-permute-start(bf16[128,256]{1,0:T(8,128)(2,1)S(1)} %shard_map.60), channel_id=1, source_target_pairs={{0,6},{2,4},{4,2},{6,0},{1,7},{3,5},{5,3},{7,1},{8,14},{10,12},{12... | collective-permute-start | bytes 196616 | tf_op jit(solution)/shard_map/ppermute | solution.py:229
  31.9 0.3 shard_map.64.kept
  32.2 0.9 %collective-permute-start.14 = (bf16[128,256]{1,0:T(8,128)(2,1)S(1)}, bf16[128,256]{1,0:T(8,128)(2,1)S(1)}, u32[]{:S(2)}, u32[]{:S(2)}) collective-permute-start(bf16[128,256]{1,0:T(8,128)(2,1)S(1)} %shard_map.66), channel_id=1, source_target_pairs={{0,6},{2,4},{4,2},{6,0},{1,7},{3,5},{5,3},{7,1},{8,14},{10,12},{12... | collective-permute-start | bytes 196616 | tf_op jit(solution)/shard_map/ppermute | solution.py:229
  33.2 0.3 shard_map.69.kept
  33.5 3.0 %collective-permute-start.17 = (bf16[128,256]{1,0:T(8,128)(2,1)S(1)}, bf16[128,256]{1,0:T(8,128)(2,1)S(1)}, u32[]{:S(2)}, u32[]{:S(2)}) collective-permute-start(bf16[128,256]{1,0:T(8,128)(2,1)S(1)} %shard_map.71), channel_id=1, source_target_pairs={{0,6},{2,4},{4,2},{6,0},{1,7},{3,5},{5,3},{7,1},{8,14},{10,12},{12... | collective-permute-start | bytes 196616 | tf_op jit(solution)/shard_map/ppermute | solution.py:229
  36.5 0.1 shard_map.61.refs_0_
  36.6 0.1 collective-permute-start.12
  36.6 2.3 %collective-permute-done.14.far = bf16[128,256]{1,0:T(8,128)(2,1)S(1)} collective-permute-done((bf16[128,256]{1,0:T(8,128)(2,1)S(1)}, bf16[128,256]{1,0:T(8,128)(2,1)S(1)}, u32[]{:S(2)}, u32[]{:S(2)}) %collective-permute-start.14) | collective-permute-done | bytes 65568 | tf_op jit(solution)/shard_map/ppermute | solution.py:229
  38.9 0.1 shard_map.67.refs_1_
  39.0 0.1 collective-permute-start.15
  39.1 0.9 %collective-permute-done.17.far = bf16[128,256]{1,0:T(8,128)(2,1)S(1)} collective-permute-done((bf16[128,256]{1,0:T(8,128)(2,1)S(1)}, bf16[128,256]{1,0:T(8,128)(2,1)S(1)}, u32[]{:S(2)}, u32[]{:S(2)}) %collective-permute-start.17) | collective-permute-done | bytes 65568 | tf_op jit(solution)/shard_map/ppermute | solution.py:229
  40.0 0.1 shard_map.72.refs_1_
  40.0 1.2 %collective-permute-start.18 = (bf16[128,256]{1,0:T(8,128)(2,1)S(1)}, bf16[128,256]{1,0:T(8,128)(2,1)S(1)}, u32[]{:S(2)}, u32[]{:S(2)}) collective-permute-start(bf16[128,256]{1,0:T(8,128)(2,1)S(1)} %shard_map.72.refs_1_), channel_id=1, source_target_pairs={{0,2},{2,0},{4,6},{6,4},{1,3},{3,1},{5,7},{7,5},{8,10},{10,8},{12,... | collective-permute-start | bytes 196616 | tf_op jit(solution)/shard_map/ppermute | solution.py:229
  41.2 0.2 collective-permute-done.12.refs_1_
  41.4 0.6 %shard_map.63.refs_0_ = bf16[1024,2,384]{2,1,0:T(2,128)(2,1)S(1)} custom-call(bf16[128,256]{1,0:T(8,128)(2,1)S(1)} %shard_map.61.refs_0_, bf16[128,256]{1,0:T(8,128)(2,1)S(1)} %collective-permute-done.12.refs_1_, bf16[256,1024]{1,0:T(8,128)(2,1)S(1)} %shard_map.62.refs_2_.refs_3_), custom_call_target="tpu_custom_call" | custom-call | bytes 1048576 | tf_op jit(solution)/shard_map/pallas_call | solution.py:20
  42.0 1.3 %collective-permute-done.15.refs_2_ = bf16[128,256]{1,0:T(8,128)(2,1)S(1)} collective-permute-done((bf16[128,256]{1,0:T(8,128)(2,1)S(1)}, bf16[128,256]{1,0:T(8,128)(2,1)S(1)}, u32[]{:S(2)}, u32[]{:S(2)}) %collective-permute-start.15) | collective-permute-done | bytes 65568 | tf_op jit(solution)/shard_map/ppermute | solution.py:229
  43.3 0.6 %shard_map.68.refs_0_ = bf16[1024,2,384]{2,1,0:T(2,128)(2,1)S(1)} custom-call(bf16[1024,2,384]{2,1,0:T(2,128)(2,1)S(1)} %shard_map.63.refs_0_, bf16[128,256]{1,0:T(8,128)(2,1)S(1)} %shard_map.67.refs_1_, bf16[128,256]{1,0:T(8,128)(2,1)S(1)} %collective-permute-done.15.refs_2_, ...), custom_call_target="tpu_custom_call", output_to_operand_aliasing={{}: (0, {})} | custom-call | bytes 1048576 | tf_op jit(solution)/shard_map/pallas_call | solution.py:20
  43.9 0.5 %collective-permute-done.18.refs_2_ = bf16[128,256]{1,0:T(8,128)(2,1)S(1)} collective-permute-done((bf16[128,256]{1,0:T(8,128)(2,1)S(1)}, bf16[128,256]{1,0:T(8,128)(2,1)S(1)}, u32[]{:S(2)}, u32[]{:S(2)}) %collective-permute-start.18) | collective-permute-done | bytes 65568 | tf_op jit(solution)/shard_map/ppermute | solution.py:229
  44.4 1.5 %shard_map.73 = bf16[1024,2,384]{2,1,0:T(2,128)(2,1)} custom-call(bf16[1024,2,384]{2,1,0:T(2,128)(2,1)S(1)} %shard_map.68.refs_0_, bf16[128,256]{1,0:T(8,128)(2,1)S(1)} %shard_map.72.refs_1_, bf16[128,256]{1,0:T(8,128)(2,1)S(1)} %collective-permute-done.18.refs_2_, bf16[256,1024]{1,0:T(8,128)(2,1)S(1)} %shard_map.62.refs_2_.refs_3_), custom_call_target="tpu_custom_call" | custom-call | bytes 4194304 | tf_op jit(solution)/shard_map/pallas_call | solution.py:20
  (17 shorter events, 0.1 us)
Async XLA Ops:
  0.0 7.6 %copy-start = (bf16[1024,1,2,384]{3,2,1,0:T(2,128)(2,1)S(1)}, bf16[1024,1,2,384]{3,2,1,0:T(2,128)(2,1)}, u32[]{:S(2)}) copy-start(bf16[1024,1,2,384]{3,2,1,0:T(2,128)(2,1)} %param.8) | copy-start | bytes 4718596
  0.0 0.8 %copy-start.1 = (s32[128,8]{0,1:T(8,128)S(1)}, s32[128,8]{0,1:T(8,128)}, u32[]{:S(2)}) copy-start(s32[128,8]{0,1:T(8,128)} %param.6) | copy-start | bytes 12292
  0.8 6.7 %copy-start.2 = (bf16[8,1,2,3]{0,2,3,1:T(2,128)(2,1)S(1)}, bf16[8,1,2,3]{0,2,3,1:T(2,128)(2,1)}, u32[]{:S(2)}) copy-start(bf16[8,1,2,3]{0,2,3,1:T(2,128)(2,1)} %param.9) | copy-start | bytes 292
  2.9 6.4 %collective-permute-start = (bf16[16,2432]{1,0:T(8,128)(2,1)S(1)}, bf16[16,2432]{1,0:T(8,128)(2,1)S(1)}, u32[]{:S(2)}, u32[]{:S(2)}) collective-permute-start(bf16[16,2432]{1,0:T(8,128)(2,1)S(1)} %get-tuple-element.30), channel_id=1, source_target_pairs={{0,24},{8,16},{16,8},{24,0},{1,25},{9,17},{17,9},{25,1},{2,26},{10... | collective-permute-start | bytes 233480 | tf_op jit(solution)/shard_map/ppermute | solution.py:225
  6.9 4.4 %collective-permute-start.1 = (bf16[16,2432]{1,0:T(8,128)(2,1)S(1)}, bf16[16,2432]{1,0:T(8,128)(2,1)S(1)}, u32[]{:S(2)}, u32[]{:S(2)}) collective-permute-start(bf16[16,2432]{1,0:T(8,128)(2,1)S(1)} %get-tuple-element.31), channel_id=1, source_target_pairs={{0,16},{8,24},{16,0},{24,8},{1,17},{9,25},{17,1},{25,9},{2,18},{10... | collective-permute-start | bytes 233480 | tf_op jit(solution)/shard_map/ppermute | solution.py:225
  7.4 4.4 %collective-permute-start.2 = (bf16[16,2432]{1,0:T(8,128)(2,1)S(1)}, bf16[16,2432]{1,0:T(8,128)(2,1)S(1)}, u32[]{:S(2)}, u32[]{:S(2)}) collective-permute-start(bf16[16,2432]{1,0:T(8,128)(2,1)S(1)} %get-tuple-element.32), channel_id=1, source_target_pairs={{0,8},{8,0},{16,24},{24,16},{1,9},{9,1},{17,25},{25,17},{2,10},{10... | collective-permute-start | bytes 233480 | tf_op jit(solution)/shard_map/ppermute | solution.py:225
  11.8 9.7 %collective-permute-start.4 = (bf16[64,896]{1,0:T(8,128)(2,1)S(1)}, bf16[64,896]{1,0:T(8,128)(2,1)S(1)}, u32[]{:S(2)}, u32[]{:S(2)}) collective-permute-start(bf16[64,896]{1,0:T(8,128)(2,1)S(1)} %get-tuple-element.38), channel_id=1, source_target_pairs={{0,6},{2,4},{4,2},{6,0},{1,7},{3,5},{5,3},{7,1},{8,14},{10,12},{12... | collective-permute-start | bytes 344072 | tf_op jit(solution)/shard_map/ppermute | solution.py:229
  15.5 4.4 %collective-permute-start.6 = (bf16[64,512]{1,0:T(8,128)(2,1)S(1)}, bf16[64,512]{1,0:T(8,128)(2,1)S(1)}, u32[]{:S(2)}, u32[]{:S(2)}) collective-permute-start(bf16[64,512]{1,0:T(8,128)(2,1)S(1)} %get-tuple-element.40), channel_id=1, source_target_pairs={{0,2},{2,0},{4,6},{6,4},{1,3},{3,1},{5,7},{7,5},{8,10},{10,8},{12,... | collective-permute-start | bytes 196616 | tf_op jit(solution)/shard_map/ppermute | solution.py:229
  15.5 6.0 %collective-permute-start.8 = (bf16[64,512]{1,0:T(8,128)(2,1)S(1)}, bf16[64,512]{1,0:T(8,128)(2,1)S(1)}, u32[]{:S(2)}, u32[]{:S(2)}) collective-permute-start(bf16[64,512]{1,0:T(8,128)(2,1)S(1)} %get-tuple-element.41), channel_id=1, source_target_pairs={{0,4},{2,6},{4,0},{6,2},{1,5},{3,7},{5,1},{7,3},{8,12},{10,14},{12... | collective-permute-start | bytes 196616 | tf_op jit(solution)/shard_map/ppermute | solution.py:229
  19.9 2.1 %collective-permute-start.7 = (bf16[64,512]{1,0:T(8,128)(2,1)S(1)}, bf16[64,512]{1,0:T(8,128)(2,1)S(1)}, u32[]{:S(2)}, u32[]{:S(2)}) collective-permute-start(bf16[64,512]{1,0:T(8,128)(2,1)S(1)} %collective-permute-done.6.refs_0_.refs_4_), channel_id=1, source_target_pairs={{0,1},{1,0},{2,3},{3,2},{4,5},{5,4},{6,7},{7,6},{8,9},{9,8},{10,11... | collective-permute-start | bytes 196616 | tf_op jit(solution)/shard_map/ppermute | solution.py:233
  21.5 1.3 %collective-permute-start.9 = (bf16[64,512]{1,0:T(8,128)(2,1)S(1)}, bf16[64,512]{1,0:T(8,128)(2,1)S(1)}, u32[]{:S(2)}, u32[]{:S(2)}) collective-permute-start(bf16[64,512]{1,0:T(8,128)(2,1)S(1)} %collective-permute-done.8.refs_2_.refs_6_), channel_id=1, source_target_pairs={{0,1},{1,0},{2,3},{3,2},{4,5},{5,4},{6,7},{7,6},{8,9},{9,8},{10,11... | collective-permute-start | bytes 196616 | tf_op jit(solution)/shard_map/ppermute | solution.py:233
  21.5 5.6 %collective-permute-start.5 = (bf16[64,896]{1,0:T(8,128)(2,1)S(1)}, bf16[64,896]{1,0:T(8,128)(2,1)S(1)}, u32[]{:S(2)}, u32[]{:S(2)}) collective-permute-start(bf16[64,896]{1,0:T(8,128)(2,1)S(1)} %collective-permute-done.4.refs_2_.far_columns), channel_id=1, source_target_pairs={{0,1},{1,0},{2,3},{3,2},{4,5},{5,4},{6,7},{7,6},{8,9},{9,8},{10,11... | collective-permute-start | bytes 344072 | tf_op jit(solution)/shard_map/ppermute | solution.py:233
  22.0 5.1 %collective-permute-start.3 = (bf16[64,512]{1,0:T(8,128)(2,1)S(1)}, bf16[64,512]{1,0:T(8,128)(2,1)S(1)}, u32[]{:S(2)}, u32[]{:S(2)}) collective-permute-start(bf16[64,512]{1,0:T(8,128)(2,1)S(1)} %get-tuple-element.37.refs_0_), channel_id=1, source_target_pairs={{0,1},{1,0},{2,3},{3,2},{4,5},{5,4},{6,7},{7,6},{8,9},{9,8},{10,11... | collective-permute-start | bytes 196616 | tf_op jit(solution)/shard_map/ppermute | solution.py:233
  23.1 4.6 %collective-permute-start.10 = (bf16[128,256]{1,0:T(8,128)(2,1)S(1)}, bf16[128,256]{1,0:T(8,128)(2,1)S(1)}, u32[]{:S(2)}, u32[]{:S(2)}) collective-permute-start(bf16[128,256]{1,0:T(8,128)(2,1)S(1)} %shard_map.59), channel_id=1, source_target_pairs={{0,2},{2,0},{4,6},{6,4},{1,3},{3,1},{5,7},{7,5},{8,10},{10,8},{12,... | collective-permute-start | bytes 196616 | tf_op jit(solution)/shard_map/ppermute | solution.py:229
  24.7 7.5 %collective-permute-start.13 = (bf16[128,256]{1,0:T(8,128)(2,1)S(1)}, bf16[128,256]{1,0:T(8,128)(2,1)S(1)}, u32[]{:S(2)}, u32[]{:S(2)}) collective-permute-start(bf16[128,256]{1,0:T(8,128)(2,1)S(1)} %shard_map.65), channel_id=1, source_target_pairs={{0,2},{2,0},{4,6},{6,4},{1,3},{3,1},{5,7},{7,5},{8,10},{10,8},{12,... | collective-permute-start | bytes 196616 | tf_op jit(solution)/shard_map/ppermute | solution.py:229
  25.8 7.7 %collective-permute-start.16 = (bf16[128,256]{1,0:T(8,128)(2,1)S(1)}, bf16[128,256]{1,0:T(8,128)(2,1)S(1)}, u32[]{:S(2)}, u32[]{:S(2)}) collective-permute-start(bf16[128,256]{1,0:T(8,128)(2,1)S(1)} %shard_map.70), channel_id=1, source_target_pairs={{0,2},{2,0},{4,6},{6,4},{1,3},{3,1},{5,7},{7,5},{8,10},{10,8},{12,... | collective-permute-start | bytes 196616 | tf_op jit(solution)/shard_map/ppermute | solution.py:229
  27.6 8.9 %collective-permute-start.11 = (bf16[128,256]{1,0:T(8,128)(2,1)S(1)}, bf16[128,256]{1,0:T(8,128)(2,1)S(1)}, u32[]{:S(2)}, u32[]{:S(2)}) collective-permute-start(bf16[128,256]{1,0:T(8,128)(2,1)S(1)} %shard_map.60), channel_id=1, source_target_pairs={{0,6},{2,4},{4,2},{6,0},{1,7},{3,5},{5,3},{7,1},{8,14},{10,12},{12... | collective-permute-start | bytes 196616 | tf_op jit(solution)/shard_map/ppermute | solution.py:229
  32.2 6.7 %collective-permute-start.14 = (bf16[128,256]{1,0:T(8,128)(2,1)S(1)}, bf16[128,256]{1,0:T(8,128)(2,1)S(1)}, u32[]{:S(2)}, u32[]{:S(2)}) collective-permute-start(bf16[128,256]{1,0:T(8,128)(2,1)S(1)} %shard_map.66), channel_id=1, source_target_pairs={{0,6},{2,4},{4,2},{6,0},{1,7},{3,5},{5,3},{7,1},{8,14},{10,12},{12... | collective-permute-start | bytes 196616 | tf_op jit(solution)/shard_map/ppermute | solution.py:229
  33.5 6.5 %collective-permute-start.17 = (bf16[128,256]{1,0:T(8,128)(2,1)S(1)}, bf16[128,256]{1,0:T(8,128)(2,1)S(1)}, u32[]{:S(2)}, u32[]{:S(2)}) collective-permute-start(bf16[128,256]{1,0:T(8,128)(2,1)S(1)} %shard_map.71), channel_id=1, source_target_pairs={{0,6},{2,4},{4,2},{6,0},{1,7},{3,5},{5,3},{7,1},{8,14},{10,12},{12... | collective-permute-start | bytes 196616 | tf_op jit(solution)/shard_map/ppermute | solution.py:229
  36.6 4.9 %collective-permute-start.12 = (bf16[128,256]{1,0:T(8,128)(2,1)S(1)}, bf16[128,256]{1,0:T(8,128)(2,1)S(1)}, u32[]{:S(2)}, u32[]{:S(2)}) collective-permute-start(bf16[128,256]{1,0:T(8,128)(2,1)S(1)} %shard_map.61.refs_0_), channel_id=1, source_target_pairs={{0,2},{2,0},{4,6},{6,4},{1,3},{3,1},{5,7},{7,5},{8,10},{10,8},{12,... | collective-permute-start | bytes 196616 | tf_op jit(solution)/shard_map/ppermute | solution.py:229
  39.0 4.3 %collective-permute-start.15 = (bf16[128,256]{1,0:T(8,128)(2,1)S(1)}, bf16[128,256]{1,0:T(8,128)(2,1)S(1)}, u32[]{:S(2)}, u32[]{:S(2)}) collective-permute-start(bf16[128,256]{1,0:T(8,128)(2,1)S(1)} %shard_map.67.refs_1_), channel_id=1, source_target_pairs={{0,2},{2,0},{4,6},{6,4},{1,3},{3,1},{5,7},{7,5},{8,10},{10,8},{12,... | collective-permute-start | bytes 196616 | tf_op jit(solution)/shard_map/ppermute | solution.py:229
  40.0 4.3 %collective-permute-start.18 = (bf16[128,256]{1,0:T(8,128)(2,1)S(1)}, bf16[128,256]{1,0:T(8,128)(2,1)S(1)}, u32[]{:S(2)}, u32[]{:S(2)}) collective-permute-start(bf16[128,256]{1,0:T(8,128)(2,1)S(1)} %shard_map.72.refs_1_), channel_id=1, source_target_pairs={{0,2},{2,0},{4,6},{6,4},{1,3},{3,1},{5,7},{7,5},{8,10},{10,8},{12,... | collective-permute-start | bytes 196616 | tf_op jit(solution)/shard_map/ppermute | solution.py:229

commit v5 on v4

--- a/solution.py
+++ b/solution.py
@@ -12,10 +12,9 @@
 F32 = jnp.float32
 VMEM_BYTES = 40 * 1024 * 1024
 PAIRED_CUTS = (1, 2)
-PACK_VMEM = 53 * 1024 * 1024
-
-
-def call(kernel, out_shape, args, in_specs, out_specs=None, scratch=(), flops=0, nbytes=0, vmem_bytes=VMEM_BYTES, aliases=None):
+
+
+def call(kernel, out_shape, args, in_specs, out_specs=None, scratch=(), flops=0, nbytes=0, aliases=None):
     vmem = pl.BlockSpec(memory_space=pltpu.VMEM)
     return pl.pallas_call(
         kernel,
@@ -24,7 +23,7 @@
         out_specs=jax.tree.map(lambda _: vmem, out_shape) if out_specs is None else out_specs,
         scratch_shapes=scratch,
         input_output_aliases=aliases or {},
-        compiler_params=pltpu.CompilerParams(vmem_limit_bytes=vmem_bytes),
+        compiler_params=pltpu.CompilerParams(vmem_limit_bytes=VMEM_BYTES),
         cost_estimate=pl.CostEstimate(flops=flops, bytes_accessed=nbytes, transcendentals=0),
     )(*args)
 
@@ -57,13 +56,17 @@
     width = tokens.shape[1] // (nb * halves)
     group, block, half = lax.axis_index("group"), lax.axis_index("blk"), own_half(halves)
     copies = [pltpu.make_async_copy(routed, routed_buf, sem.at[0])]
-    copies.append(pltpu.make_async_copy(act, act_buf, sem.at[1]))
     for p in range(nb):
         partner = block ^ p
         start = pl.multiple_of((partner * halves + half) * width, width)
         copies.append(
-            pltpu.make_async_copy(tokens.at[:, pl.ds(start, width)], token_buf.at[p], sem.at[2 + p])
+            pltpu.make_async_copy(tokens.at[:, pl.ds(start, width)], token_buf.at[p], sem.at[1 + p])
         )
+    first = len(copies)
+    size = count // 4
+    for k in range(4):
+        at = pl.ds(k * size, size)
+        copies.append(pltpu.make_async_copy(act.at[at], act_buf.at[at], sem.at[first + k]))
     for copy in copies:
         copy.start()
     upto = (iota((count, count), 0) <= iota((count, count), 1)).astype(F32).astype(BF16)
@@ -81,16 +84,17 @@
     ids_wide = dot(ids.astype(F32).astype(BF16), spread)
     ids_flat = jnp.sum(jnp.where(own_slot, ids_wide, 0.0), axis=0, keepdims=True)
     pair = jnp.where(ids_flat == expert, dot(selector, spread), 0.0).astype(BF16)
-    copies[1].wait()
+    for p in range(nb):
+        copies[1 + p].wait()
+        part = dot(selector, token_buf[p]).astype(BF16)
+        for s in range(ng):
+            outs[s][:, p * width : (p + 1) * width] = part[s * CAP : (s + 1) * CAP]
+    for copy in copies[first:]:
+        copy.wait()
     hidden = act.shape[2]
     cot = dot(pair, act_buf[...].reshape(count * top, hidden)).astype(BF16)
     for s in range(ng):
         outs[s][:, nb * width :] = cot[s * CAP : (s + 1) * CAP]
-    for p in range(nb):
-        copies[2 + p].wait()
-        part = dot(selector, token_buf[p]).astype(BF16)
-        for s in range(ng):
-            outs[s][:, p * width : (p + 1) * width] = part[s * CAP : (s + 1) * CAP]
 
 
 def regroup_kernel(ng, nb, width, with_cot, *refs):
@@ -105,16 +109,24 @@
         outs[nb][at, :] = cot
 
 
-def weights_kernel(halves, scales, codes, out):
+def weights_kernel(halves, scales, codes_hbm, out, codes, sem):
     depth, _, hidden = codes.shape
     blocks, _, cols = scales.shape
     qrows, qcols = depth // blocks, hidden // cols
+    copies = [
+        pltpu.make_async_copy(codes_hbm.at[at], codes.at[at], sem.at[q])
+        for q, at in enumerate(pl.ds(q * qrows, qrows) for q in range(blocks))
+    ]
+    for copy in copies:
+        copy.start()
     half = own_half(halves)
     per_half = blocks // halves
     pick = [
         (iota((qrows, 2 * qrows), 1) == 2 * iota((qrows, 2 * qrows), 0) + j).astype(F32).astype(BF16)
         for j in range(2)
     ]
+    for copy in copies:
+        copy.wait()
     for q in range(blocks):
         source = (q + half * per_half) % blocks if halves > 1 else q
         rows = codes[pl.ds(pl.multiple_of(source * qrows, qrows), qrows)].reshape(2 * qrows, hidden)
@@ -244,29 +256,32 @@
     sent = call(
         functools.partial(pack_kernel, ng, nb, halves),
         [sds((CAP, nb * width + hidden), BF16)] * ng,
-        (tokens, routed_experts.T, act_cotangent),
+        [pltpu.with_memory_space_constraint(a, pltpu.HBM) for a in (tokens, routed_experts.T, act_cotangent)],
         [HBM, HBM, HBM],
         scratch=[
             pltpu.VMEM((nb, count, width), BF16),
             pltpu.VMEM((top, count), jnp.int32),
             pltpu.VMEM(act_cotangent.shape, BF16),
-            pltpu.SemaphoreType.DMA((2 + nb,)),
+            pltpu.SemaphoreType.DMA((5 + nb,)),
         ],
         nbytes=2 << 20,
-        vmem_bytes=PACK_VMEM,
     )
     codes, *sent = lax.optimization_barrier((weight_codes, *sent))
     weights = call(
         functools.partial(weights_kernel, halves),
         sds((depth, 2 * hidden), BF16),
-        (weight_scales[:, 0].astype(F32), codes[:, 0]),
-        [SMEM, VMEM],
+        (weight_scales[:, 0].astype(F32), pltpu.with_memory_space_constraint(codes[:, 0], pltpu.HBM)),
+        [SMEM, HBM],
+        scratch=[
+            pltpu.VMEM((depth, 2, hidden), BF16),
+            pltpu.SemaphoreType.DMA((weight_scales.shape[0],)),
+        ],
         nbytes=4 << 20,
     )
     pieces = [sent[0]] + [swap_group(sent[s], ng, s) for s in range(1, ng)]
     weights, *pieces = lax.optimization_barrier((weights, *pieces))
     paired = halves == 2 and nb == 4
-    with_cot = (3,) if paired else ()
+    with_cot = ()
     *columns, cot = call(
         functools.partial(regroup_kernel, ng, nb, width, with_cot),
         [sds((rows, width + hidden * (p in with_cot)), BF16) for p in range(nb)] + [sds((rows, hidden), BF16)],
@@ -288,11 +303,13 @@
             nbytes=1 << 20,
         )
 
-    block_order = (0, 3, 1, 2) if paired else tuple(range(nb))
+    block_order = (0, 2, 1, 3) if paired else tuple(range(nb))
     if paired:
         cuts = [0, *(size * c for c in PAIRED_CUTS if size * c < hidden), hidden]
         chunks = list(zip(cuts[:-1], cuts[1:]))
-        away = [gate_up((1, 2), *chunk, BF16) for chunk in chunks]
+        away = [gate_up((1, 3), *chunk, BF16) for chunk in chunks]
+        held, away[0] = lax.optimization_barrier((cot, away[0]))
+        far_cot = swap_blk(held, nb, 2)
         features = call(
             functools.partial(features_kernel, halves),
             sds((nb * rows, depth), BF16),
@@ -300,18 +317,19 @@
             [VMEM] * (nb * halves),
             nbytes=3 << 20,
         )
-        kept = [gate_up((0, 3), *chunk, F32) for chunk in chunks]
+        kept = [gate_up((0, 2), *chunk, F32) for chunk in chunks]
         near = [swap_blk(a, nb, 1) for a in away]
         pair = [
             call(add_kernel, sds(k.shape, BF16), (k, n), [VMEM] * 2, nbytes=1 << 18)
             for k, n in zip(kept, near)
         ]
-        far = [swap_blk(p, nb, 3) for p in pair]
+        far_cot, pair[1] = lax.optimization_barrier((far_cot, pair[1]))
+        far = [swap_blk(p, nb, 2) for p in pair]
         own = [
             call(
                 functools.partial(pair_swiglu_kernel, at, size),
                 sds((2 * rows, 2 * (to - at)), BF16),
-                (kept[c], near[c], far[c], cot, x[3][0]),
+                (kept[c], near[c], far[c], cot, far_cot),
                 [VMEM] * 5,
                 nbytes=1 << 18,
             )

time: 46 us -> 44.4 us (0.965)
  starting transfers between devices: 22.6 us -> 20.5 us
  Pallas kernels: 8.2 us -> 9.53 us
  local copies, waits for them, and re-layouts: 0.91 us -> 0.1 us
    ppermute x12 -> x13, waiting for transfers between devices: 10.6 us -> 12.8 us  [swap_blk(): return lax.ppermute(x, 'blk', [(i, i ^ p) for i in range(size)])]
    ppermute x12 -> x13, starting transfers between devices: 17.4 us -> 15.3 us  [swap_blk(): return lax.ppermute(x, 'blk', [(i, i ^ p) for i in range(size)])]
    ppermute x3, waiting for transfers between devices: 2.67 us -> 1.14 us  [swap_group(): return lax.ppermute(x, 'group', [(i, i ^ s) for i in range(size)])]
    pallas_call x19, Pallas kernels: 8.2 us -> 9.53 us  [call(): pl.pallas_call(kernel, out_shape=out_shape, in_specs=in_specs, out_specs=...]
    unnamed x6 -> x2, local copies, waits for them, and re-layouts: 0.81 us -> 0.01 us
    ppermute x4, waiting for transfers between devices: 0.74 us -> 0.01 us  [swap_att(): return lax.ppermute(x, 'att', [(0, 1), (1, 0)])]
  transfers between devices with their start and end apart: 19 -> 20, of which waited for: 12 -> 11; matrix products, arithmetic and copies ran while one was open for 0% -> 0% of each run, Pallas kernels for 10% -> 14%
where the time goes in v5:
time: 44.4 us; the launch traced here: 44.3 us
  starting transfers between devices  20.5 us (46%)
  waiting for transfers between devices  14 us (32%)
  Pallas kernels  9.53 us (21%)
    ppermute x13, starting transfers between devices, swap_blk(): return lax.ppermute(x, 'blk', [(i, i ^ p) for i in range(size)])  15.3 us
    ppermute x13, waiting for transfers between devices, swap_blk(): return lax.ppermute(x, 'blk', [(i, i ^ p) for i in range(size)])  12.8 us
    pallas_call x19, Pallas kernels, call(): pl.pallas_call(kernel, out_shape=out_shape, in_specs=in_specs, out_specs=...  9.53 us
    ppermute x3, starting transfers between devices, swap_group(): return lax.ppermute(x, 'group', [(i, i ^ s) for i in range(size)])  4.61 us
    ppermute x3, waiting for transfers between devices, swap_group(): return lax.ppermute(x, 'group', [(i, i ^ s) for i in range(size)])  1.14 us
  transfers between devices with their start and end apart: 20, of which 11 were waited for; matrix products, arithmetic and copies ran while one was open for 0% of the time, Pallas kernels for 14%

profile of v5, /device:TPU:0, one launch (start us, length us, event | category | flops | bytes accessed | tf_op | source)
XLA Modules:
  0.0 44.3 jit_solution(7131700187280393307)
XLA Ops:
  0.0 1.9 %shard_map.55 = (bf16[16,2432]{1,0:T(8,128)(2,1)S(1)}, bf16[16,2432]{1,0:T(8,128)(2,1)S(1)}, bf16[16,2432]{1,0:T(8,128)(2,1)S(1)}, bf16[16,2432]{1,0:T(8,128)(2,1)S(1)}) custom-call(bf16[128,4096]{1,0:T(8,128)(2,1)} %tokens.1, s32[8,128]{1,0:T(8,128)} %bitcast.9, bf16[128,8,384]{2,1,0:T(8,128)(2,1)} %act.1), custom_call_target="tpu_custom_call" | custom-call | bytes 2097152 | tf_op jit(solution)/shard_map/pallas_call | solution.py:19
  1.9 4.0 %collective-permute-start = (bf16[16,2432]{1,0:T(8,128)(2,1)S(1)}, bf16[16,2432]{1,0:T(8,128)(2,1)S(1)}, u32[]{:S(2)}, u32[]{:S(2)}) collective-permute-start(bf16[16,2432]{1,0:T(8,128)(2,1)S(1)} %get-tuple-element.34), channel_id=1, source_target_pairs={{0,24},{8,16},{16,8},{24,0},{1,25},{9,17},{17,9},{25,1},{2,26},{10... | collective-permute-start | bytes 233480 | tf_op jit(solution)/shard_map/ppermute | solution.py:237
  5.9 0.5 %collective-permute-start.1 = (bf16[16,2432]{1,0:T(8,128)(2,1)S(1)}, bf16[16,2432]{1,0:T(8,128)(2,1)S(1)}, u32[]{:S(2)}, u32[]{:S(2)}) collective-permute-start(bf16[16,2432]{1,0:T(8,128)(2,1)S(1)} %get-tuple-element.35), channel_id=1, source_target_pairs={{0,16},{8,24},{16,0},{24,8},{1,17},{9,25},{17,1},{25,9},{2,18},{10... | collective-permute-start | bytes 233480 | tf_op jit(solution)/shard_map/ppermute | solution.py:237
  6.4 0.1 collective-permute-start.2
  6.5 0.1 copy.7.scales
  6.6 3.0 %shard_map.56.refs_4_ = bf16[1024,768]{1,0:T(8,128)(2,1)S(1)} custom-call(f32[8,2,3]{2,1,0:T(2,128)S(1)} %copy.7.scales, bf16[1024,2,384]{2,1,0:T(2,128)(2,1)} %bitcast.8), custom_call_target="tpu_custom_call" | custom-call | bytes 4194304 | tf_op jit(solution)/shard_map/pallas_call | solution.py:19
  9.7 0.0 collective-permute-done.refs_1_
  9.7 0.6 %collective-permute-done.1.refs_2_ = bf16[16,2432]{1,0:T(8,128)(2,1)S(1)} collective-permute-done((bf16[16,2432]{1,0:T(8,128)(2,1)S(1)}, bf16[16,2432]{1,0:T(8,128)(2,1)S(1)}, u32[]{:S(2)}, u32[]{:S(2)}) %collective-permute-start.1) | collective-permute-done | bytes 77856 | tf_op jit(solution)/shard_map/ppermute | solution.py:237
  10.3 0.5 %collective-permute-done.2.refs_3_ = bf16[16,2432]{1,0:T(8,128)(2,1)S(1)} collective-permute-done((bf16[16,2432]{1,0:T(8,128)(2,1)S(1)}, bf16[16,2432]{1,0:T(8,128)(2,1)S(1)}, u32[]{:S(2)}, u32[]{:S(2)}) %collective-permute-start.2) | collective-permute-done | bytes 77856 | tf_op jit(solution)/shard_map/ppermute | solution.py:237
  10.8 1.6 %collective-permute-start.6 = (bf16[64,512]{1,0:T(8,128)(2,1)S(1)}, bf16[64,512]{1,0:T(8,128)(2,1)S(1)}, u32[]{:S(2)}, u32[]{:S(2)}) collective-permute-start(bf16[64,512]{1,0:T(8,128)(2,1)S(1)} %get-tuple-element.45), channel_id=1, source_target_pairs={{0,2},{2,0},{4,6},{6,4},{1,3},{3,1},{5,7},{7,5},{8,10},{10,8},{12,... | collective-permute-start | bytes 196616 | tf_op jit(solution)/shard_map/ppermute | solution.py:241
  12.5 2.5 %collective-permute-start.8 = (bf16[64,512]{1,0:T(8,128)(2,1)S(1)}, bf16[64,512]{1,0:T(8,128)(2,1)S(1)}, u32[]{:S(2)}, u32[]{:S(2)}) collective-permute-start(bf16[64,512]{1,0:T(8,128)(2,1)S(1)} %get-tuple-element.46), channel_id=1, source_target_pairs={{0,6},{2,4},{4,2},{6,0},{1,7},{3,5},{5,3},{7,1},{8,14},{10,12},{12... | collective-permute-start | bytes 196616 | tf_op jit(solution)/shard_map/ppermute | solution.py:241
  14.9 0.1 collective-permute-start.4
  15.1 0.1 collective-permute-done.6.refs_0_.refs_4_
  15.2 3.4 %collective-permute-done.8.refs_2_.refs_6_ = bf16[64,512]{1,0:T(8,128)(2,1)S(1)} collective-permute-done((bf16[64,512]{1,0:T(8,128)(2,1)S(1)}, bf16[64,512]{1,0:T(8,128)(2,1)S(1)}, u32[]{:S(2)}, u32[]{:S(2)}) %collective-permute-start.8) | collective-permute-done | bytes 65568 | tf_op jit(solution)/shard_map/ppermute | solution.py:241
  18.6 0.5 %collective-permute-start.3 = (bf16[64,512]{1,0:T(8,128)(2,1)S(1)}, bf16[64,512]{1,0:T(8,128)(2,1)S(1)}, u32[]{:S(2)}, u32[]{:S(2)}) collective-permute-start(bf16[64,512]{1,0:T(8,128)(2,1)S(1)} %get-tuple-element.41.refs_0_), channel_id=1, source_target_pairs={{0,1},{1,0},{2,3},{3,2},{4,5},{5,4},{6,7},{7,6},{8,9},{9,8},{10,11... | collective-permute-start | bytes 196616 | tf_op jit(solution)/shard_map/ppermute | solution.py:245
  19.1 1.7 %collective-permute-done.4.refs_2_ = bf16[64,512]{1,0:T(8,128)(2,1)S(1)} collective-permute-done((bf16[64,512]{1,0:T(8,128)(2,1)S(1)}, bf16[64,512]{1,0:T(8,128)(2,1)S(1)}, u32[]{:S(2)}, u32[]{:S(2)}) %collective-permute-start.4) | collective-permute-done | bytes 65568 | tf_op jit(solution)/shard_map/ppermute | solution.py:241
  20.8 0.0 collective-permute-start.5
  20.8 0.3 shard_map.59
  21.1 0.2 collective-permute-start.10
  21.3 0.3 shard_map.62
  21.6 1.9 %collective-permute-start.13 = (bf16[128,256]{1,0:T(8,128)(2,1)S(1)}, bf16[128,256]{1,0:T(8,128)(2,1)S(1)}, u32[]{:S(2)}, u32[]{:S(2)}) collective-permute-start(bf16[128,256]{1,0:T(8,128)(2,1)S(1)} %shard_map.62), channel_id=1, source_target_pairs={{0,2},{2,0},{4,6},{6,4},{1,3},{3,1},{5,7},{7,5},{8,10},{10,8},{12,... | collective-permute-start | bytes 196616 | tf_op jit(solution)/shard_map/ppermute | solution.py:241
  23.6 0.3 shard_map.70
  23.9 0.2 collective-permute-start.17
  24.1 2.7 %collective-permute-start.12 = (bf16[64,384]{1,0:T(8,128)(2,1)S(1)}, bf16[64,384]{1,0:T(8,128)(2,1)S(1)}, u32[]{:S(2)}, u32[]{:S(2)}) collective-permute-start(bf16[64,384]{1,0:T(8,128)(2,1)S(1)} %get-tuple-element.48.cot), channel_id=1, source_target_pairs={{0,4},{2,6},{4,0},{6,2},{1,5},{3,7},{5,1},{7,3},{8,12},{10,14},{12... | collective-permute-start | bytes 147464 | tf_op jit(solution)/shard_map/ppermute | solution.py:241
  26.8 0.3 shard_map.69.kept
  27.1 0.3 shard_map.61.kept
  27.4 0.3 shard_map.58.kept
  27.7 0.0 collective-permute-done.10.arrived.near
  27.7 0.3 collective-permute-start.11
  28.1 1.3 %collective-permute-done.12.far_columns = bf16[64,384]{1,0:T(8,128)(2,1)S(1)} collective-permute-done((bf16[64,384]{1,0:T(8,128)(2,1)S(1)}, bf16[64,384]{1,0:T(8,128)(2,1)S(1)}, u32[]{:S(2)}, u32[]{:S(2)}) %collective-permute-start.12) | collective-permute-done | bytes 49184 | tf_op jit(solution)/shard_map/ppermute | solution.py:241
  29.3 3.1 %collective-permute-start.15 = (bf16[128,256]{1,0:T(8,128)(2,1)S(1)}, bf16[128,256]{1,0:T(8,128)(2,1)S(1)}, u32[]{:S(2)}, u32[]{:S(2)}) collective-permute-start(bf16[128,256]{1,0:T(8,128)(2,1)S(1)} %shard_map.63), channel_id=1, source_target_pairs={{0,4},{2,6},{4,0},{6,2},{1,5},{3,7},{5,1},{7,3},{8,12},{10,14},{12... | collective-permute-start | bytes 196616 | tf_op jit(solution)/shard_map/ppermute | solution.py:241
  32.4 0.0 collective-permute-done.17.arrived.near
  32.4 0.1 collective-permute-start.18
  32.5 3.4 %collective-permute-done.11.far = bf16[128,256]{1,0:T(8,128)(2,1)S(1)} collective-permute-done((bf16[128,256]{1,0:T(8,128)(2,1)S(1)}, bf16[128,256]{1,0:T(8,128)(2,1)S(1)}, u32[]{:S(2)}, u32[]{:S(2)}) %collective-permute-start.11) | collective-permute-done | bytes 65568 | tf_op jit(solution)/shard_map/ppermute | solution.py:241
  35.9 0.1 shard_map.64.refs_0_
  35.9 0.1 collective-permute-start.14
  36.0 1.6 %collective-permute-done.15.far = bf16[128,256]{1,0:T(8,128)(2,1)S(1)} collective-permute-done((bf16[128,256]{1,0:T(8,128)(2,1)S(1)}, bf16[128,256]{1,0:T(8,128)(2,1)S(1)}, u32[]{:S(2)}, u32[]{:S(2)}) %collective-permute-start.15) | collective-permute-done | bytes 65568 | tf_op jit(solution)/shard_map/ppermute | solution.py:241
  37.7 0.1 shard_map.67.refs_1_
  37.7 0.4 collective-permute-start.16
  38.2 0.2 collective-permute-done.18.far
  38.4 0.1 shard_map.72.refs_1_
  38.4 2.1 %collective-permute-start.19 = (bf16[128,256]{1,0:T(8,128)(2,1)S(1)}, bf16[128,256]{1,0:T(8,128)(2,1)S(1)}, u32[]{:S(2)}, u32[]{:S(2)}) collective-permute-start(bf16[128,256]{1,0:T(8,128)(2,1)S(1)} %shard_map.72.refs_1_), channel_id=1, source_target_pairs={{0,2},{2,0},{4,6},{6,4},{1,3},{3,1},{5,7},{7,5},{8,10},{10,8},{12,... | collective-permute-start | bytes 196616 | tf_op jit(solution)/shard_map/ppermute | solution.py:241
  40.6 0.0 collective-permute-done.14.refs_1_
  40.6 0.6 %shard_map.66.refs_0_ = bf16[1024,2,384]{2,1,0:T(2,128)(2,1)S(1)} custom-call(bf16[128,256]{1,0:T(8,128)(2,1)S(1)} %shard_map.64.refs_0_, bf16[128,256]{1,0:T(8,128)(2,1)S(1)} %collective-permute-done.14.refs_1_, bf16[256,1024]{1,0:T(8,128)(2,1)S(1)} %shard_map.65.refs_2_.refs_3_), custom_call_target="tpu_custom_call" | custom-call | bytes 1048576 | tf_op jit(solution)/shard_map/pallas_call | solution.py:19
  41.2 0.9 %collective-permute-done.16.refs_2_ = bf16[128,256]{1,0:T(8,128)(2,1)S(1)} collective-permute-done((bf16[128,256]{1,0:T(8,128)(2,1)S(1)}, bf16[128,256]{1,0:T(8,128)(2,1)S(1)}, u32[]{:S(2)}, u32[]{:S(2)}) %collective-permute-start.16) | collective-permute-done | bytes 65568 | tf_op jit(solution)/shard_map/ppermute | solution.py:241
  42.1 0.6 %shard_map.68.refs_0_ = bf16[1024,2,384]{2,1,0:T(2,128)(2,1)S(1)} custom-call(bf16[1024,2,384]{2,1,0:T(2,128)(2,1)S(1)} %shard_map.66.refs_0_, bf16[128,256]{1,0:T(8,128)(2,1)S(1)} %shard_map.67.refs_1_, bf16[128,256]{1,0:T(8,128)(2,1)S(1)} %collective-permute-done.16.refs_2_, ...), custom_call_target="tpu_custom_call", output_to_operand_aliasing={{}: (0, {})} | custom-call | bytes 1048576 | tf_op jit(solution)/shard_map/pallas_call | solution.py:19
  42.6 0.2 collective-permute-done.19.refs_2_
  42.8 1.5 %shard_map.73 = bf16[1024,2,384]{2,1,0:T(2,128)(2,1)} custom-call(bf16[1024,2,384]{2,1,0:T(2,128)(2,1)S(1)} %shard_map.68.refs_0_, bf16[128,256]{1,0:T(8,128)(2,1)S(1)} %shard_map.72.refs_1_, bf16[128,256]{1,0:T(8,128)(2,1)S(1)} %collective-permute-done.19.refs_2_, bf16[256,1024]{1,0:T(8,128)(2,1)S(1)} %shard_map.65.refs_2_.refs_3_), custom_call_target="tpu_custom_call" | custom-call | bytes 4194304 | tf_op jit(solution)/shard_map/pallas_call | solution.py:19
  (15 shorter events, 0.1 us)
Async XLA Ops:
  0.0 6.5 %copy-start = (bf16[8,1,2,3]{0,2,3,1:T(2,128)(2,1)S(1)}, bf16[8,1,2,3]{0,2,3,1:T(2,128)(2,1)}, u32[]{:S(2)}) copy-start(bf16[8,1,2,3]{0,2,3,1:T(2,128)(2,1)} %param.9) | copy-start | bytes 292
  1.9 7.7 %collective-permute-start = (bf16[16,2432]{1,0:T(8,128)(2,1)S(1)}, bf16[16,2432]{1,0:T(8,128)(2,1)S(1)}, u32[]{:S(2)}, u32[]{:S(2)}) collective-permute-start(bf16[16,2432]{1,0:T(8,128)(2,1)S(1)} %get-tuple-element.34), channel_id=1, source_target_pairs={{0,24},{8,16},{16,8},{24,0},{1,25},{9,17},{17,9},{25,1},{2,26},{10... | collective-permute-start | bytes 233480 | tf_op jit(solution)/shard_map/ppermute | solution.py:237
  5.9 4.4 %collective-permute-start.1 = (bf16[16,2432]{1,0:T(8,128)(2,1)S(1)}, bf16[16,2432]{1,0:T(8,128)(2,1)S(1)}, u32[]{:S(2)}, u32[]{:S(2)}) collective-permute-start(bf16[16,2432]{1,0:T(8,128)(2,1)S(1)} %get-tuple-element.35), channel_id=1, source_target_pairs={{0,16},{8,24},{16,0},{24,8},{1,17},{9,25},{17,1},{25,9},{2,18},{10... | collective-permute-start | bytes 233480 | tf_op jit(solution)/shard_map/ppermute | solution.py:237
  6.4 4.4 %collective-permute-start.2 = (bf16[16,2432]{1,0:T(8,128)(2,1)S(1)}, bf16[16,2432]{1,0:T(8,128)(2,1)S(1)}, u32[]{:S(2)}, u32[]{:S(2)}) collective-permute-start(bf16[16,2432]{1,0:T(8,128)(2,1)S(1)} %get-tuple-element.36), channel_id=1, source_target_pairs={{0,8},{8,0},{16,24},{24,16},{1,9},{9,1},{17,25},{25,17},{2,10},{10... | collective-permute-start | bytes 233480 | tf_op jit(solution)/shard_map/ppermute | solution.py:237
  10.8 4.3 %collective-permute-start.6 = (bf16[64,512]{1,0:T(8,128)(2,1)S(1)}, bf16[64,512]{1,0:T(8,128)(2,1)S(1)}, u32[]{:S(2)}, u32[]{:S(2)}) collective-permute-start(bf16[64,512]{1,0:T(8,128)(2,1)S(1)} %get-tuple-element.45), channel_id=1, source_target_pairs={{0,2},{2,0},{4,6},{6,4},{1,3},{3,1},{5,7},{7,5},{8,10},{10,8},{12,... | collective-permute-start | bytes 196616 | tf_op jit(solution)/shard_map/ppermute | solution.py:241
  12.5 6.1 %collective-permute-start.8 = (bf16[64,512]{1,0:T(8,128)(2,1)S(1)}, bf16[64,512]{1,0:T(8,128)(2,1)S(1)}, u32[]{:S(2)}, u32[]{:S(2)}) collective-permute-start(bf16[64,512]{1,0:T(8,128)(2,1)S(1)} %get-tuple-element.46), channel_id=1, source_target_pairs={{0,6},{2,4},{4,2},{6,0},{1,7},{3,5},{5,3},{7,1},{8,14},{10,12},{12... | collective-permute-start | bytes 196616 | tf_op jit(solution)/shard_map/ppermute | solution.py:241
  14.9 5.9 %collective-permute-start.4 = (bf16[64,512]{1,0:T(8,128)(2,1)S(1)}, bf16[64,512]{1,0:T(8,128)(2,1)S(1)}, u32[]{:S(2)}, u32[]{:S(2)}) collective-permute-start(bf16[64,512]{1,0:T(8,128)(2,1)S(1)} %get-tuple-element.42), channel_id=1, source_target_pairs={{0,4},{2,6},{4,0},{6,2},{1,5},{3,7},{5,1},{7,3},{8,12},{10,14},{12... | collective-permute-start | bytes 196616 | tf_op jit(solution)/shard_map/ppermute | solution.py:241
  15.2 5.7 %collective-permute-start.7 = (bf16[64,512]{1,0:T(8,128)(2,1)S(1)}, bf16[64,512]{1,0:T(8,128)(2,1)S(1)}, u32[]{:S(2)}, u32[]{:S(2)}) collective-permute-start(bf16[64,512]{1,0:T(8,128)(2,1)S(1)} %collective-permute-done.6.refs_0_.refs_4_), channel_id=1, source_target_pairs={{0,1},{1,0},{2,3},{3,2},{4,5},{5,4},{6,7},{7,6},{8,9},{9,8},{10,11... | collective-permute-start | bytes 196616 | tf_op jit(solution)/shard_map/ppermute | solution.py:245
  18.6 2.2 %collective-permute-start.9 = (bf16[64,512]{1,0:T(8,128)(2,1)S(1)}, bf16[64,512]{1,0:T(8,128)(2,1)S(1)}, u32[]{:S(2)}, u32[]{:S(2)}) collective-permute-start(bf16[64,512]{1,0:T(8,128)(2,1)S(1)} %collective-permute-done.8.refs_2_.refs_6_), channel_id=1, source_target_pairs={{0,1},{1,0},{2,3},{3,2},{4,5},{5,4},{6,7},{7,6},{8,9},{9,8},{10,11... | collective-permute-start | bytes 196616 | tf_op jit(solution)/shard_map/ppermute | solution.py:245
  18.6 5.5 %collective-permute-start.3 = (bf16[64,512]{1,0:T(8,128)(2,1)S(1)}, bf16[64,512]{1,0:T(8,128)(2,1)S(1)}, u32[]{:S(2)}, u32[]{:S(2)}) collective-permute-start(bf16[64,512]{1,0:T(8,128)(2,1)S(1)} %get-tuple-element.41.refs_0_), channel_id=1, source_target_pairs={{0,1},{1,0},{2,3},{3,2},{4,5},{5,4},{6,7},{7,6},{8,9},{9,8},{10,11... | collective-permute-start | bytes 196616 | tf_op jit(solution)/shard_map/ppermute | solution.py:245
  20.8 6.0 %collective-permute-start.5 = (bf16[64,512]{1,0:T(8,128)(2,1)S(1)}, bf16[64,512]{1,0:T(8,128)(2,1)S(1)}, u32[]{:S(2)}, u32[]{:S(2)}) collective-permute-start(bf16[64,512]{1,0:T(8,128)(2,1)S(1)} %collective-permute-done.4.refs_2_), channel_id=1, source_target_pairs={{0,1},{1,0},{2,3},{3,2},{4,5},{5,4},{6,7},{7,6},{8,9},{9,8},{10,11... | collective-permute-start | bytes 196616 | tf_op jit(solution)/shard_map/ppermute | solution.py:245
  21.1 6.5 %collective-permute-start.10 = (bf16[128,256]{1,0:T(8,128)(2,1)S(1)}, bf16[128,256]{1,0:T(8,128)(2,1)S(1)}, u32[]{:S(2)}, u32[]{:S(2)}) collective-permute-start(bf16[128,256]{1,0:T(8,128)(2,1)S(1)} %shard_map.59), channel_id=1, source_target_pairs={{0,2},{2,0},{4,6},{6,4},{1,3},{3,1},{5,7},{7,5},{8,10},{10,8},{12,... | collective-permute-start | bytes 196616 | tf_op jit(solution)/shard_map/ppermute | solution.py:241
  21.6 6.4 %collective-permute-start.13 = (bf16[128,256]{1,0:T(8,128)(2,1)S(1)}, bf16[128,256]{1,0:T(8,128)(2,1)S(1)}, u32[]{:S(2)}, u32[]{:S(2)}) collective-permute-start(bf16[128,256]{1,0:T(8,128)(2,1)S(1)} %shard_map.62), channel_id=1, source_target_pairs={{0,2},{2,0},{4,6},{6,4},{1,3},{3,1},{5,7},{7,5},{8,10},{10,8},{12,... | collective-permute-start | bytes 196616 | tf_op jit(solution)/shard_map/ppermute | solution.py:241
  23.9 8.5 %collective-permute-start.17 = (bf16[128,256]{1,0:T(8,128)(2,1)S(1)}, bf16[128,256]{1,0:T(8,128)(2,1)S(1)}, u32[]{:S(2)}, u32[]{:S(2)}) collective-permute-start(bf16[128,256]{1,0:T(8,128)(2,1)S(1)} %shard_map.70), channel_id=1, source_target_pairs={{0,2},{2,0},{4,6},{6,4},{1,3},{3,1},{5,7},{7,5},{8,10},{10,8},{12,... | collective-permute-start | bytes 196616 | tf_op jit(solution)/shard_map/ppermute | solution.py:241
  24.1 5.2 %collective-permute-start.12 = (bf16[64,384]{1,0:T(8,128)(2,1)S(1)}, bf16[64,384]{1,0:T(8,128)(2,1)S(1)}, u32[]{:S(2)}, u32[]{:S(2)}) collective-permute-start(bf16[64,384]{1,0:T(8,128)(2,1)S(1)} %get-tuple-element.48.cot), channel_id=1, source_target_pairs={{0,4},{2,6},{4,0},{6,2},{1,5},{3,7},{5,1},{7,3},{8,12},{10,14},{12... | collective-permute-start | bytes 147464 | tf_op jit(solution)/shard_map/ppermute | solution.py:241
  27.7 8.2 %collective-permute-start.11 = (bf16[128,256]{1,0:T(8,128)(2,1)S(1)}, bf16[128,256]{1,0:T(8,128)(2,1)S(1)}, u32[]{:S(2)}, u32[]{:S(2)}) collective-permute-start(bf16[128,256]{1,0:T(8,128)(2,1)S(1)} %shard_map.60), channel_id=1, source_target_pairs={{0,4},{2,6},{4,0},{6,2},{1,5},{3,7},{5,1},{7,3},{8,12},{10,14},{12... | collective-permute-start | bytes 196616 | tf_op jit(solution)/shard_map/ppermute | solution.py:241
  29.3 8.3 %collective-permute-start.15 = (bf16[128,256]{1,0:T(8,128)(2,1)S(1)}, bf16[128,256]{1,0:T(8,128)(2,1)S(1)}, u32[]{:S(2)}, u32[]{:S(2)}) collective-permute-start(bf16[128,256]{1,0:T(8,128)(2,1)S(1)} %shard_map.63), channel_id=1, source_target_pairs={{0,4},{2,6},{4,0},{6,2},{1,5},{3,7},{5,1},{7,3},{8,12},{10,14},{12... | collective-permute-start | bytes 196616 | tf_op jit(solution)/shard_map/ppermute | solution.py:241
  32.4 6.0 %collective-permute-start.18 = (bf16[128,256]{1,0:T(8,128)(2,1)S(1)}, bf16[128,256]{1,0:T(8,128)(2,1)S(1)}, u32[]{:S(2)}, u32[]{:S(2)}) collective-permute-start(bf16[128,256]{1,0:T(8,128)(2,1)S(1)} %shard_map.71), channel_id=1, source_target_pairs={{0,4},{2,6},{4,0},{6,2},{1,5},{3,7},{5,1},{7,3},{8,12},{10,14},{12... | collective-permute-start | bytes 196616 | tf_op jit(solution)/shard_map/ppermute | solution.py:241
  35.9 4.7 %collective-permute-start.14 = (bf16[128,256]{1,0:T(8,128)(2,1)S(1)}, bf16[128,256]{1,0:T(8,128)(2,1)S(1)}, u32[]{:S(2)}, u32[]{:S(2)}) collective-permute-start(bf16[128,256]{1,0:T(8,128)(2,1)S(1)} %shard_map.64.refs_0_), channel_id=1, source_target_pairs={{0,2},{2,0},{4,6},{6,4},{1,3},{3,1},{5,7},{7,5},{8,10},{10,8},{12,... | collective-permute-start | bytes 196616 | tf_op jit(solution)/shard_map/ppermute | solution.py:241
  37.7 4.3 %collective-permute-start.16 = (bf16[128,256]{1,0:T(8,128)(2,1)S(1)}, bf16[128,256]{1,0:T(8,128)(2,1)S(1)}, u32[]{:S(2)}, u32[]{:S(2)}) collective-permute-start(bf16[128,256]{1,0:T(8,128)(2,1)S(1)} %shard_map.67.refs_1_), channel_id=1, source_target_pairs={{0,2},{2,0},{4,6},{6,4},{1,3},{3,1},{5,7},{7,5},{8,10},{10,8},{12,... | collective-permute-start | bytes 196616 | tf_op jit(solution)/shard_map/ppermute | solution.py:241
  38.4 4.4 %collective-permute-start.19 = (bf16[128,256]{1,0:T(8,128)(2,1)S(1)}, bf16[128,256]{1,0:T(8,128)(2,1)S(1)}, u32[]{:S(2)}, u32[]{:S(2)}) collective-permute-start(bf16[128,256]{1,0:T(8,128)(2,1)S(1)} %shard_map.72.refs_1_), channel_id=1, source_target_pairs={{0,2},{2,0},{4,6},{6,4},{1,3},{3,1},{5,7},{7,5},{8,10},{10,8},{12,... | collective-permute-start | bytes 196616 | tf_op jit(solution)/shard_map/ppermute | solution.py:241

commit v6 on v5

--- a/solution.py
+++ b/solution.py
@@ -11,7 +11,6 @@
 BF16 = jnp.bfloat16
 F32 = jnp.float32
 VMEM_BYTES = 40 * 1024 * 1024
-PAIRED_CUTS = (1, 2)
 
 
 def call(kernel, out_shape, args, in_specs, out_specs=None, scratch=(), flops=0, nbytes=0, aliases=None):
@@ -97,46 +96,44 @@
         outs[s][:, nb * width :] = cot[s * CAP : (s + 1) * CAP]
 
 
-def regroup_kernel(ng, nb, width, with_cot, *refs):
+def regroup_kernel(ng, nb, width, *refs):
     pieces, outs = refs[:ng], refs[ng:]
     for s in range(ng):
         at = slice(s * CAP, (s + 1) * CAP)
-        cot = pieces[s][:, nb * width :]
         for p in range(nb):
-            outs[p][at, :width] = pieces[s][:, p * width : (p + 1) * width]
-            if p in with_cot:
-                outs[p][at, width:] = cot
-        outs[nb][at, :] = cot
+            outs[p][at, :] = pieces[s][:, p * width : (p + 1) * width]
+        outs[nb][at, :] = pieces[s][:, nb * width :]
 
 
 def weights_kernel(halves, scales, codes_hbm, out, codes, sem):
     depth, _, hidden = codes.shape
     blocks, _, cols = scales.shape
     qrows, qcols = depth // blocks, hidden // cols
-    copies = [
-        pltpu.make_async_copy(codes_hbm.at[at], codes.at[at], sem.at[q])
-        for q, at in enumerate(pl.ds(q * qrows, qrows) for q in range(blocks))
-    ]
-    for copy in copies:
-        copy.start()
     half = own_half(halves)
     per_half = blocks // halves
+    copies = []
+    for h in range(halves):
+        at = pl.ds(pl.multiple_of((half ^ h) * (depth // halves), depth // halves), depth // halves)
+        to = slice(h * (depth // halves), (h + 1) * (depth // halves))
+        copies.append(pltpu.make_async_copy(codes_hbm.at[at], codes.at[to], sem.at[h]))
+        copies[-1].start()
     pick = [
         (iota((qrows, 2 * qrows), 1) == 2 * iota((qrows, 2 * qrows), 0) + j).astype(F32).astype(BF16)
         for j in range(2)
     ]
-    for copy in copies:
-        copy.wait()
-    for q in range(blocks):
-        source = (q + half * per_half) % blocks if halves > 1 else q
-        rows = codes[pl.ds(pl.multiple_of(source * qrows, qrows), qrows)].reshape(2 * qrows, hidden)
-        for j in range(2):
-            values = dot(pick[j], rows)
-            for c in range(cols):
-                at = (2 * c + j) * qcols
-                out[q * qrows : (q + 1) * qrows, at : at + qcols] = (
-                    values[:, c * qcols : (c + 1) * qcols] * scales[source, j, c]
-                ).astype(BF16)
+    for h in range(halves):
+        copies[h].wait()
+        for k in range(per_half):
+            q, source = h * per_half + k, (half ^ h) * per_half + k
+            to = slice(q * qrows, (q + 1) * qrows)
+            rows = codes[to].reshape(2 * qrows, hidden)
+            for j in range(2):
+                values = dot(pick[j], rows)
+                for c in range(cols):
+                    at = (2 * c + j) * qcols
+                    out[to, at : at + qcols] = (
+                        values[:, c * qcols : (c + 1) * qcols] * scales[source, j, c]
+                    ).astype(BF16)
 
 
 def gate_up_kernel(halves, at, *refs):
@@ -173,15 +170,14 @@
     out[:, size:] = (c * gate * s).astype(BF16)
 
 
-def pair_swiglu_kernel(at, size, kept, near, far, cot, far_columns, out):
-    rows, hidden = cot.shape
+def pair_swiglu_kernel(at, size, kept, near, far, cot, far_cot, out):
+    rows = cot.shape[0]
     total = kept[...] + near[...].astype(F32)
     total += jnp.concatenate([far[rows:, :], far[:rows, :]], axis=0).astype(F32)
-    skip = far_columns.shape[1] - hidden
     for c in range(out.shape[1] // (2 * size)):
         cols = slice(2 * c * size, 2 * (c + 1) * size)
         h = at + c * size
-        cots = [cot[:, h : h + size], far_columns[:, skip + h : skip + h + size]]
+        cots = [cot[:, h : h + size], far_cot[:, h : h + size]]
         swiglu(total[:, cols], jnp.concatenate(cots, axis=0), out.at[:, cols])
 
 
@@ -281,10 +277,9 @@
     pieces = [sent[0]] + [swap_group(sent[s], ng, s) for s in range(1, ng)]
     weights, *pieces = lax.optimization_barrier((weights, *pieces))
     paired = halves == 2 and nb == 4
-    with_cot = ()
     *columns, cot = call(
-        functools.partial(regroup_kernel, ng, nb, width, with_cot),
-        [sds((rows, width + hidden * (p in with_cot)), BF16) for p in range(nb)] + [sds((rows, hidden), BF16)],
+        functools.partial(regroup_kernel, ng, nb, width),
+        [sds((rows, width), BF16)] * nb + [sds((rows, hidden), BF16)],
         pieces,
         [VMEM] * ng,
         nbytes=1 << 20,
@@ -305,8 +300,7 @@
 
     block_order = (0, 2, 1, 3) if paired else tuple(range(nb))
     if paired:
-        cuts = [0, *(size * c for c in PAIRED_CUTS if size * c < hidden), hidden]
-        chunks = list(zip(cuts[:-1], cuts[1:]))
+        chunks = [(at, at + size) for at in range(0, hidden, size)]
         away = [gate_up((1, 3), *chunk, BF16) for chunk in chunks]
         held, away[0] = lax.optimization_barrier((cot, away[0]))
         far_cot = swap_blk(held, nb, 2)
@@ -323,7 +317,7 @@
             call(add_kernel, sds(k.shape, BF16), (k, n), [VMEM] * 2, nbytes=1 << 18)
             for k, n in zip(kept, near)
         ]
-        far_cot, pair[1] = lax.optimization_barrier((far_cot, pair[1]))
+        far_cot, pair[1 % len(pair)] = lax.optimization_barrier((far_cot, pair[1 % len(pair)]))
         far = [swap_blk(p, nb, 2) for p in pair]
         own = [
             call(

time: 44.4 us -> 44.4 us (level)
  transfers between devices with their start and end apart: 20 -> 20, of which waited for: 11 -> 11; matrix products, arithmetic and copies ran while one was open for 0% -> 0% of each run, Pallas kernels for 14% -> 13%
where the time goes in v6:
time: 44.4 us; the launch traced here: 44.3 us
  starting transfers between devices  20.5 us (46%)
  waiting for transfers between devices  14.2 us (32%)
  Pallas kernels  9.36 us (21%)
    ppermute x13, starting transfers between devices, swap_blk(): return lax.ppermute(x, 'blk', [(i, i ^ p) for i in range(size)])  15.3 us
    ppermute x13, waiting for transfers between devices, swap_blk(): return lax.ppermute(x, 'blk', [(i, i ^ p) for i in range(size)])  12.8 us
    pallas_call x19, Pallas kernels, call(): pl.pallas_call(kernel, out_shape=out_shape, in_specs=in_specs, out_specs=...  9.36 us
    ppermute x3, starting transfers between devices, swap_group(): return lax.ppermute(x, 'group', [(i, i ^ s) for i in range(size)])  4.61 us
    ppermute x3, waiting for transfers between devices, swap_group(): return lax.ppermute(x, 'group', [(i, i ^ s) for i in range(size)])  1.31 us
  transfers between devices with their start and end apart: 20, of which 11 were waited for; matrix products, arithmetic and copies ran while one was open for 0% of the time, Pallas kernels for 13%

profile of v6, /device:TPU:0, one launch (start us, length us, event | category | flops | bytes accessed | tf_op | source)
XLA Modules:
  0.0 44.3 jit_solution(3824325425942937690)
XLA Ops:
  0.0 1.9 %shard_map.55 = (bf16[16,2432]{1,0:T(8,128)(2,1)S(1)}, bf16[16,2432]{1,0:T(8,128)(2,1)S(1)}, bf16[16,2432]{1,0:T(8,128)(2,1)S(1)}, bf16[16,2432]{1,0:T(8,128)(2,1)S(1)}) custom-call(bf16[128,4096]{1,0:T(8,128)(2,1)} %tokens.1, s32[8,128]{1,0:T(8,128)} %bitcast.9, bf16[128,8,384]{2,1,0:T(8,128)(2,1)} %act.1), custom_call_target="tpu_custom_call" | custom-call | bytes 2097152 | tf_op jit(solution)/shard_map/pallas_call | solution.py:18
  1.9 4.0 %collective-permute-start = (bf16[16,2432]{1,0:T(8,128)(2,1)S(1)}, bf16[16,2432]{1,0:T(8,128)(2,1)S(1)}, u32[]{:S(2)}, u32[]{:S(2)}) collective-permute-start(bf16[16,2432]{1,0:T(8,128)(2,1)S(1)} %get-tuple-element.34), channel_id=1, source_target_pairs={{0,24},{8,16},{16,8},{24,0},{1,25},{9,17},{17,9},{25,1},{2,26},{10... | collective-permute-start | bytes 233480 | tf_op jit(solution)/shard_map/ppermute | solution.py:233
  5.9 0.5 %collective-permute-start.1 = (bf16[16,2432]{1,0:T(8,128)(2,1)S(1)}, bf16[16,2432]{1,0:T(8,128)(2,1)S(1)}, u32[]{:S(2)}, u32[]{:S(2)}) collective-permute-start(bf16[16,2432]{1,0:T(8,128)(2,1)S(1)} %get-tuple-element.35), channel_id=1, source_target_pairs={{0,16},{8,24},{16,0},{24,8},{1,17},{9,25},{17,1},{25,9},{2,18},{10... | collective-permute-start | bytes 233480 | tf_op jit(solution)/shard_map/ppermute | solution.py:233
  6.4 0.1 collective-permute-start.2
  6.5 0.1 copy.7.scales
  6.6 2.8 %shard_map.56.refs_4_ = bf16[1024,768]{1,0:T(8,128)(2,1)S(1)} custom-call(f32[8,2,3]{2,1,0:T(2,128)S(1)} %copy.7.scales, bf16[1024,2,384]{2,1,0:T(2,128)(2,1)} %bitcast.8), custom_call_target="tpu_custom_call" | custom-call | bytes 4194304 | tf_op jit(solution)/shard_map/pallas_call | solution.py:18
  9.5 0.0 collective-permute-done.refs_1_
  9.5 0.8 %collective-permute-done.1.refs_2_ = bf16[16,2432]{1,0:T(8,128)(2,1)S(1)} collective-permute-done((bf16[16,2432]{1,0:T(8,128)(2,1)S(1)}, bf16[16,2432]{1,0:T(8,128)(2,1)S(1)}, u32[]{:S(2)}, u32[]{:S(2)}) %collective-permute-start.1) | collective-permute-done | bytes 77856 | tf_op jit(solution)/shard_map/ppermute | solution.py:233
  10.3 0.5 %collective-permute-done.2.refs_3_ = bf16[16,2432]{1,0:T(8,128)(2,1)S(1)} collective-permute-done((bf16[16,2432]{1,0:T(8,128)(2,1)S(1)}, bf16[16,2432]{1,0:T(8,128)(2,1)S(1)}, u32[]{:S(2)}, u32[]{:S(2)}) %collective-permute-start.2) | collective-permute-done | bytes 77856 | tf_op jit(solution)/shard_map/ppermute | solution.py:233
  10.8 1.6 %collective-permute-start.6 = (bf16[64,512]{1,0:T(8,128)(2,1)S(1)}, bf16[64,512]{1,0:T(8,128)(2,1)S(1)}, u32[]{:S(2)}, u32[]{:S(2)}) collective-permute-start(bf16[64,512]{1,0:T(8,128)(2,1)S(1)} %get-tuple-element.45), channel_id=1, source_target_pairs={{0,2},{2,0},{4,6},{6,4},{1,3},{3,1},{5,7},{7,5},{8,10},{10,8},{12,... | collective-permute-start | bytes 196616 | tf_op jit(solution)/shard_map/ppermute | solution.py:237
  12.5 2.5 %collective-permute-start.8 = (bf16[64,512]{1,0:T(8,128)(2,1)S(1)}, bf16[64,512]{1,0:T(8,128)(2,1)S(1)}, u32[]{:S(2)}, u32[]{:S(2)}) collective-permute-start(bf16[64,512]{1,0:T(8,128)(2,1)S(1)} %get-tuple-element.46), channel_id=1, source_target_pairs={{0,6},{2,4},{4,2},{6,0},{1,7},{3,5},{5,3},{7,1},{8,14},{10,12},{12... | collective-permute-start | bytes 196616 | tf_op jit(solution)/shard_map/ppermute | solution.py:237
  14.9 0.1 collective-permute-start.4
  15.1 0.1 collective-permute-done.6.refs_0_.refs_4_
  15.2 3.4 %collective-permute-done.8.refs_2_.refs_6_ = bf16[64,512]{1,0:T(8,128)(2,1)S(1)} collective-permute-done((bf16[64,512]{1,0:T(8,128)(2,1)S(1)}, bf16[64,512]{1,0:T(8,128)(2,1)S(1)}, u32[]{:S(2)}, u32[]{:S(2)}) %collective-permute-start.8) | collective-permute-done | bytes 65568 | tf_op jit(solution)/shard_map/ppermute | solution.py:237
  18.6 0.5 %collective-permute-start.3 = (bf16[64,512]{1,0:T(8,128)(2,1)S(1)}, bf16[64,512]{1,0:T(8,128)(2,1)S(1)}, u32[]{:S(2)}, u32[]{:S(2)}) collective-permute-start(bf16[64,512]{1,0:T(8,128)(2,1)S(1)} %get-tuple-element.41.refs_0_), channel_id=1, source_target_pairs={{0,1},{1,0},{2,3},{3,2},{4,5},{5,4},{6,7},{7,6},{8,9},{9,8},{10,11... | collective-permute-start | bytes 196616 | tf_op jit(solution)/shard_map/ppermute | solution.py:241
  19.1 1.7 %collective-permute-done.4.refs_2_ = bf16[64,512]{1,0:T(8,128)(2,1)S(1)} collective-permute-done((bf16[64,512]{1,0:T(8,128)(2,1)S(1)}, bf16[64,512]{1,0:T(8,128)(2,1)S(1)}, u32[]{:S(2)}, u32[]{:S(2)}) %collective-permute-start.4) | collective-permute-done | bytes 65568 | tf_op jit(solution)/shard_map/ppermute | solution.py:237
  20.8 0.0 collective-permute-start.5
  20.8 0.3 shard_map.59
  21.1 0.2 collective-permute-start.10
  21.3 0.3 shard_map.62
  21.6 1.9 %collective-permute-start.13 = (bf16[128,256]{1,0:T(8,128)(2,1)S(1)}, bf16[128,256]{1,0:T(8,128)(2,1)S(1)}, u32[]{:S(2)}, u32[]{:S(2)}) collective-permute-start(bf16[128,256]{1,0:T(8,128)(2,1)S(1)} %shard_map.62), channel_id=1, source_target_pairs={{0,2},{2,0},{4,6},{6,4},{1,3},{3,1},{5,7},{7,5},{8,10},{10,8},{12,... | collective-permute-start | bytes 196616 | tf_op jit(solution)/shard_map/ppermute | solution.py:237
  23.6 0.3 shard_map.70
  23.9 0.2 collective-permute-start.17
  24.1 2.7 %collective-permute-start.12 = (bf16[64,384]{1,0:T(8,128)(2,1)S(1)}, bf16[64,384]{1,0:T(8,128)(2,1)S(1)}, u32[]{:S(2)}, u32[]{:S(2)}) collective-permute-start(bf16[64,384]{1,0:T(8,128)(2,1)S(1)} %get-tuple-element.48.cot), channel_id=1, source_target_pairs={{0,4},{2,6},{4,0},{6,2},{1,5},{3,7},{5,1},{7,3},{8,12},{10,14},{12... | collective-permute-start | bytes 147464 | tf_op jit(solution)/shard_map/ppermute | solution.py:237
  26.8 0.3 shard_map.69.kept
  27.1 0.3 shard_map.61.kept
  27.4 0.3 shard_map.58.kept
  27.7 0.0 collective-permute-done.10.arrived.near
  27.7 0.3 collective-permute-start.11
  28.1 1.3 %collective-permute-done.12.far_cot = bf16[64,384]{1,0:T(8,128)(2,1)S(1)} collective-permute-done((bf16[64,384]{1,0:T(8,128)(2,1)S(1)}, bf16[64,384]{1,0:T(8,128)(2,1)S(1)}, u32[]{:S(2)}, u32[]{:S(2)}) %collective-permute-start.12) | collective-permute-done | bytes 49184 | tf_op jit(solution)/shard_map/ppermute | solution.py:237
  29.3 3.1 %collective-permute-start.15 = (bf16[128,256]{1,0:T(8,128)(2,1)S(1)}, bf16[128,256]{1,0:T(8,128)(2,1)S(1)}, u32[]{:S(2)}, u32[]{:S(2)}) collective-permute-start(bf16[128,256]{1,0:T(8,128)(2,1)S(1)} %shard_map.63), channel_id=1, source_target_pairs={{0,4},{2,6},{4,0},{6,2},{1,5},{3,7},{5,1},{7,3},{8,12},{10,14},{12... | collective-permute-start | bytes 196616 | tf_op jit(solution)/shard_map/ppermute | solution.py:237
  32.4 0.0 collective-permute-done.17.arrived.near
  32.4 0.1 collective-permute-start.18
  32.5 3.4 %collective-permute-done.11.far = bf16[128,256]{1,0:T(8,128)(2,1)S(1)} collective-permute-done((bf16[128,256]{1,0:T(8,128)(2,1)S(1)}, bf16[128,256]{1,0:T(8,128)(2,1)S(1)}, u32[]{:S(2)}, u32[]{:S(2)}) %collective-permute-start.11) | collective-permute-done | bytes 65568 | tf_op jit(solution)/shard_map/ppermute | solution.py:237
  35.9 0.1 shard_map.64.refs_0_
  35.9 0.1 collective-permute-start.14
  36.0 1.6 %collective-permute-done.15.far = bf16[128,256]{1,0:T(8,128)(2,1)S(1)} collective-permute-done((bf16[128,256]{1,0:T(8,128)(2,1)S(1)}, bf16[128,256]{1,0:T(8,128)(2,1)S(1)}, u32[]{:S(2)}, u32[]{:S(2)}) %collective-permute-start.15) | collective-permute-done | bytes 65568 | tf_op jit(solution)/shard_map/ppermute | solution.py:237
  37.7 0.1 shard_map.67.refs_1_
  37.7 0.4 collective-permute-start.16
  38.2 0.2 collective-permute-done.18.far
  38.4 0.1 shard_map.72.refs_1_
  38.4 2.1 %collective-permute-start.19 = (bf16[128,256]{1,0:T(8,128)(2,1)S(1)}, bf16[128,256]{1,0:T(8,128)(2,1)S(1)}, u32[]{:S(2)}, u32[]{:S(2)}) collective-permute-start(bf16[128,256]{1,0:T(8,128)(2,1)S(1)} %shard_map.72.refs_1_), channel_id=1, source_target_pairs={{0,2},{2,0},{4,6},{6,4},{1,3},{3,1},{5,7},{7,5},{8,10},{10,8},{12,... | collective-permute-start | bytes 196616 | tf_op jit(solution)/shard_map/ppermute | solution.py:237
  40.6 0.0 collective-permute-done.14.refs_1_
  40.6 0.6 %shard_map.66.refs_0_ = bf16[1024,2,384]{2,1,0:T(2,128)(2,1)S(1)} custom-call(bf16[128,256]{1,0:T(8,128)(2,1)S(1)} %shard_map.64.refs_0_, bf16[128,256]{1,0:T(8,128)(2,1)S(1)} %collective-permute-done.14.refs_1_, bf16[256,1024]{1,0:T(8,128)(2,1)S(1)} %shard_map.65.refs_2_.refs_3_), custom_call_target="tpu_custom_call" | custom-call | bytes 1048576 | tf_op jit(solution)/shard_map/pallas_call | solution.py:18
  41.2 0.9 %collective-permute-done.16.refs_2_ = bf16[128,256]{1,0:T(8,128)(2,1)S(1)} collective-permute-done((bf16[128,256]{1,0:T(8,128)(2,1)S(1)}, bf16[128,256]{1,0:T(8,128)(2,1)S(1)}, u32[]{:S(2)}, u32[]{:S(2)}) %collective-permute-start.16) | collective-permute-done | bytes 65568 | tf_op jit(solution)/shard_map/ppermute | solution.py:237
  42.1 0.6 %shard_map.68.refs_0_ = bf16[1024,2,384]{2,1,0:T(2,128)(2,1)S(1)} custom-call(bf16[1024,2,384]{2,1,0:T(2,128)(2,1)S(1)} %shard_map.66.refs_0_, bf16[128,256]{1,0:T(8,128)(2,1)S(1)} %shard_map.67.refs_1_, bf16[128,256]{1,0:T(8,128)(2,1)S(1)} %collective-permute-done.16.refs_2_, ...), custom_call_target="tpu_custom_call", output_to_operand_aliasing={{}: (0, {})} | custom-call | bytes 1048576 | tf_op jit(solution)/shard_map/pallas_call | solution.py:18
  42.6 0.2 collective-permute-done.19.refs_2_
  42.8 1.5 %shard_map.73 = bf16[1024,2,384]{2,1,0:T(2,128)(2,1)} custom-call(bf16[1024,2,384]{2,1,0:T(2,128)(2,1)S(1)} %shard_map.68.refs_0_, bf16[128,256]{1,0:T(8,128)(2,1)S(1)} %shard_map.72.refs_1_, bf16[128,256]{1,0:T(8,128)(2,1)S(1)} %collective-permute-done.19.refs_2_, bf16[256,1024]{1,0:T(8,128)(2,1)S(1)} %shard_map.65.refs_2_.refs_3_), custom_call_target="tpu_custom_call" | custom-call | bytes 4194304 | tf_op jit(solution)/shard_map/pallas_call | solution.py:18
  (15 shorter events, 0.1 us)
Async XLA Ops:
  0.0 6.5 %copy-start = (bf16[8,1,2,3]{0,2,3,1:T(2,128)(2,1)S(1)}, bf16[8,1,2,3]{0,2,3,1:T(2,128)(2,1)}, u32[]{:S(2)}) copy-start(bf16[8,1,2,3]{0,2,3,1:T(2,128)(2,1)} %param.9) | copy-start | bytes 292
  1.9 7.6 %collective-permute-start = (bf16[16,2432]{1,0:T(8,128)(2,1)S(1)}, bf16[16,2432]{1,0:T(8,128)(2,1)S(1)}, u32[]{:S(2)}, u32[]{:S(2)}) collective-permute-start(bf16[16,2432]{1,0:T(8,128)(2,1)S(1)} %get-tuple-element.34), channel_id=1, source_target_pairs={{0,24},{8,16},{16,8},{24,0},{1,25},{9,17},{17,9},{25,1},{2,26},{10... | collective-permute-start | bytes 233480 | tf_op jit(solution)/shard_map/ppermute | solution.py:233
  5.9 4.4 %collective-permute-start.1 = (bf16[16,2432]{1,0:T(8,128)(2,1)S(1)}, bf16[16,2432]{1,0:T(8,128)(2,1)S(1)}, u32[]{:S(2)}, u32[]{:S(2)}) collective-permute-start(bf16[16,2432]{1,0:T(8,128)(2,1)S(1)} %get-tuple-element.35), channel_id=1, source_target_pairs={{0,16},{8,24},{16,0},{24,8},{1,17},{9,25},{17,1},{25,9},{2,18},{10... | collective-permute-start | bytes 233480 | tf_op jit(solution)/shard_map/ppermute | solution.py:233
  6.4 4.4 %collective-permute-start.2 = (bf16[16,2432]{1,0:T(8,128)(2,1)S(1)}, bf16[16,2432]{1,0:T(8,128)(2,1)S(1)}, u32[]{:S(2)}, u32[]{:S(2)}) collective-permute-start(bf16[16,2432]{1,0:T(8,128)(2,1)S(1)} %get-tuple-element.36), channel_id=1, source_target_pairs={{0,8},{8,0},{16,24},{24,16},{1,9},{9,1},{17,25},{25,17},{2,10},{10... | collective-permute-start | bytes 233480 | tf_op jit(solution)/shard_map/ppermute | solution.py:233
  10.8 4.3 %collective-permute-start.6 = (bf16[64,512]{1,0:T(8,128)(2,1)S(1)}, bf16[64,512]{1,0:T(8,128)(2,1)S(1)}, u32[]{:S(2)}, u32[]{:S(2)}) collective-permute-start(bf16[64,512]{1,0:T(8,128)(2,1)S(1)} %get-tuple-element.45), channel_id=1, source_target_pairs={{0,2},{2,0},{4,6},{6,4},{1,3},{3,1},{5,7},{7,5},{8,10},{10,8},{12,... | collective-permute-start | bytes 196616 | tf_op jit(solution)/shard_map/ppermute | solution.py:237
  12.5 6.1 %collective-permute-start.8 = (bf16[64,512]{1,0:T(8,128)(2,1)S(1)}, bf16[64,512]{1,0:T(8,128)(2,1)S(1)}, u32[]{:S(2)}, u32[]{:S(2)}) collective-permute-start(bf16[64,512]{1,0:T(8,128)(2,1)S(1)} %get-tuple-element.46), channel_id=1, source_target_pairs={{0,6},{2,4},{4,2},{6,0},{1,7},{3,5},{5,3},{7,1},{8,14},{10,12},{12... | collective-permute-start | bytes 196616 | tf_op jit(solution)/shard_map/ppermute | solution.py:237
  14.9 5.9 %collective-permute-start.4 = (bf16[64,512]{1,0:T(8,128)(2,1)S(1)}, bf16[64,512]{1,0:T(8,128)(2,1)S(1)}, u32[]{:S(2)}, u32[]{:S(2)}) collective-permute-start(bf16[64,512]{1,0:T(8,128)(2,1)S(1)} %get-tuple-element.42), channel_id=1, source_target_pairs={{0,4},{2,6},{4,0},{6,2},{1,5},{3,7},{5,1},{7,3},{8,12},{10,14},{12... | collective-permute-start | bytes 196616 | tf_op jit(solution)/shard_map/ppermute | solution.py:237
  15.2 5.7 %collective-permute-start.7 = (bf16[64,512]{1,0:T(8,128)(2,1)S(1)}, bf16[64,512]{1,0:T(8,128)(2,1)S(1)}, u32[]{:S(2)}, u32[]{:S(2)}) collective-permute-start(bf16[64,512]{1,0:T(8,128)(2,1)S(1)} %collective-permute-done.6.refs_0_.refs_4_), channel_id=1, source_target_pairs={{0,1},{1,0},{2,3},{3,2},{4,5},{5,4},{6,7},{7,6},{8,9},{9,8},{10,11... | collective-permute-start | bytes 196616 | tf_op jit(solution)/shard_map/ppermute | solution.py:241
  18.6 2.2 %collective-permute-start.9 = (bf16[64,512]{1,0:T(8,128)(2,1)S(1)}, bf16[64,512]{1,0:T(8,128)(2,1)S(1)}, u32[]{:S(2)}, u32[]{:S(2)}) collective-permute-start(bf16[64,512]{1,0:T(8,128)(2,1)S(1)} %collective-permute-done.8.refs_2_.refs_6_), channel_id=1, source_target_pairs={{0,1},{1,0},{2,3},{3,2},{4,5},{5,4},{6,7},{7,6},{8,9},{9,8},{10,11... | collective-permute-start | bytes 196616 | tf_op jit(solution)/shard_map/ppermute | solution.py:241
  18.6 5.5 %collective-permute-start.3 = (bf16[64,512]{1,0:T(8,128)(2,1)S(1)}, bf16[64,512]{1,0:T(8,128)(2,1)S(1)}, u32[]{:S(2)}, u32[]{:S(2)}) collective-permute-start(bf16[64,512]{1,0:T(8,128)(2,1)S(1)} %get-tuple-element.41.refs_0_), channel_id=1, source_target_pairs={{0,1},{1,0},{2,3},{3,2},{4,5},{5,4},{6,7},{7,6},{8,9},{9,8},{10,11... | collective-permute-start | bytes 196616 | tf_op jit(solution)/shard_map/ppermute | solution.py:241
  20.8 6.0 %collective-permute-start.5 = (bf16[64,512]{1,0:T(8,128)(2,1)S(1)}, bf16[64,512]{1,0:T(8,128)(2,1)S(1)}, u32[]{:S(2)}, u32[]{:S(2)}) collective-permute-start(bf16[64,512]{1,0:T(8,128)(2,1)S(1)} %collective-permute-done.4.refs_2_), channel_id=1, source_target_pairs={{0,1},{1,0},{2,3},{3,2},{4,5},{5,4},{6,7},{7,6},{8,9},{9,8},{10,11... | collective-permute-start | bytes 196616 | tf_op jit(solution)/shard_map/ppermute | solution.py:241
  21.1 6.5 %collective-permute-start.10 = (bf16[128,256]{1,0:T(8,128)(2,1)S(1)}, bf16[128,256]{1,0:T(8,128)(2,1)S(1)}, u32[]{:S(2)}, u32[]{:S(2)}) collective-permute-start(bf16[128,256]{1,0:T(8,128)(2,1)S(1)} %shard_map.59), channel_id=1, source_target_pairs={{0,2},{2,0},{4,6},{6,4},{1,3},{3,1},{5,7},{7,5},{8,10},{10,8},{12,... | collective-permute-start | bytes 196616 | tf_op jit(solution)/shard_map/ppermute | solution.py:237
  21.6 6.4 %collective-permute-start.13 = (bf16[128,256]{1,0:T(8,128)(2,1)S(1)}, bf16[128,256]{1,0:T(8,128)(2,1)S(1)}, u32[]{:S(2)}, u32[]{:S(2)}) collective-permute-start(bf16[128,256]{1,0:T(8,128)(2,1)S(1)} %shard_map.62), channel_id=1, source_target_pairs={{0,2},{2,0},{4,6},{6,4},{1,3},{3,1},{5,7},{7,5},{8,10},{10,8},{12,... | collective-permute-start | bytes 196616 | tf_op jit(solution)/shard_map/ppermute | solution.py:237
  23.9 8.5 %collective-permute-start.17 = (bf16[128,256]{1,0:T(8,128)(2,1)S(1)}, bf16[128,256]{1,0:T(8,128)(2,1)S(1)}, u32[]{:S(2)}, u32[]{:S(2)}) collective-permute-start(bf16[128,256]{1,0:T(8,128)(2,1)S(1)} %shard_map.70), channel_id=1, source_target_pairs={{0,2},{2,0},{4,6},{6,4},{1,3},{3,1},{5,7},{7,5},{8,10},{10,8},{12,... | collective-permute-start | bytes 196616 | tf_op jit(solution)/shard_map/ppermute | solution.py:237
  24.1 5.2 %collective-permute-start.12 = (bf16[64,384]{1,0:T(8,128)(2,1)S(1)}, bf16[64,384]{1,0:T(8,128)(2,1)S(1)}, u32[]{:S(2)}, u32[]{:S(2)}) collective-permute-start(bf16[64,384]{1,0:T(8,128)(2,1)S(1)} %get-tuple-element.48.cot), channel_id=1, source_target_pairs={{0,4},{2,6},{4,0},{6,2},{1,5},{3,7},{5,1},{7,3},{8,12},{10,14},{12... | collective-permute-start | bytes 147464 | tf_op jit(solution)/shard_map/ppermute | solution.py:237
  27.7 8.2 %collective-permute-start.11 = (bf16[128,256]{1,0:T(8,128)(2,1)S(1)}, bf16[128,256]{1,0:T(8,128)(2,1)S(1)}, u32[]{:S(2)}, u32[]{:S(2)}) collective-permute-start(bf16[128,256]{1,0:T(8,128)(2,1)S(1)} %shard_map.60), channel_id=1, source_target_pairs={{0,4},{2,6},{4,0},{6,2},{1,5},{3,7},{5,1},{7,3},{8,12},{10,14},{12... | collective-permute-start | bytes 196616 | tf_op jit(solution)/shard_map/ppermute | solution.py:237
  29.3 8.3 %collective-permute-start.15 = (bf16[128,256]{1,0:T(8,128)(2,1)S(1)}, bf16[128,256]{1,0:T(8,128)(2,1)S(1)}, u32[]{:S(2)}, u32[]{:S(2)}) collective-permute-start(bf16[128,256]{1,0:T(8,128)(2,1)S(1)} %shard_map.63), channel_id=1, source_target_pairs={{0,4},{2,6},{4,0},{6,2},{1,5},{3,7},{5,1},{7,3},{8,12},{10,14},{12... | collective-permute-start | bytes 196616 | tf_op jit(solution)/shard_map/ppermute | solution.py:237
  32.4 6.0 %collective-permute-start.18 = (bf16[128,256]{1,0:T(8,128)(2,1)S(1)}, bf16[128,256]{1,0:T(8,128)(2,1)S(1)}, u32[]{:S(2)}, u32[]{:S(2)}) collective-permute-start(bf16[128,256]{1,0:T(8,128)(2,1)S(1)} %shard_map.71), channel_id=1, source_target_pairs={{0,4},{2,6},{4,0},{6,2},{1,5},{3,7},{5,1},{7,3},{8,12},{10,14},{12... | collective-permute-start | bytes 196616 | tf_op jit(solution)/shard_map/ppermute | solution.py:237
  35.9 4.7 %collective-permute-start.14 = (bf16[128,256]{1,0:T(8,128)(2,1)S(1)}, bf16[128,256]{1,0:T(8,128)(2,1)S(1)}, u32[]{:S(2)}, u32[]{:S(2)}) collective-permute-start(bf16[128,256]{1,0:T(8,128)(2,1)S(1)} %shard_map.64.refs_0_), channel_id=1, source_target_pairs={{0,2},{2,0},{4,6},{6,4},{1,3},{3,1},{5,7},{7,5},{8,10},{10,8},{12,... | collective-permute-start | bytes 196616 | tf_op jit(solution)/shard_map/ppermute | solution.py:237
  37.7 4.3 %collective-permute-start.16 = (bf16[128,256]{1,0:T(8,128)(2,1)S(1)}, bf16[128,256]{1,0:T(8,128)(2,1)S(1)}, u32[]{:S(2)}, u32[]{:S(2)}) collective-permute-start(bf16[128,256]{1,0:T(8,128)(2,1)S(1)} %shard_map.67.refs_1_), channel_id=1, source_target_pairs={{0,2},{2,0},{4,6},{6,4},{1,3},{3,1},{5,7},{7,5},{8,10},{10,8},{12,... | collective-permute-start | bytes 196616 | tf_op jit(solution)/shard_map/ppermute | solution.py:237
  38.4 4.4 %collective-permute-start.19 = (bf16[128,256]{1,0:T(8,128)(2,1)S(1)}, bf16[128,256]{1,0:T(8,128)(2,1)S(1)}, u32[]{:S(2)}, u32[]{:S(2)}) collective-permute-start(bf16[128,256]{1,0:T(8,128)(2,1)S(1)} %shard_map.72.refs_1_), channel_id=1, source_target_pairs={{0,2},{2,0},{4,6},{6,4},{1,3},{3,1},{5,7},{7,5},{8,10},{10,8},{12,... | collective-permute-start | bytes 196616 | tf_op jit(solution)/shard_map/ppermute | solution.py:237

commit v7 on v6

--- a/solution.py
+++ b/solution.py
@@ -157,7 +157,7 @@
             out[i * rows : (i + 1) * rows, pl.ds(start, width)] = blocks[halves * i + h][:, :width]
 
 
-def add_kernel(kept, arrived, out):
+def add_kernel(arrived, kept, out):
     out[...] = (kept[...] + arrived[...].astype(F32)).astype(BF16)
 
 
@@ -314,7 +314,7 @@
         kept = [gate_up((0, 2), *chunk, F32) for chunk in chunks]
         near = [swap_blk(a, nb, 1) for a in away]
         pair = [
-            call(add_kernel, sds(k.shape, BF16), (k, n), [VMEM] * 2, nbytes=1 << 18)
+            call(add_kernel, sds(k.shape, BF16), (n, k), [VMEM] * 2, nbytes=1 << 18)
             for k, n in zip(kept, near)
         ]
         far_cot, pair[1 % len(pair)] = lax.optimization_barrier((far_cot, pair[1 % len(pair)]))
@@ -352,7 +352,7 @@
     def buffers(at, to):
         return [
             pltpu.VMEM((nb * rows, 2 * (to - at)), BF16),
-            pltpu.VMEM(((to - at) // size, 2 * depth, size), F32),
+            pltpu.VMEM(((to - at) // size, 2 * depth + 8, size), F32),
         ]
 
     finished = []

time: 44.4 us -> 44.4 us (level)
  no operation moved by 1% of the time
where the time goes in v7:
time: 44.4 us; the launch traced here: 44.3 us
  starting transfers between devices  20.5 us (46%)
  waiting for transfers between devices  14.2 us (32%)
  Pallas kernels  9.36 us (21%)
    ppermute x13, starting transfers between devices, swap_blk(): return lax.ppermute(x, 'blk', [(i, i ^ p) for i in range(size)])  15.3 us
    ppermute x13, waiting for transfers between devices, swap_blk(): return lax.ppermute(x, 'blk', [(i, i ^ p) for i in range(size)])  12.8 us
    pallas_call x19, Pallas kernels, call(): pl.pallas_call(kernel, out_shape=out_shape, in_specs=in_specs, out_specs=...  9.36 us
    ppermute x3, starting transfers between devices, swap_group(): return lax.ppermute(x, 'group', [(i, i ^ s) for i in range(size)])  4.61 us
    ppermute x3, waiting for transfers between devices, swap_group(): return lax.ppermute(x, 'group', [(i, i ^ s) for i in range(size)])  1.31 us
  transfers between devices with their start and end apart: 20, of which 11 were waited for; matrix products, arithmetic and copies ran while one was open for 0% of the time, Pallas kernels for 13%

profile of v7, /device:TPU:0, one launch (start us, length us, event | category | flops | bytes accessed | tf_op | source)
XLA Modules:
  0.0 44.3 jit_solution(11031932237549981166)
XLA Ops:
  0.0 1.9 %shard_map.55 = (bf16[16,2432]{1,0:T(8,128)(2,1)S(1)}, bf16[16,2432]{1,0:T(8,128)(2,1)S(1)}, bf16[16,2432]{1,0:T(8,128)(2,1)S(1)}, bf16[16,2432]{1,0:T(8,128)(2,1)S(1)}) custom-call(bf16[128,4096]{1,0:T(8,128)(2,1)} %tokens.1, s32[8,128]{1,0:T(8,128)} %bitcast.9, bf16[128,8,384]{2,1,0:T(8,128)(2,1)} %act.1), custom_call_target="tpu_custom_call" | custom-call | bytes 2097152 | tf_op jit(solution)/shard_map/pallas_call | solution.py:18
  1.9 4.0 %collective-permute-start = (bf16[16,2432]{1,0:T(8,128)(2,1)S(1)}, bf16[16,2432]{1,0:T(8,128)(2,1)S(1)}, u32[]{:S(2)}, u32[]{:S(2)}) collective-permute-start(bf16[16,2432]{1,0:T(8,128)(2,1)S(1)} %get-tuple-element.34), channel_id=1, source_target_pairs={{0,24},{8,16},{16,8},{24,0},{1,25},{9,17},{17,9},{25,1},{2,26},{10... | collective-permute-start | bytes 233480 | tf_op jit(solution)/shard_map/ppermute | solution.py:233
  5.9 0.5 %collective-permute-start.1 = (bf16[16,2432]{1,0:T(8,128)(2,1)S(1)}, bf16[16,2432]{1,0:T(8,128)(2,1)S(1)}, u32[]{:S(2)}, u32[]{:S(2)}) collective-permute-start(bf16[16,2432]{1,0:T(8,128)(2,1)S(1)} %get-tuple-element.35), channel_id=1, source_target_pairs={{0,16},{8,24},{16,0},{24,8},{1,17},{9,25},{17,1},{25,9},{2,18},{10... | collective-permute-start | bytes 233480 | tf_op jit(solution)/shard_map/ppermute | solution.py:233
  6.4 0.1 collective-permute-start.2
  6.5 0.1 copy.7.scales
  6.6 2.8 %shard_map.56.refs_4_ = bf16[1024,768]{1,0:T(8,128)(2,1)S(1)} custom-call(f32[8,2,3]{2,1,0:T(2,128)S(1)} %copy.7.scales, bf16[1024,2,384]{2,1,0:T(2,128)(2,1)} %bitcast.8), custom_call_target="tpu_custom_call" | custom-call | bytes 4194304 | tf_op jit(solution)/shard_map/pallas_call | solution.py:18
  9.5 0.0 collective-permute-done.refs_1_
  9.5 0.8 %collective-permute-done.1.refs_2_ = bf16[16,2432]{1,0:T(8,128)(2,1)S(1)} collective-permute-done((bf16[16,2432]{1,0:T(8,128)(2,1)S(1)}, bf16[16,2432]{1,0:T(8,128)(2,1)S(1)}, u32[]{:S(2)}, u32[]{:S(2)}) %collective-permute-start.1) | collective-permute-done | bytes 77856 | tf_op jit(solution)/shard_map/ppermute | solution.py:233
  10.3 0.5 %collective-permute-done.2.refs_3_ = bf16[16,2432]{1,0:T(8,128)(2,1)S(1)} collective-permute-done((bf16[16,2432]{1,0:T(8,128)(2,1)S(1)}, bf16[16,2432]{1,0:T(8,128)(2,1)S(1)}, u32[]{:S(2)}, u32[]{:S(2)}) %collective-permute-start.2) | collective-permute-done | bytes 77856 | tf_op jit(solution)/shard_map/ppermute | solution.py:233
  10.8 1.6 %collective-permute-start.6 = (bf16[64,512]{1,0:T(8,128)(2,1)S(1)}, bf16[64,512]{1,0:T(8,128)(2,1)S(1)}, u32[]{:S(2)}, u32[]{:S(2)}) collective-permute-start(bf16[64,512]{1,0:T(8,128)(2,1)S(1)} %get-tuple-element.45), channel_id=1, source_target_pairs={{0,2},{2,0},{4,6},{6,4},{1,3},{3,1},{5,7},{7,5},{8,10},{10,8},{12,... | collective-permute-start | bytes 196616 | tf_op jit(solution)/shard_map/ppermute | solution.py:237
  12.5 2.5 %collective-permute-start.8 = (bf16[64,512]{1,0:T(8,128)(2,1)S(1)}, bf16[64,512]{1,0:T(8,128)(2,1)S(1)}, u32[]{:S(2)}, u32[]{:S(2)}) collective-permute-start(bf16[64,512]{1,0:T(8,128)(2,1)S(1)} %get-tuple-element.46), channel_id=1, source_target_pairs={{0,6},{2,4},{4,2},{6,0},{1,7},{3,5},{5,3},{7,1},{8,14},{10,12},{12... | collective-permute-start | bytes 196616 | tf_op jit(solution)/shard_map/ppermute | solution.py:237
  14.9 0.1 collective-permute-start.4
  15.1 0.1 collective-permute-done.6.refs_0_.refs_4_
  15.2 3.4 %collective-permute-done.8.refs_2_.refs_6_ = bf16[64,512]{1,0:T(8,128)(2,1)S(1)} collective-permute-done((bf16[64,512]{1,0:T(8,128)(2,1)S(1)}, bf16[64,512]{1,0:T(8,128)(2,1)S(1)}, u32[]{:S(2)}, u32[]{:S(2)}) %collective-permute-start.8) | collective-permute-done | bytes 65568 | tf_op jit(solution)/shard_map/ppermute | solution.py:237
  18.6 0.5 %collective-permute-start.3 = (bf16[64,512]{1,0:T(8,128)(2,1)S(1)}, bf16[64,512]{1,0:T(8,128)(2,1)S(1)}, u32[]{:S(2)}, u32[]{:S(2)}) collective-permute-start(bf16[64,512]{1,0:T(8,128)(2,1)S(1)} %get-tuple-element.41.refs_0_), channel_id=1, source_target_pairs={{0,1},{1,0},{2,3},{3,2},{4,5},{5,4},{6,7},{7,6},{8,9},{9,8},{10,11... | collective-permute-start | bytes 196616 | tf_op jit(solution)/shard_map/ppermute | solution.py:241
  19.1 1.7 %collective-permute-done.4.refs_2_ = bf16[64,512]{1,0:T(8,128)(2,1)S(1)} collective-permute-done((bf16[64,512]{1,0:T(8,128)(2,1)S(1)}, bf16[64,512]{1,0:T(8,128)(2,1)S(1)}, u32[]{:S(2)}, u32[]{:S(2)}) %collective-permute-start.4) | collective-permute-done | bytes 65568 | tf_op jit(solution)/shard_map/ppermute | solution.py:237
  20.8 0.0 collective-permute-start.5
  20.8 0.3 shard_map.59
  21.1 0.2 collective-permute-start.10
  21.3 0.3 shard_map.61
  21.6 1.9 %collective-permute-start.13 = (bf16[128,256]{1,0:T(8,128)(2,1)S(1)}, bf16[128,256]{1,0:T(8,128)(2,1)S(1)}, u32[]{:S(2)}, u32[]{:S(2)}) collective-permute-start(bf16[128,256]{1,0:T(8,128)(2,1)S(1)} %shard_map.61), channel_id=1, source_target_pairs={{0,2},{2,0},{4,6},{6,4},{1,3},{3,1},{5,7},{7,5},{8,10},{10,8},{12,... | collective-permute-start | bytes 196616 | tf_op jit(solution)/shard_map/ppermute | solution.py:237
  23.6 0.3 shard_map.70
  23.9 0.2 collective-permute-start.17
  24.1 2.7 %collective-permute-start.12 = (bf16[64,384]{1,0:T(8,128)(2,1)S(1)}, bf16[64,384]{1,0:T(8,128)(2,1)S(1)}, u32[]{:S(2)}, u32[]{:S(2)}) collective-permute-start(bf16[64,384]{1,0:T(8,128)(2,1)S(1)} %get-tuple-element.48.cot), channel_id=1, source_target_pairs={{0,4},{2,6},{4,0},{6,2},{1,5},{3,7},{5,1},{7,3},{8,12},{10,14},{12... | collective-permute-start | bytes 147464 | tf_op jit(solution)/shard_map/ppermute | solution.py:237
  26.8 0.3 shard_map.69.kept
  27.1 0.3 shard_map.62.kept
  27.4 0.3 shard_map.58.kept
  27.7 0.0 collective-permute-done.10.arrived.near
  27.7 0.3 collective-permute-start.11
  28.1 1.3 %collective-permute-done.12.far_cot = bf16[64,384]{1,0:T(8,128)(2,1)S(1)} collective-permute-done((bf16[64,384]{1,0:T(8,128)(2,1)S(1)}, bf16[64,384]{1,0:T(8,128)(2,1)S(1)}, u32[]{:S(2)}, u32[]{:S(2)}) %collective-permute-start.12) | collective-permute-done | bytes 49184 | tf_op jit(solution)/shard_map/ppermute | solution.py:237
  29.3 3.1 %collective-permute-start.15 = (bf16[128,256]{1,0:T(8,128)(2,1)S(1)}, bf16[128,256]{1,0:T(8,128)(2,1)S(1)}, u32[]{:S(2)}, u32[]{:S(2)}) collective-permute-start(bf16[128,256]{1,0:T(8,128)(2,1)S(1)} %shard_map.63), channel_id=1, source_target_pairs={{0,4},{2,6},{4,0},{6,2},{1,5},{3,7},{5,1},{7,3},{8,12},{10,14},{12... | collective-permute-start | bytes 196616 | tf_op jit(solution)/shard_map/ppermute | solution.py:237
  32.4 0.0 collective-permute-done.17.arrived.near
  32.4 0.1 collective-permute-start.18
  32.5 3.4 %collective-permute-done.11.far = bf16[128,256]{1,0:T(8,128)(2,1)S(1)} collective-permute-done((bf16[128,256]{1,0:T(8,128)(2,1)S(1)}, bf16[128,256]{1,0:T(8,128)(2,1)S(1)}, u32[]{:S(2)}, u32[]{:S(2)}) %collective-permute-start.11) | collective-permute-done | bytes 65568 | tf_op jit(solution)/shard_map/ppermute | solution.py:237
  35.9 0.1 shard_map.64.refs_0_
  35.9 0.1 collective-permute-start.14
  36.0 1.6 %collective-permute-done.15.far = bf16[128,256]{1,0:T(8,128)(2,1)S(1)} collective-permute-done((bf16[128,256]{1,0:T(8,128)(2,1)S(1)}, bf16[128,256]{1,0:T(8,128)(2,1)S(1)}, u32[]{:S(2)}, u32[]{:S(2)}) %collective-permute-start.15) | collective-permute-done | bytes 65568 | tf_op jit(solution)/shard_map/ppermute | solution.py:237
  37.7 0.1 shard_map.67.refs_1_
  37.7 0.4 collective-permute-start.16
  38.2 0.2 collective-permute-done.18.far
  38.4 0.1 shard_map.72.refs_1_
  38.4 2.1 %collective-permute-start.19 = (bf16[128,256]{1,0:T(8,128)(2,1)S(1)}, bf16[128,256]{1,0:T(8,128)(2,1)S(1)}, u32[]{:S(2)}, u32[]{:S(2)}) collective-permute-start(bf16[128,256]{1,0:T(8,128)(2,1)S(1)} %shard_map.72.refs_1_), channel_id=1, source_target_pairs={{0,2},{2,0},{4,6},{6,4},{1,3},{3,1},{5,7},{7,5},{8,10},{10,8},{12,... | collective-permute-start | bytes 196616 | tf_op jit(solution)/shard_map/ppermute | solution.py:237
  40.6 0.0 collective-permute-done.14.refs_1_
  40.6 0.6 %shard_map.66.refs_0_ = bf16[1024,2,384]{2,1,0:T(2,128)(2,1)S(1)} custom-call(bf16[128,256]{1,0:T(8,128)(2,1)S(1)} %shard_map.64.refs_0_, bf16[128,256]{1,0:T(8,128)(2,1)S(1)} %collective-permute-done.14.refs_1_, bf16[256,1024]{1,0:T(8,128)(2,1)S(1)} %shard_map.65.refs_2_.refs_3_), custom_call_target="tpu_custom_call" | custom-call | bytes 1048576 | tf_op jit(solution)/shard_map/pallas_call | solution.py:18
  41.2 0.9 %collective-permute-done.16.refs_2_ = bf16[128,256]{1,0:T(8,128)(2,1)S(1)} collective-permute-done((bf16[128,256]{1,0:T(8,128)(2,1)S(1)}, bf16[128,256]{1,0:T(8,128)(2,1)S(1)}, u32[]{:S(2)}, u32[]{:S(2)}) %collective-permute-start.16) | collective-permute-done | bytes 65568 | tf_op jit(solution)/shard_map/ppermute | solution.py:237
  42.1 0.6 %shard_map.68.refs_0_ = bf16[1024,2,384]{2,1,0:T(2,128)(2,1)S(1)} custom-call(bf16[1024,2,384]{2,1,0:T(2,128)(2,1)S(1)} %shard_map.66.refs_0_, bf16[128,256]{1,0:T(8,128)(2,1)S(1)} %shard_map.67.refs_1_, bf16[128,256]{1,0:T(8,128)(2,1)S(1)} %collective-permute-done.16.refs_2_, ...), custom_call_target="tpu_custom_call", output_to_operand_aliasing={{}: (0, {})} | custom-call | bytes 1048576 | tf_op jit(solution)/shard_map/pallas_call | solution.py:18
  42.6 0.2 collective-permute-done.19.refs_2_
  42.8 1.5 %shard_map.73 = bf16[1024,2,384]{2,1,0:T(2,128)(2,1)} custom-call(bf16[1024,2,384]{2,1,0:T(2,128)(2,1)S(1)} %shard_map.68.refs_0_, bf16[128,256]{1,0:T(8,128)(2,1)S(1)} %shard_map.72.refs_1_, bf16[128,256]{1,0:T(8,128)(2,1)S(1)} %collective-permute-done.19.refs_2_, bf16[256,1024]{1,0:T(8,128)(2,1)S(1)} %shard_map.65.refs_2_.refs_3_), custom_call_target="tpu_custom_call" | custom-call | bytes 4194304 | tf_op jit(solution)/shard_map/pallas_call | solution.py:18
  (15 shorter events, 0.1 us)
Async XLA Ops:
  0.0 6.5 %copy-start = (bf16[8,1,2,3]{0,2,3,1:T(2,128)(2,1)S(1)}, bf16[8,1,2,3]{0,2,3,1:T(2,128)(2,1)}, u32[]{:S(2)}) copy-start(bf16[8,1,2,3]{0,2,3,1:T(2,128)(2,1)} %param.9) | copy-start | bytes 292
  1.9 7.6 %collective-permute-start = (bf16[16,2432]{1,0:T(8,128)(2,1)S(1)}, bf16[16,2432]{1,0:T(8,128)(2,1)S(1)}, u32[]{:S(2)}, u32[]{:S(2)}) collective-permute-start(bf16[16,2432]{1,0:T(8,128)(2,1)S(1)} %get-tuple-element.34), channel_id=1, source_target_pairs={{0,24},{8,16},{16,8},{24,0},{1,25},{9,17},{17,9},{25,1},{2,26},{10... | collective-permute-start | bytes 233480 | tf_op jit(solution)/shard_map/ppermute | solution.py:233
  5.9 4.4 %collective-permute-start.1 = (bf16[16,2432]{1,0:T(8,128)(2,1)S(1)}, bf16[16,2432]{1,0:T(8,128)(2,1)S(1)}, u32[]{:S(2)}, u32[]{:S(2)}) collective-permute-start(bf16[16,2432]{1,0:T(8,128)(2,1)S(1)} %get-tuple-element.35), channel_id=1, source_target_pairs={{0,16},{8,24},{16,0},{24,8},{1,17},{9,25},{17,1},{25,9},{2,18},{10... | collective-permute-start | bytes 233480 | tf_op jit(solution)/shard_map/ppermute | solution.py:233
  6.4 4.4 %collective-permute-start.2 = (bf16[16,2432]{1,0:T(8,128)(2,1)S(1)}, bf16[16,2432]{1,0:T(8,128)(2,1)S(1)}, u32[]{:S(2)}, u32[]{:S(2)}) collective-permute-start(bf16[16,2432]{1,0:T(8,128)(2,1)S(1)} %get-tuple-element.36), channel_id=1, source_target_pairs={{0,8},{8,0},{16,24},{24,16},{1,9},{9,1},{17,25},{25,17},{2,10},{10... | collective-permute-start | bytes 233480 | tf_op jit(solution)/shard_map/ppermute | solution.py:233
  10.8 4.3 %collective-permute-start.6 = (bf16[64,512]{1,0:T(8,128)(2,1)S(1)}, bf16[64,512]{1,0:T(8,128)(2,1)S(1)}, u32[]{:S(2)}, u32[]{:S(2)}) collective-permute-start(bf16[64,512]{1,0:T(8,128)(2,1)S(1)} %get-tuple-element.45), channel_id=1, source_target_pairs={{0,2},{2,0},{4,6},{6,4},{1,3},{3,1},{5,7},{7,5},{8,10},{10,8},{12,... | collective-permute-start | bytes 196616 | tf_op jit(solution)/shard_map/ppermute | solution.py:237
  12.5 6.1 %collective-permute-start.8 = (bf16[64,512]{1,0:T(8,128)(2,1)S(1)}, bf16[64,512]{1,0:T(8,128)(2,1)S(1)}, u32[]{:S(2)}, u32[]{:S(2)}) collective-permute-start(bf16[64,512]{1,0:T(8,128)(2,1)S(1)} %get-tuple-element.46), channel_id=1, source_target_pairs={{0,6},{2,4},{4,2},{6,0},{1,7},{3,5},{5,3},{7,1},{8,14},{10,12},{12... | collective-permute-start | bytes 196616 | tf_op jit(solution)/shard_map/ppermute | solution.py:237
  14.9 5.9 %collective-permute-start.4 = (bf16[64,512]{1,0:T(8,128)(2,1)S(1)}, bf16[64,512]{1,0:T(8,128)(2,1)S(1)}, u32[]{:S(2)}, u32[]{:S(2)}) collective-permute-start(bf16[64,512]{1,0:T(8,128)(2,1)S(1)} %get-tuple-element.42), channel_id=1, source_target_pairs={{0,4},{2,6},{4,0},{6,2},{1,5},{3,7},{5,1},{7,3},{8,12},{10,14},{12... | collective-permute-start | bytes 196616 | tf_op jit(solution)/shard_map/ppermute | solution.py:237
  15.2 5.7 %collective-permute-start.7 = (bf16[64,512]{1,0:T(8,128)(2,1)S(1)}, bf16[64,512]{1,0:T(8,128)(2,1)S(1)}, u32[]{:S(2)}, u32[]{:S(2)}) collective-permute-start(bf16[64,512]{1,0:T(8,128)(2,1)S(1)} %collective-permute-done.6.refs_0_.refs_4_), channel_id=1, source_target_pairs={{0,1},{1,0},{2,3},{3,2},{4,5},{5,4},{6,7},{7,6},{8,9},{9,8},{10,11... | collective-permute-start | bytes 196616 | tf_op jit(solution)/shard_map/ppermute | solution.py:241
  18.6 2.2 %collective-permute-start.9 = (bf16[64,512]{1,0:T(8,128)(2,1)S(1)}, bf16[64,512]{1,0:T(8,128)(2,1)S(1)}, u32[]{:S(2)}, u32[]{:S(2)}) collective-permute-start(bf16[64,512]{1,0:T(8,128)(2,1)S(1)} %collective-permute-done.8.refs_2_.refs_6_), channel_id=1, source_target_pairs={{0,1},{1,0},{2,3},{3,2},{4,5},{5,4},{6,7},{7,6},{8,9},{9,8},{10,11... | collective-permute-start | bytes 196616 | tf_op jit(solution)/shard_map/ppermute | solution.py:241
  18.6 5.5 %collective-permute-start.3 = (bf16[64,512]{1,0:T(8,128)(2,1)S(1)}, bf16[64,512]{1,0:T(8,128)(2,1)S(1)}, u32[]{:S(2)}, u32[]{:S(2)}) collective-permute-start(bf16[64,512]{1,0:T(8,128)(2,1)S(1)} %get-tuple-element.41.refs_0_), channel_id=1, source_target_pairs={{0,1},{1,0},{2,3},{3,2},{4,5},{5,4},{6,7},{7,6},{8,9},{9,8},{10,11... | collective-permute-start | bytes 196616 | tf_op jit(solution)/shard_map/ppermute | solution.py:241
  20.8 6.0 %collective-permute-start.5 = (bf16[64,512]{1,0:T(8,128)(2,1)S(1)}, bf16[64,512]{1,0:T(8,128)(2,1)S(1)}, u32[]{:S(2)}, u32[]{:S(2)}) collective-permute-start(bf16[64,512]{1,0:T(8,128)(2,1)S(1)} %collective-permute-done.4.refs_2_), channel_id=1, source_target_pairs={{0,1},{1,0},{2,3},{3,2},{4,5},{5,4},{6,7},{7,6},{8,9},{9,8},{10,11... | collective-permute-start | bytes 196616 | tf_op jit(solution)/shard_map/ppermute | solution.py:241
  21.1 6.5 %collective-permute-start.10 = (bf16[128,256]{1,0:T(8,128)(2,1)S(1)}, bf16[128,256]{1,0:T(8,128)(2,1)S(1)}, u32[]{:S(2)}, u32[]{:S(2)}) collective-permute-start(bf16[128,256]{1,0:T(8,128)(2,1)S(1)} %shard_map.59), channel_id=1, source_target_pairs={{0,2},{2,0},{4,6},{6,4},{1,3},{3,1},{5,7},{7,5},{8,10},{10,8},{12,... | collective-permute-start | bytes 196616 | tf_op jit(solution)/shard_map/ppermute | solution.py:237
  21.6 6.4 %collective-permute-start.13 = (bf16[128,256]{1,0:T(8,128)(2,1)S(1)}, bf16[128,256]{1,0:T(8,128)(2,1)S(1)}, u32[]{:S(2)}, u32[]{:S(2)}) collective-permute-start(bf16[128,256]{1,0:T(8,128)(2,1)S(1)} %shard_map.61), channel_id=1, source_target_pairs={{0,2},{2,0},{4,6},{6,4},{1,3},{3,1},{5,7},{7,5},{8,10},{10,8},{12,... | collective-permute-start | bytes 196616 | tf_op jit(solution)/shard_map/ppermute | solution.py:237
  23.9 8.5 %collective-permute-start.17 = (bf16[128,256]{1,0:T(8,128)(2,1)S(1)}, bf16[128,256]{1,0:T(8,128)(2,1)S(1)}, u32[]{:S(2)}, u32[]{:S(2)}) collective-permute-start(bf16[128,256]{1,0:T(8,128)(2,1)S(1)} %shard_map.70), channel_id=1, source_target_pairs={{0,2},{2,0},{4,6},{6,4},{1,3},{3,1},{5,7},{7,5},{8,10},{10,8},{12,... | collective-permute-start | bytes 196616 | tf_op jit(solution)/shard_map/ppermute | solution.py:237
  24.1 5.2 %collective-permute-start.12 = (bf16[64,384]{1,0:T(8,128)(2,1)S(1)}, bf16[64,384]{1,0:T(8,128)(2,1)S(1)}, u32[]{:S(2)}, u32[]{:S(2)}) collective-permute-start(bf16[64,384]{1,0:T(8,128)(2,1)S(1)} %get-tuple-element.48.cot), channel_id=1, source_target_pairs={{0,4},{2,6},{4,0},{6,2},{1,5},{3,7},{5,1},{7,3},{8,12},{10,14},{12... | collective-permute-start | bytes 147464 | tf_op jit(solution)/shard_map/ppermute | solution.py:237
  27.7 8.2 %collective-permute-start.11 = (bf16[128,256]{1,0:T(8,128)(2,1)S(1)}, bf16[128,256]{1,0:T(8,128)(2,1)S(1)}, u32[]{:S(2)}, u32[]{:S(2)}) collective-permute-start(bf16[128,256]{1,0:T(8,128)(2,1)S(1)} %shard_map.60), channel_id=1, source_target_pairs={{0,4},{2,6},{4,0},{6,2},{1,5},{3,7},{5,1},{7,3},{8,12},{10,14},{12... | collective-permute-start | bytes 196616 | tf_op jit(solution)/shard_map/ppermute | solution.py:237
  29.3 8.3 %collective-permute-start.15 = (bf16[128,256]{1,0:T(8,128)(2,1)S(1)}, bf16[128,256]{1,0:T(8,128)(2,1)S(1)}, u32[]{:S(2)}, u32[]{:S(2)}) collective-permute-start(bf16[128,256]{1,0:T(8,128)(2,1)S(1)} %shard_map.63), channel_id=1, source_target_pairs={{0,4},{2,6},{4,0},{6,2},{1,5},{3,7},{5,1},{7,3},{8,12},{10,14},{12... | collective-permute-start | bytes 196616 | tf_op jit(solution)/shard_map/ppermute | solution.py:237
  32.4 6.0 %collective-permute-start.18 = (bf16[128,256]{1,0:T(8,128)(2,1)S(1)}, bf16[128,256]{1,0:T(8,128)(2,1)S(1)}, u32[]{:S(2)}, u32[]{:S(2)}) collective-permute-start(bf16[128,256]{1,0:T(8,128)(2,1)S(1)} %shard_map.71), channel_id=1, source_target_pairs={{0,4},{2,6},{4,0},{6,2},{1,5},{3,7},{5,1},{7,3},{8,12},{10,14},{12... | collective-permute-start | bytes 196616 | tf_op jit(solution)/shard_map/ppermute | solution.py:237
  35.9 4.7 %collective-permute-start.14 = (bf16[128,256]{1,0:T(8,128)(2,1)S(1)}, bf16[128,256]{1,0:T(8,128)(2,1)S(1)}, u32[]{:S(2)}, u32[]{:S(2)}) collective-permute-start(bf16[128,256]{1,0:T(8,128)(2,1)S(1)} %shard_map.64.refs_0_), channel_id=1, source_target_pairs={{0,2},{2,0},{4,6},{6,4},{1,3},{3,1},{5,7},{7,5},{8,10},{10,8},{12,... | collective-permute-start | bytes 196616 | tf_op jit(solution)/shard_map/ppermute | solution.py:237
  37.7 4.3 %collective-permute-start.16 = (bf16[128,256]{1,0:T(8,128)(2,1)S(1)}, bf16[128,256]{1,0:T(8,128)(2,1)S(1)}, u32[]{:S(2)}, u32[]{:S(2)}) collective-permute-start(bf16[128,256]{1,0:T(8,128)(2,1)S(1)} %shard_map.67.refs_1_), channel_id=1, source_target_pairs={{0,2},{2,0},{4,6},{6,4},{1,3},{3,1},{5,7},{7,5},{8,10},{10,8},{12,... | collective-permute-start | bytes 196616 | tf_op jit(solution)/shard_map/ppermute | solution.py:237
  38.4 4.4 %collective-permute-start.19 = (bf16[128,256]{1,0:T(8,128)(2,1)S(1)}, bf16[128,256]{1,0:T(8,128)(2,1)S(1)}, u32[]{:S(2)}, u32[]{:S(2)}) collective-permute-start(bf16[128,256]{1,0:T(8,128)(2,1)S(1)} %shard_map.72.refs_1_), channel_id=1, source_target_pairs={{0,2},{2,0},{4,6},{6,4},{1,3},{3,1},{5,7},{7,5},{8,10},{10,8},{12,... | collective-permute-start | bytes 196616 | tf_op jit(solution)/shard_map/ppermute | solution.py:237

commit v8 on v7

--- a/solution.py
+++ b/solution.py
@@ -149,12 +149,12 @@
 
 def features_kernel(halves, *refs):
     blocks, out = refs[:-1], refs[-1]
-    rows, width = blocks[0].shape[0], out.shape[1] // halves
+    rows, width = blocks[0].shape[0], out.shape[0] // halves
     half = own_half(halves)
-    for i in range(len(blocks) // halves):
-        for h in range(halves):
-            start = pl.multiple_of((half ^ h) * width, width)
-            out[i * rows : (i + 1) * rows, pl.ds(start, width)] = blocks[halves * i + h][:, :width]
+    for h in range(halves):
+        start = pl.multiple_of((half ^ h) * width, width)
+        side = [blocks[halves * i + h][:, :width] for i in range(len(blocks) // halves)]
+        out[pl.ds(start, width), :] = jnp.concatenate(side, axis=0).T
 
 
 def add_kernel(arrived, kept, out):
@@ -192,13 +192,13 @@
 
 
 def gradient_chunk(parts, features, size, stacked, rows, out, written):
-    count, depth = parts[0].shape[0], features.shape[1]
+    count, depth = parts[0].shape[0], features.shape[0]
     for i, part in enumerate(parts):
         stacked[i * count : (i + 1) * count, :] = part[...]
     step = min(128, depth)
     for k in range(depth // step):
         d = slice(k * step, (k + 1) * step)
-        values = dot(features[:, d], stacked[...], ((0,), (0,)))
+        values = dot(features[d, :], stacked[...])
         for c in range(stacked.shape[1] // (2 * size)):
             for j in range(2):
                 at = (2 * c + j) * size
@@ -306,7 +306,7 @@
         far_cot = swap_blk(held, nb, 2)
         features = call(
             functools.partial(features_kernel, halves),
-            sds((nb * rows, depth), BF16),
+            sds((depth, nb * rows), BF16),
             [piece for p in block_order for piece in x[p]],
             [VMEM] * (nb * halves),
             nbytes=3 << 20,
@@ -334,7 +334,7 @@
         chunks = [(0, hidden)]
         features = call(
             functools.partial(features_kernel, halves),
-            sds((nb * rows, depth), BF16),
+            sds((depth, nb * rows), BF16),
             [piece for p in block_order for piece in x[p]],
             [VMEM] * (nb * halves),
             nbytes=3 << 20,

time: 44.4 us -> 44.4 us (level)
  transfers between devices with their start and end apart: 20 -> 20, of which waited for: 11 -> 11; matrix products, arithmetic and copies ran while one was open for 0% -> 0% of each run, Pallas kernels for 13% -> 14%
where the time goes in v8:
time: 44.4 us; the launch traced here: 44.3 us
  starting transfers between devices  20.5 us (46%)
  waiting for transfers between devices  14.1 us (32%)
  Pallas kernels  9.42 us (21%)
    ppermute x13, starting transfers between devices, swap_blk(): return lax.ppermute(x, 'blk', [(i, i ^ p) for i in range(size)])  15.3 us
    ppermute x13, waiting for transfers between devices, swap_blk(): return lax.ppermute(x, 'blk', [(i, i ^ p) for i in range(size)])  12.8 us
    pallas_call x19, Pallas kernels, call(): pl.pallas_call(kernel, out_shape=out_shape, in_specs=in_specs, out_specs=...  9.42 us
    ppermute x3, starting transfers between devices, swap_group(): return lax.ppermute(x, 'group', [(i, i ^ s) for i in range(size)])  4.61 us
    ppermute x3, waiting for transfers between devices, swap_group(): return lax.ppermute(x, 'group', [(i, i ^ s) for i in range(size)])  1.31 us
  transfers between devices with their start and end apart: 20, of which 11 were waited for; matrix products, arithmetic and copies ran while one was open for 0% of the time, Pallas kernels for 14%

profile of v8, /device:TPU:0, one launch (start us, length us, event | category | flops | bytes accessed | tf_op | source)
XLA Modules:
  0.0 44.3 jit_solution(14933556442284631355)
XLA Ops:
  0.0 1.9 %shard_map.55 = (bf16[16,2432]{1,0:T(8,128)(2,1)S(1)}, bf16[16,2432]{1,0:T(8,128)(2,1)S(1)}, bf16[16,2432]{1,0:T(8,128)(2,1)S(1)}, bf16[16,2432]{1,0:T(8,128)(2,1)S(1)}) custom-call(bf16[128,4096]{1,0:T(8,128)(2,1)} %tokens.1, s32[8,128]{1,0:T(8,128)} %bitcast.9, bf16[128,8,384]{2,1,0:T(8,128)(2,1)} %act.1), custom_call_target="tpu_custom_call" | custom-call | bytes 2097152 | tf_op jit(solution)/shard_map/pallas_call | solution.py:18
  1.9 4.0 %collective-permute-start = (bf16[16,2432]{1,0:T(8,128)(2,1)S(1)}, bf16[16,2432]{1,0:T(8,128)(2,1)S(1)}, u32[]{:S(2)}, u32[]{:S(2)}) collective-permute-start(bf16[16,2432]{1,0:T(8,128)(2,1)S(1)} %get-tuple-element.34), channel_id=1, source_target_pairs={{0,24},{8,16},{16,8},{24,0},{1,25},{9,17},{17,9},{25,1},{2,26},{10... | collective-permute-start | bytes 233480 | tf_op jit(solution)/shard_map/ppermute | solution.py:233
  5.9 0.5 %collective-permute-start.1 = (bf16[16,2432]{1,0:T(8,128)(2,1)S(1)}, bf16[16,2432]{1,0:T(8,128)(2,1)S(1)}, u32[]{:S(2)}, u32[]{:S(2)}) collective-permute-start(bf16[16,2432]{1,0:T(8,128)(2,1)S(1)} %get-tuple-element.35), channel_id=1, source_target_pairs={{0,16},{8,24},{16,0},{24,8},{1,17},{9,25},{17,1},{25,9},{2,18},{10... | collective-permute-start | bytes 233480 | tf_op jit(solution)/shard_map/ppermute | solution.py:233
  6.4 0.1 collective-permute-start.2
  6.5 0.1 copy.7.scales
  6.6 2.8 %shard_map.56.refs_4_ = bf16[1024,768]{1,0:T(8,128)(2,1)S(1)} custom-call(f32[8,2,3]{2,1,0:T(2,128)S(1)} %copy.7.scales, bf16[1024,2,384]{2,1,0:T(2,128)(2,1)} %bitcast.8), custom_call_target="tpu_custom_call" | custom-call | bytes 4194304 | tf_op jit(solution)/shard_map/pallas_call | solution.py:18
  9.5 0.0 collective-permute-done.refs_1_
  9.5 0.8 %collective-permute-done.1.refs_2_ = bf16[16,2432]{1,0:T(8,128)(2,1)S(1)} collective-permute-done((bf16[16,2432]{1,0:T(8,128)(2,1)S(1)}, bf16[16,2432]{1,0:T(8,128)(2,1)S(1)}, u32[]{:S(2)}, u32[]{:S(2)}) %collective-permute-start.1) | collective-permute-done | bytes 77856 | tf_op jit(solution)/shard_map/ppermute | solution.py:233
  10.3 0.5 %collective-permute-done.2.refs_3_ = bf16[16,2432]{1,0:T(8,128)(2,1)S(1)} collective-permute-done((bf16[16,2432]{1,0:T(8,128)(2,1)S(1)}, bf16[16,2432]{1,0:T(8,128)(2,1)S(1)}, u32[]{:S(2)}, u32[]{:S(2)}) %collective-permute-start.2) | collective-permute-done | bytes 77856 | tf_op jit(solution)/shard_map/ppermute | solution.py:233
  10.8 1.6 %collective-permute-start.6 = (bf16[64,512]{1,0:T(8,128)(2,1)S(1)}, bf16[64,512]{1,0:T(8,128)(2,1)S(1)}, u32[]{:S(2)}, u32[]{:S(2)}) collective-permute-start(bf16[64,512]{1,0:T(8,128)(2,1)S(1)} %get-tuple-element.45), channel_id=1, source_target_pairs={{0,2},{2,0},{4,6},{6,4},{1,3},{3,1},{5,7},{7,5},{8,10},{10,8},{12,... | collective-permute-start | bytes 196616 | tf_op jit(solution)/shard_map/ppermute | solution.py:237
  12.5 2.5 %collective-permute-start.8 = (bf16[64,512]{1,0:T(8,128)(2,1)S(1)}, bf16[64,512]{1,0:T(8,128)(2,1)S(1)}, u32[]{:S(2)}, u32[]{:S(2)}) collective-permute-start(bf16[64,512]{1,0:T(8,128)(2,1)S(1)} %get-tuple-element.46), channel_id=1, source_target_pairs={{0,6},{2,4},{4,2},{6,0},{1,7},{3,5},{5,3},{7,1},{8,14},{10,12},{12... | collective-permute-start | bytes 196616 | tf_op jit(solution)/shard_map/ppermute | solution.py:237
  14.9 0.1 collective-permute-start.4
  15.1 0.1 collective-permute-done.6.refs_0_.refs_4_
  15.2 3.4 %collective-permute-done.8.refs_2_.refs_6_ = bf16[64,512]{1,0:T(8,128)(2,1)S(1)} collective-permute-done((bf16[64,512]{1,0:T(8,128)(2,1)S(1)}, bf16[64,512]{1,0:T(8,128)(2,1)S(1)}, u32[]{:S(2)}, u32[]{:S(2)}) %collective-permute-start.8) | collective-permute-done | bytes 65568 | tf_op jit(solution)/shard_map/ppermute | solution.py:237
  18.6 0.5 %collective-permute-start.3 = (bf16[64,512]{1,0:T(8,128)(2,1)S(1)}, bf16[64,512]{1,0:T(8,128)(2,1)S(1)}, u32[]{:S(2)}, u32[]{:S(2)}) collective-permute-start(bf16[64,512]{1,0:T(8,128)(2,1)S(1)} %get-tuple-element.41.refs_0_), channel_id=1, source_target_pairs={{0,1},{1,0},{2,3},{3,2},{4,5},{5,4},{6,7},{7,6},{8,9},{9,8},{10,11... | collective-permute-start | bytes 196616 | tf_op jit(solution)/shard_map/ppermute | solution.py:241
  19.1 1.7 %collective-permute-done.4.refs_2_ = bf16[64,512]{1,0:T(8,128)(2,1)S(1)} collective-permute-done((bf16[64,512]{1,0:T(8,128)(2,1)S(1)}, bf16[64,512]{1,0:T(8,128)(2,1)S(1)}, u32[]{:S(2)}, u32[]{:S(2)}) %collective-permute-start.4) | collective-permute-done | bytes 65568 | tf_op jit(solution)/shard_map/ppermute | solution.py:237
  20.8 0.0 collective-permute-start.5
  20.8 0.3 shard_map.59
  21.1 0.2 collective-permute-start.10
  21.3 0.3 shard_map.61
  21.6 1.9 %collective-permute-start.13 = (bf16[128,256]{1,0:T(8,128)(2,1)S(1)}, bf16[128,256]{1,0:T(8,128)(2,1)S(1)}, u32[]{:S(2)}, u32[]{:S(2)}) collective-permute-start(bf16[128,256]{1,0:T(8,128)(2,1)S(1)} %shard_map.61), channel_id=1, source_target_pairs={{0,2},{2,0},{4,6},{6,4},{1,3},{3,1},{5,7},{7,5},{8,10},{10,8},{12,... | collective-permute-start | bytes 196616 | tf_op jit(solution)/shard_map/ppermute | solution.py:237
  23.6 0.3 shard_map.70
  23.9 0.2 collective-permute-start.17
  24.1 2.7 %collective-permute-start.12 = (bf16[64,384]{1,0:T(8,128)(2,1)S(1)}, bf16[64,384]{1,0:T(8,128)(2,1)S(1)}, u32[]{:S(2)}, u32[]{:S(2)}) collective-permute-start(bf16[64,384]{1,0:T(8,128)(2,1)S(1)} %get-tuple-element.48.cot), channel_id=1, source_target_pairs={{0,4},{2,6},{4,0},{6,2},{1,5},{3,7},{5,1},{7,3},{8,12},{10,14},{12... | collective-permute-start | bytes 147464 | tf_op jit(solution)/shard_map/ppermute | solution.py:237
  26.8 0.3 shard_map.69.kept
  27.1 0.3 shard_map.62.kept
  27.4 0.3 shard_map.58.kept
  27.7 0.0 collective-permute-done.10.arrived.near
  27.7 0.3 collective-permute-start.11
  28.1 1.3 %collective-permute-done.12.far_cot = bf16[64,384]{1,0:T(8,128)(2,1)S(1)} collective-permute-done((bf16[64,384]{1,0:T(8,128)(2,1)S(1)}, bf16[64,384]{1,0:T(8,128)(2,1)S(1)}, u32[]{:S(2)}, u32[]{:S(2)}) %collective-permute-start.12) | collective-permute-done | bytes 49184 | tf_op jit(solution)/shard_map/ppermute | solution.py:237
  29.3 3.1 %collective-permute-start.15 = (bf16[128,256]{1,0:T(8,128)(2,1)S(1)}, bf16[128,256]{1,0:T(8,128)(2,1)S(1)}, u32[]{:S(2)}, u32[]{:S(2)}) collective-permute-start(bf16[128,256]{1,0:T(8,128)(2,1)S(1)} %shard_map.63), channel_id=1, source_target_pairs={{0,4},{2,6},{4,0},{6,2},{1,5},{3,7},{5,1},{7,3},{8,12},{10,14},{12... | collective-permute-start | bytes 196616 | tf_op jit(solution)/shard_map/ppermute | solution.py:237
  32.4 0.0 collective-permute-done.17.arrived.near
  32.4 0.1 collective-permute-start.18
  32.5 3.4 %collective-permute-done.11.far = bf16[128,256]{1,0:T(8,128)(2,1)S(1)} collective-permute-done((bf16[128,256]{1,0:T(8,128)(2,1)S(1)}, bf16[128,256]{1,0:T(8,128)(2,1)S(1)}, u32[]{:S(2)}, u32[]{:S(2)}) %collective-permute-start.11) | collective-permute-done | bytes 65568 | tf_op jit(solution)/shard_map/ppermute | solution.py:237
  35.9 0.1 shard_map.64.refs_0_
  35.9 0.1 collective-permute-start.14
  36.0 1.6 %collective-permute-done.15.far = bf16[128,256]{1,0:T(8,128)(2,1)S(1)} collective-permute-done((bf16[128,256]{1,0:T(8,128)(2,1)S(1)}, bf16[128,256]{1,0:T(8,128)(2,1)S(1)}, u32[]{:S(2)}, u32[]{:S(2)}) %collective-permute-start.15) | collective-permute-done | bytes 65568 | tf_op jit(solution)/shard_map/ppermute | solution.py:237
  37.7 0.1 shard_map.67.refs_1_
  37.7 0.4 collective-permute-start.16
  38.2 0.2 collective-permute-done.18.far
  38.4 0.1 shard_map.72.refs_1_
  38.4 2.1 %collective-permute-start.19 = (bf16[128,256]{1,0:T(8,128)(2,1)S(1)}, bf16[128,256]{1,0:T(8,128)(2,1)S(1)}, u32[]{:S(2)}, u32[]{:S(2)}) collective-permute-start(bf16[128,256]{1,0:T(8,128)(2,1)S(1)} %shard_map.72.refs_1_), channel_id=1, source_target_pairs={{0,2},{2,0},{4,6},{6,4},{1,3},{3,1},{5,7},{7,5},{8,10},{10,8},{12,... | collective-permute-start | bytes 196616 | tf_op jit(solution)/shard_map/ppermute | solution.py:237
  40.6 0.2 shard_map.65.refs_2_.refs_3_
  40.8 0.5 %shard_map.66.refs_0_ = bf16[1024,2,384]{2,1,0:T(2,128)(2,1)S(1)} custom-call(bf16[128,256]{1,0:T(8,128)(2,1)S(1)} %shard_map.64.refs_0_, bf16[128,256]{1,0:T(8,128)(2,1)S(1)} %collective-permute-done.14.refs_1_, bf16[1024,256]{1,0:T(8,128)(2,1)S(1)} %shard_map.65.refs_2_.refs_3_), custom_call_target="tpu_custom_call" | custom-call | bytes 1048576 | tf_op jit(solution)/shard_map/pallas_call | solution.py:18
  41.3 0.8 %collective-permute-done.16.refs_2_ = bf16[128,256]{1,0:T(8,128)(2,1)S(1)} collective-permute-done((bf16[128,256]{1,0:T(8,128)(2,1)S(1)}, bf16[128,256]{1,0:T(8,128)(2,1)S(1)}, u32[]{:S(2)}, u32[]{:S(2)}) %collective-permute-start.16) | collective-permute-done | bytes 65568 | tf_op jit(solution)/shard_map/ppermute | solution.py:237
  42.1 0.5 %shard_map.68.refs_0_ = bf16[1024,2,384]{2,1,0:T(2,128)(2,1)S(1)} custom-call(bf16[1024,2,384]{2,1,0:T(2,128)(2,1)S(1)} %shard_map.66.refs_0_, bf16[128,256]{1,0:T(8,128)(2,1)S(1)} %shard_map.67.refs_1_, bf16[128,256]{1,0:T(8,128)(2,1)S(1)} %collective-permute-done.16.refs_2_, ...), custom_call_target="tpu_custom_call", output_to_operand_aliasing={{}: (0, {})} | custom-call | bytes 1048576 | tf_op jit(solution)/shard_map/pallas_call | solution.py:18
  42.6 0.2 collective-permute-done.19.refs_2_
  42.8 1.5 %shard_map.73 = bf16[1024,2,384]{2,1,0:T(2,128)(2,1)} custom-call(bf16[1024,2,384]{2,1,0:T(2,128)(2,1)S(1)} %shard_map.68.refs_0_, bf16[128,256]{1,0:T(8,128)(2,1)S(1)} %shard_map.72.refs_1_, bf16[128,256]{1,0:T(8,128)(2,1)S(1)} %collective-permute-done.19.refs_2_, bf16[1024,256]{1,0:T(8,128)(2,1)S(1)} %shard_map.65.refs_2_.refs_3_), custom_call_target="tpu_custom_call" | custom-call | bytes 4194304 | tf_op jit(solution)/shard_map/pallas_call | solution.py:18
  (15 shorter events, 0.1 us)
Async XLA Ops:
  0.0 6.5 %copy-start = (bf16[8,1,2,3]{0,2,3,1:T(2,128)(2,1)S(1)}, bf16[8,1,2,3]{0,2,3,1:T(2,128)(2,1)}, u32[]{:S(2)}) copy-start(bf16[8,1,2,3]{0,2,3,1:T(2,128)(2,1)} %param.9) | copy-start | bytes 292
  1.9 7.6 %collective-permute-start = (bf16[16,2432]{1,0:T(8,128)(2,1)S(1)}, bf16[16,2432]{1,0:T(8,128)(2,1)S(1)}, u32[]{:S(2)}, u32[]{:S(2)}) collective-permute-start(bf16[16,2432]{1,0:T(8,128)(2,1)S(1)} %get-tuple-element.34), channel_id=1, source_target_pairs={{0,24},{8,16},{16,8},{24,0},{1,25},{9,17},{17,9},{25,1},{2,26},{10... | collective-permute-start | bytes 233480 | tf_op jit(solution)/shard_map/ppermute | solution.py:233
  5.9 4.4 %collective-permute-start.1 = (bf16[16,2432]{1,0:T(8,128)(2,1)S(1)}, bf16[16,2432]{1,0:T(8,128)(2,1)S(1)}, u32[]{:S(2)}, u32[]{:S(2)}) collective-permute-start(bf16[16,2432]{1,0:T(8,128)(2,1)S(1)} %get-tuple-element.35), channel_id=1, source_target_pairs={{0,16},{8,24},{16,0},{24,8},{1,17},{9,25},{17,1},{25,9},{2,18},{10... | collective-permute-start | bytes 233480 | tf_op jit(solution)/shard_map/ppermute | solution.py:233
  6.4 4.4 %collective-permute-start.2 = (bf16[16,2432]{1,0:T(8,128)(2,1)S(1)}, bf16[16,2432]{1,0:T(8,128)(2,1)S(1)}, u32[]{:S(2)}, u32[]{:S(2)}) collective-permute-start(bf16[16,2432]{1,0:T(8,128)(2,1)S(1)} %get-tuple-element.36), channel_id=1, source_target_pairs={{0,8},{8,0},{16,24},{24,16},{1,9},{9,1},{17,25},{25,17},{2,10},{10... | collective-permute-start | bytes 233480 | tf_op jit(solution)/shard_map/ppermute | solution.py:233
  10.8 4.3 %collective-permute-start.6 = (bf16[64,512]{1,0:T(8,128)(2,1)S(1)}, bf16[64,512]{1,0:T(8,128)(2,1)S(1)}, u32[]{:S(2)}, u32[]{:S(2)}) collective-permute-start(bf16[64,512]{1,0:T(8,128)(2,1)S(1)} %get-tuple-element.45), channel_id=1, source_target_pairs={{0,2},{2,0},{4,6},{6,4},{1,3},{3,1},{5,7},{7,5},{8,10},{10,8},{12,... | collective-permute-start | bytes 196616 | tf_op jit(solution)/shard_map/ppermute | solution.py:237
  12.5 6.1 %collective-permute-start.8 = (bf16[64,512]{1,0:T(8,128)(2,1)S(1)}, bf16[64,512]{1,0:T(8,128)(2,1)S(1)}, u32[]{:S(2)}, u32[]{:S(2)}) collective-permute-start(bf16[64,512]{1,0:T(8,128)(2,1)S(1)} %get-tuple-element.46), channel_id=1, source_target_pairs={{0,6},{2,4},{4,2},{6,0},{1,7},{3,5},{5,3},{7,1},{8,14},{10,12},{12... | collective-permute-start | bytes 196616 | tf_op jit(solution)/shard_map/ppermute | solution.py:237
  14.9 5.9 %collective-permute-start.4 = (bf16[64,512]{1,0:T(8,128)(2,1)S(1)}, bf16[64,512]{1,0:T(8,128)(2,1)S(1)}, u32[]{:S(2)}, u32[]{:S(2)}) collective-permute-start(bf16[64,512]{1,0:T(8,128)(2,1)S(1)} %get-tuple-element.42), channel_id=1, source_target_pairs={{0,4},{2,6},{4,0},{6,2},{1,5},{3,7},{5,1},{7,3},{8,12},{10,14},{12... | collective-permute-start | bytes 196616 | tf_op jit(solution)/shard_map/ppermute | solution.py:237
  15.2 5.7 %collective-permute-start.7 = (bf16[64,512]{1,0:T(8,128)(2,1)S(1)}, bf16[64,512]{1,0:T(8,128)(2,1)S(1)}, u32[]{:S(2)}, u32[]{:S(2)}) collective-permute-start(bf16[64,512]{1,0:T(8,128)(2,1)S(1)} %collective-permute-done.6.refs_0_.refs_4_), channel_id=1, source_target_pairs={{0,1},{1,0},{2,3},{3,2},{4,5},{5,4},{6,7},{7,6},{8,9},{9,8},{10,11... | collective-permute-start | bytes 196616 | tf_op jit(solution)/shard_map/ppermute | solution.py:241
  18.6 2.2 %collective-permute-start.9 = (bf16[64,512]{1,0:T(8,128)(2,1)S(1)}, bf16[64,512]{1,0:T(8,128)(2,1)S(1)}, u32[]{:S(2)}, u32[]{:S(2)}) collective-permute-start(bf16[64,512]{1,0:T(8,128)(2,1)S(1)} %collective-permute-done.8.refs_2_.refs_6_), channel_id=1, source_target_pairs={{0,1},{1,0},{2,3},{3,2},{4,5},{5,4},{6,7},{7,6},{8,9},{9,8},{10,11... | collective-permute-start | bytes 196616 | tf_op jit(solution)/shard_map/ppermute | solution.py:241
  18.6 5.5 %collective-permute-start.3 = (bf16[64,512]{1,0:T(8,128)(2,1)S(1)}, bf16[64,512]{1,0:T(8,128)(2,1)S(1)}, u32[]{:S(2)}, u32[]{:S(2)}) collective-permute-start(bf16[64,512]{1,0:T(8,128)(2,1)S(1)} %get-tuple-element.41.refs_0_), channel_id=1, source_target_pairs={{0,1},{1,0},{2,3},{3,2},{4,5},{5,4},{6,7},{7,6},{8,9},{9,8},{10,11... | collective-permute-start | bytes 196616 | tf_op jit(solution)/shard_map/ppermute | solution.py:241
  20.8 6.0 %collective-permute-start.5 = (bf16[64,512]{1,0:T(8,128)(2,1)S(1)}, bf16[64,512]{1,0:T(8,128)(2,1)S(1)}, u32[]{:S(2)}, u32[]{:S(2)}) collective-permute-start(bf16[64,512]{1,0:T(8,128)(2,1)S(1)} %collective-permute-done.4.refs_2_), channel_id=1, source_target_pairs={{0,1},{1,0},{2,3},{3,2},{4,5},{5,4},{6,7},{7,6},{8,9},{9,8},{10,11... | collective-permute-start | bytes 196616 | tf_op jit(solution)/shard_map/ppermute | solution.py:241
  21.1 6.5 %collective-permute-start.10 = (bf16[128,256]{1,0:T(8,128)(2,1)S(1)}, bf16[128,256]{1,0:T(8,128)(2,1)S(1)}, u32[]{:S(2)}, u32[]{:S(2)}) collective-permute-start(bf16[128,256]{1,0:T(8,128)(2,1)S(1)} %shard_map.59), channel_id=1, source_target_pairs={{0,2},{2,0},{4,6},{6,4},{1,3},{3,1},{5,7},{7,5},{8,10},{10,8},{12,... | collective-permute-start | bytes 196616 | tf_op jit(solution)/shard_map/ppermute | solution.py:237
  21.6 6.4 %collective-permute-start.13 = (bf16[128,256]{1,0:T(8,128)(2,1)S(1)}, bf16[128,256]{1,0:T(8,128)(2,1)S(1)}, u32[]{:S(2)}, u32[]{:S(2)}) collective-permute-start(bf16[128,256]{1,0:T(8,128)(2,1)S(1)} %shard_map.61), channel_id=1, source_target_pairs={{0,2},{2,0},{4,6},{6,4},{1,3},{3,1},{5,7},{7,5},{8,10},{10,8},{12,... | collective-permute-start | bytes 196616 | tf_op jit(solution)/shard_map/ppermute | solution.py:237
  23.9 8.5 %collective-permute-start.17 = (bf16[128,256]{1,0:T(8,128)(2,1)S(1)}, bf16[128,256]{1,0:T(8,128)(2,1)S(1)}, u32[]{:S(2)}, u32[]{:S(2)}) collective-permute-start(bf16[128,256]{1,0:T(8,128)(2,1)S(1)} %shard_map.70), channel_id=1, source_target_pairs={{0,2},{2,0},{4,6},{6,4},{1,3},{3,1},{5,7},{7,5},{8,10},{10,8},{12,... | collective-permute-start | bytes 196616 | tf_op jit(solution)/shard_map/ppermute | solution.py:237
  24.1 5.2 %collective-permute-start.12 = (bf16[64,384]{1,0:T(8,128)(2,1)S(1)}, bf16[64,384]{1,0:T(8,128)(2,1)S(1)}, u32[]{:S(2)}, u32[]{:S(2)}) collective-permute-start(bf16[64,384]{1,0:T(8,128)(2,1)S(1)} %get-tuple-element.48.cot), channel_id=1, source_target_pairs={{0,4},{2,6},{4,0},{6,2},{1,5},{3,7},{5,1},{7,3},{8,12},{10,14},{12... | collective-permute-start | bytes 147464 | tf_op jit(solution)/shard_map/ppermute | solution.py:237
  27.7 8.2 %collective-permute-start.11 = (bf16[128,256]{1,0:T(8,128)(2,1)S(1)}, bf16[128,256]{1,0:T(8,128)(2,1)S(1)}, u32[]{:S(2)}, u32[]{:S(2)}) collective-permute-start(bf16[128,256]{1,0:T(8,128)(2,1)S(1)} %shard_map.60), channel_id=1, source_target_pairs={{0,4},{2,6},{4,0},{6,2},{1,5},{3,7},{5,1},{7,3},{8,12},{10,14},{12... | collective-permute-start | bytes 196616 | tf_op jit(solution)/shard_map/ppermute | solution.py:237
  29.3 8.3 %collective-permute-start.15 = (bf16[128,256]{1,0:T(8,128)(2,1)S(1)}, bf16[128,256]{1,0:T(8,128)(2,1)S(1)}, u32[]{:S(2)}, u32[]{:S(2)}) collective-permute-start(bf16[128,256]{1,0:T(8,128)(2,1)S(1)} %shard_map.63), channel_id=1, source_target_pairs={{0,4},{2,6},{4,0},{6,2},{1,5},{3,7},{5,1},{7,3},{8,12},{10,14},{12... | collective-permute-start | bytes 196616 | tf_op jit(solution)/shard_map/ppermute | solution.py:237
  32.4 6.0 %collective-permute-start.18 = (bf16[128,256]{1,0:T(8,128)(2,1)S(1)}, bf16[128,256]{1,0:T(8,128)(2,1)S(1)}, u32[]{:S(2)}, u32[]{:S(2)}) collective-permute-start(bf16[128,256]{1,0:T(8,128)(2,1)S(1)} %shard_map.71), channel_id=1, source_target_pairs={{0,4},{2,6},{4,0},{6,2},{1,5},{3,7},{5,1},{7,3},{8,12},{10,14},{12... | collective-permute-start | bytes 196616 | tf_op jit(solution)/shard_map/ppermute | solution.py:237
  35.9 4.8 %collective-permute-start.14 = (bf16[128,256]{1,0:T(8,128)(2,1)S(1)}, bf16[128,256]{1,0:T(8,128)(2,1)S(1)}, u32[]{:S(2)}, u32[]{:S(2)}) collective-permute-start(bf16[128,256]{1,0:T(8,128)(2,1)S(1)} %shard_map.64.refs_0_), channel_id=1, source_target_pairs={{0,2},{2,0},{4,6},{6,4},{1,3},{3,1},{5,7},{7,5},{8,10},{10,8},{12,... | collective-permute-start | bytes 196616 | tf_op jit(solution)/shard_map/ppermute | solution.py:237
  37.7 4.3 %collective-permute-start.16 = (bf16[128,256]{1,0:T(8,128)(2,1)S(1)}, bf16[128,256]{1,0:T(8,128)(2,1)S(1)}, u32[]{:S(2)}, u32[]{:S(2)}) collective-permute-start(bf16[128,256]{1,0:T(8,128)(2,1)S(1)} %shard_map.67.refs_1_), channel_id=1, source_target_pairs={{0,2},{2,0},{4,6},{6,4},{1,3},{3,1},{5,7},{7,5},{8,10},{10,8},{12,... | collective-permute-start | bytes 196616 | tf_op jit(solution)/shard_map/ppermute | solution.py:237
  38.4 4.4 %collective-permute-start.19 = (bf16[128,256]{1,0:T(8,128)(2,1)S(1)}, bf16[128,256]{1,0:T(8,128)(2,1)S(1)}, u32[]{:S(2)}, u32[]{:S(2)}) collective-permute-start(bf16[128,256]{1,0:T(8,128)(2,1)S(1)} %shard_map.72.refs_1_), channel_id=1, source_target_pairs={{0,2},{2,0},{4,6},{6,4},{1,3},{3,1},{5,7},{7,5},{8,10},{10,8},{12,... | collective-permute-start | bytes 196616 | tf_op jit(solution)/shard_map/ppermute | solution.py:237
